TPU v7x, 256 devices: a whole 4x4x8 slice. The times are simulated.
256 devices in a mesh: dp: 8 (over y_hi, x), cols: 32 (over z, y_lo, core).
Axes of the slice: x: 4, y: 4 (y_hi: 2, y_lo: 2; y = y_hi * 2 + y_lo), z: 8, core: 2. Of those that a mesh axis runs over, the one named last changes fastest.
Arguments:
- prefix_ids: int32 [8, 32, 32, 128], P('dp', 'cols'), may hold values from 0 to 65535, as said below
- suffix_ids: int32 [8, 32, 32, 128], P('dp', 'cols'), may hold values from 0 to 65535, as said below
- weights: float32 [8, 32, 32, 128], P('dp', 'cols'), may hold values from 0.25 to 36
- counts: int32 [8, 32, 32], P('dp', 'cols'), may hold values from 42 to 128, as said below
- omega: bfloat16 [65536, 512], P('cols'), may hold values from -6 to 6
Outputs:
- basis: float32 [65536, 512], P('cols')
- coefficients: float32 [512, 65536], P('dp', 'cols')
Inputs may be any that keep to these rules, and one draw needn't show every extreme that they name: `prefix_ids`: the prefix ids of block (d, c, j) lie in [j * 2048, (j + 1) * 2048), on dead slots too. `suffix_ids`: the suffix ids of block (d, c, j) lie in [c * 2048, (c + 1) * 2048), on dead slots too. For every d some j has counts[d, c, j] = 128 for every c.
All inputs are finite; a program needn't handle non-finite values.
Results may differ from a plain program's by a relative error of at most 0.0028.
The roundings to bfloat16 on the way count: a program that leaves them out, or rounds other values in their place, can miss the bound.
Values may be sent and summed in bfloat16 or wider, within the bound.
A program may use at most 128 MiB of HBM per device.

v0:
```python
import math

import jax
import jax.numpy as jnp
from jax import lax
from jax.sharding import PartitionSpec as P


def gram_of(rows):
    return lax.dot_general(
        rows,
        rows,
        (((0,), (0,)), ((), ())),
        precision=lax.Precision.HIGHEST,
        preferred_element_type=jnp.float32,
    )


def basis_from(rows, gram):
    lower = jnp.linalg.cholesky(gram)
    identity = jnp.eye(gram.shape[0], dtype=jnp.float32)
    inverse_factor = jax.scipy.linalg.solve_triangular(lower, identity, lower=True)
    return lax.dot_general(
        rows,
        inverse_factor,
        (((1,), (1,)), ((), ())),
        precision=lax.Precision.HIGHEST,
        preferred_element_type=jnp.float32,
    )


def shards(prefix_ids, suffix_ids, weights, counts, omega):
    ncols = lax.axis_size("cols")
    ndata = lax.axis_size("dp")
    block, width = omega.shape
    slots = prefix_ids.shape[-1]
    col_start = lax.axis_index("cols") * block
    prefix_here = prefix_ids.reshape(ncols, slots)
    suffix_local = suffix_ids.reshape(ncols, slots) - col_start
    live = lax.broadcasted_iota(jnp.int32, (ncols, slots), 1) < counts.reshape(ncols, 1)
    live_weights = jnp.where(live, weights.reshape(ncols, slots), 0.0)
    own_total = jnp.sum(live_weights)
    own_rows = jnp.sum(live.astype(jnp.float32))
    total_weight, live_rows = lax.psum((own_total, own_rows), ("dp", "cols"))
    omega_rows = jnp.take(omega, suffix_local, axis=0).astype(jnp.float32)
    sketch_rows = (live_weights[:, :, None] * omega_rows).astype(jnp.bfloat16)
    arrived, arrived_prefix = (
        lax.all_to_all(sketch_rows, "cols", split_axis=0, concat_axis=0, tiled=True),
        lax.all_to_all(prefix_here, "cols", split_axis=0, concat_axis=0, tiled=True),
    )
    prefix_local = (arrived_prefix - col_start).reshape(-1)
    partial_sketch = (
        jnp.zeros((block, width), jnp.float32)
        .at[prefix_local]
        .add(arrived.reshape(-1, width).astype(jnp.float32))
    )
    share = block // ndata
    summed = lax.psum(partial_sketch, "dp")
    sketch_share = lax.dynamic_slice_in_dim(summed, lax.axis_index("dp") * share, share, 0)
    gram_part = gram_of(sketch_share)
    gram = lax.psum(gram_part, ("dp", "cols"))
    q_block = basis_from(summed, gram)
    scale = math.sqrt(block * ncols)
    basis = scale * q_block
    q_rows = (
        jnp.take(q_block, prefix_local, axis=0).astype(jnp.bfloat16).reshape(ncols, slots, width)
    )
    returned = lax.all_to_all(q_rows, "cols", split_axis=0, concat_axis=0, tiled=True)
    terms = (live_weights[:, :, None] * returned.astype(jnp.float32)).reshape(-1, width)
    partial_coef = jnp.zeros((block, width), jnp.float32).at[suffix_local.reshape(-1)].add(terms)
    coef_share = lax.psum_scatter(partial_coef, "dp", scatter_dimension=1, tiled=True)
    mean_weight = total_weight / live_rows
    coefficients = scale / mean_weight * coef_share.T
    return (basis, coefficients)


def solution(mesh):
    placed = (
        P("dp", "cols", None, None),
        P("dp", "cols", None, None),
        P("dp", "cols", None, None),
        P("dp", "cols", None),
        P("cols", None),
    )
    return jax.shard_map(
        shards,
        mesh=mesh,
        in_specs=placed,
        out_specs=(P("cols", None), P("dp", "cols")),
        check_vma=False,
    )
```

profile of v0, /device:TPU:1, one launch (start us, length us, event | category | flops | bytes accessed | tf_op | source)
XLA Modules:
  0.0 956.3 jit_solution(14610603264344754040)
XLA Ops:
  7.2 11.3 %all-to-all-start = ((s32[32,1,128]{2,1,0:T(1,128)}), s32[32,1,128]{2,1,0:T(1,128)S(1)}, u32[]{:S(2)}, u32[]{:S(2)}) async-start(s32[32,1,128]{2,1,0:T(1,128)} %bitcast.88), calls=%async_computation | async-start | bytes 32768 | tf_op jit(solution)/shard_map/all_to_all | solution.py:49
  18.5 0.7 compare_and_fusion.1
  19.2 1.5 fusion.50
  20.7 17.3 %gather_fusion = bf16[4096,512]{1,0:T(8,128)(2,1)} fusion(bf16[2048,512]{1,0:T(8,128)(2,1)S(1)} %copy-done, s32[4096]{0:T(1024)S(1)} %fusion.45), kind=kCustom, calls=%fused_computation | custom fusion | bytes 8404992 | tf_op jit(solution)/shard_map/jit(_take)/gather | solution.py:45
  38.0 5.7 multiply_convert_fusion
  43.7 8.3 all-to-all-start.1
  52.1 94.0 %all-to-all-done.1 = bf16[32,128,512]{2,1,0:T(8,128)(2,1)} async-done(((bf16[32,128,512]{2,1,0:T(8,128)(2,1)}), bf16[32,128,512]{2,1,0:T(8,128)(2,1)}, u32[]{:S(2)}, u32[]{:S(2)}) %all-to-all-start.1) | async-done | bytes 4194336 | tf_op jit(solution)/shard_map/all_to_all | solution.py:48
  146.1 27.8 %scatter_custom_fusion = f32[2048,512]{1,0:T(8,128)} fusion(s32[4096]{0:T(1024)S(1)} %bitcast.86, bf16[4096,512]{1,0:T(8,128)(2,1)} %bitcast.32, f32[]{:T(128)} %constant.177.clone.1), kind=kCustom, calls=%fused_computation.6 | custom fusion | flops 4194304 | bytes 8388612 | tf_op jit(solution)/shard_map/scatter-add | solution.py:55
  173.9 0.6 all-reduce.7.cloned.1.call-start
  174.5 0.8 iota_compare_fusion
  175.4 112.0 %all-reduce.5.cloned.1.call-done = f32[2048,512]{1,0:T(8,128)} async-done(((f32[2048,512]{1,0:T(8,128)}), f32[2048,512]{1,0:T(8,128)}) %all-reduce.5.cloned.1.call-update) | async-done | bytes 4194320 | tf_op jit(solution)/shard_map/psum | solution.py:58
  287.4 3.2 fusion.22
  290.7 255.9 %all-reduce.7.cloned.1.call-done = f32[512,512]{0,1:T(8,128)} async-done(((f32[512,512]{0,1:T(8,128)}), f32[512,512]{0,1:T(8,128)}) %all-reduce.7.cloned.1.call-update) | async-done | bytes 1048592 | tf_op jit(solution)/shard_map/psum | solution.py:61
  546.5 1.6 copy.15
  548.1 1.4 fusion.13
  549.6 11.7 %cholesky.104 = f32[128,128]{1,0:T(8,128)S(1)} custom-call(f32[128,128]{1,0:T(8,128)S(1)} %cholesky.266), custom_call_target="Cholesky" | custom-call | tf_op jit(solution)/shard_map/jit(cholesky)/cholesky | solution.py:20
  561.3 0.1 cholesky.224
  561.4 9.8 %custom-call.31 = f32[1,128,128]{1,2,0:T(8,128)S(1)} custom-call(f32[1,128,128]{2,1,0:T(8,128)S(1)} %get-tuple-element.41), custom_call_target="InvertDiagBlocksLowerTriangular" | custom-call | tf_op jit(solution)/shard_map/jit(cholesky)/cholesky | solution.py:20
  571.2 0.3 constant_dynamic-update-slice_fusion.2
  571.6 0.3 convolution_subtract_fusion.3
  571.9 11.9 %cholesky.217 = f32[128,128]{1,0:T(8,128)S(1)} custom-call(f32[128,128]{1,0:T(8,128)S(1)} %cholesky.270), custom_call_target="Cholesky" | custom-call | tf_op jit(solution)/shard_map/jit(cholesky)/cholesky | solution.py:20
  583.8 9.8 %custom-call.32 = f32[1,128,128]{1,2,0:T(8,128)S(1)} custom-call(f32[1,128,128]{2,1,0:T(8,128)S(1)} %get-tuple-element.38), custom_call_target="InvertDiagBlocksLowerTriangular" | custom-call | tf_op jit(solution)/shard_map/jit(cholesky)/cholesky | solution.py:20
  593.6 0.3 convolution_dynamic-update-slice_fusion
  593.9 0.4 convolution_subtract_fusion.4
  594.3 11.7 %cholesky.238 = f32[128,128]{1,0:T(8,128)S(1)} custom-call(f32[128,128]{1,0:T(8,128)S(1)} %cholesky.275), custom_call_target="Cholesky" | custom-call | tf_op jit(solution)/shard_map/jit(cholesky)/cholesky | solution.py:20
  606.1 0.7 compare_reduce_fusion.1
  606.7 9.8 %custom-call.33 = f32[1,128,128]{1,2,0:T(8,128)S(1)} custom-call(f32[1,128,128]{2,1,0:T(8,128)S(1)} %get-tuple-element.35), custom_call_target="InvertDiagBlocksLowerTriangular" | custom-call | tf_op jit(solution)/shard_map/jit(cholesky)/cholesky | solution.py:20
  616.5 0.2 convolution_dynamic-update-slice_fusion.1
  616.7 0.4 convolution_subtract_fusion.5
  617.1 11.9 %cholesky.255 = f32[128,128]{1,0:T(8,128)S(1)} custom-call(f32[128,128]{1,0:T(8,128)S(1)} %convolution_subtract_fusion.5), custom_call_target="Cholesky" | custom-call | tf_op jit(solution)/shard_map/jit(cholesky)/cholesky | solution.py:20
  629.1 0.7 compare_reduce_fusion
  629.7 0.7 compare_reduce_fusion.2
  633.0 0.1 select_select_fusion
  633.2 10.3 %while.1 = (s32[]{:T(128)}, f32[512,512]{1,0:T(8,128)S(1)}, s32[4,2]{0,1:T(2,128)S(1)}, f32[4,128,128]{2,1,0:T(8,128)}, s32[]{:T(128)}) while((s32[]{:T(128)}, f32[512,512]{1,0:T(8,128)S(1)}, s32[4,2]{0,1:T(2,128)S(1)}, f32[4,128,128]{2,1,0:T(8,128)}, s32[]{:T(128)}) %tuple.39), condition=%wide.while_cond, body=%wide.while_body.sunk | while | flops 2 | bytes 132205 | solution.py:22
  633.2 0.5 fusion.59
  633.8 2.0 bitcast_dynamic-update-slice_fusion.2
  635.8 0.5 fusion.59
  636.3 2.0 bitcast_dynamic-update-slice_fusion.2
  638.4 0.5 fusion.59
  638.9 2.0 bitcast_dynamic-update-slice_fusion.2
  641.0 0.5 fusion.59
  641.5 2.0 bitcast_dynamic-update-slice_fusion.2
  643.5 40.1 %custom-call.34 = f32[4,128,128]{1,2,0:T(8,128)S(1)} custom-call(f32[4,128,128]{2,1,0:T(8,128)} %get-tuple-element.9), custom_call_target="InvertDiagBlocksLowerTriangular" | custom-call | tf_op jit(solution)/shard_map/jit(_solve_triangular)/triangular_solve | solution.py:22
  683.6 1.2 fusion.26
  684.8 0.4 convolution_subtract_fusion.1
  685.2 0.4 fusion.38
  685.6 0.4 convolution_subtract_fusion
  686.1 0.4 fusion.36
  686.5 0.6 convolution_subtract_fusion.2
  687.1 0.4 fusion.35
  687.6 8.3 broadcast_multiply_fusion
  695.9 17.3 %gather_fusion.1 = bf16[4096,512]{1,0:T(8,128)(2,1)} fusion(bf16[2048,512]{1,0:T(8,128)(2,1)S(1)} %get-tuple-element.46, s32[4096]{0:T(1024)S(1)} %broadcast_clamp_fusion), kind=kCustom, calls=%fused_computation.1 | custom fusion | bytes 8404992 | tf_op jit(solution)/shard_map/jit(_take)/gather | solution.py:66
  713.2 4.0 select_convert_fusion
  717.2 8.6 all-to-all-start.2
  725.8 0.3 reduce-scatter.4.cloned.1.call-start
  726.2 93.7 %all-to-all-done.2 = bf16[32,128,512]{2,1,0:T(8,128)(2,1)} async-done(((bf16[32,128,512]{2,1,0:T(8,128)(2,1)}), bf16[32,128,512]{2,1,0:T(8,128)(2,1)}, u32[]{:S(2)}, u32[]{:S(2)}) %all-to-all-start.2) | async-done | bytes 4194336 | tf_op jit(solution)/shard_map/all_to_all | solution.py:68
  819.9 5.2 convert_multiply_fusion
  825.1 27.4 %scatter_custom_fusion.1 = f32[2048,512]{1,0:T(8,128)} fusion(s32[4096]{0:T(1024)S(1)} %bitcast.89, f32[4096,512]{1,0:T(8,128)} %bitcast.82, f32[]{:T(128)} %constant.177.clone.1), kind=kCustom, calls=%fused_computation.12 | custom fusion | flops 2097152 | bytes 4194816 | tf_op jit(solution)/shard_map/scatter-add | solution.py:70
  852.5 5.4 copy.18
  857.8 82.7 %all-reduce.1 = (f32[]{:T(128)}, f32[]{:T(128)}) all-reduce(f32[]{:T(128)} %get-tuple-element.42, f32[]{:T(128)} %get-tuple-element.24), channel_id=1, replica_groups=mesh['dp'=8,'cols'=32] {'dp','cols'}, use_global_device_ids=true, to_apply=%region_12.13 | all-reduce | flops 2 | bytes 16 | tf_op jit(solution)/shard_map/psum | solution.py:44
  941.8 2.9 reduce-scatter.4.cloned.1.call-done
  944.7 1.4 copy.19
  946.1 1.1 multiply_bitcast_fusion
  947.2 2.3 copy.16
  (31 shorter events, 0.8 us)
Async XLA Ops:
  7.2 13.5 %copy-start = (bf16[2048,512]{1,0:T(8,128)(2,1)S(1)}, bf16[2048,512]{1,0:T(8,128)(2,1)}, u32[]{:S(2)}) copy-start(bf16[2048,512]{1,0:T(8,128)(2,1)} %param.9) | copy-start | bytes 6291460
  7.2 36.5 %all-to-all-start = ((s32[32,1,128]{2,1,0:T(1,128)}), s32[32,1,128]{2,1,0:T(1,128)S(1)}, u32[]{:S(2)}, u32[]{:S(2)}) async-start(s32[32,1,128]{2,1,0:T(1,128)} %bitcast.88), calls=%async_computation | async-start | bytes 32768 | tf_op jit(solution)/shard_map/all_to_all | solution.py:49
  43.7 102.4 %all-to-all-start.1 = ((bf16[32,128,512]{2,1,0:T(8,128)(2,1)}), bf16[32,128,512]{2,1,0:T(8,128)(2,1)}, u32[]{:S(2)}, u32[]{:S(2)}) async-start(bf16[32,128,512]{2,1,0:T(8,128)(2,1)} %multiply_convert_fusion), calls=%async_computation.1 | async-start | bytes 8388608 | tf_op jit(solution)/shard_map/all_to_all | solution.py:48
  52.0 235.3 %all-reduce.5.cloned.1.call-start = ((), (), s32[]{:S(2)}) async-start(), calls=%async_computation.4 | async-start | bytes 8388608 | tf_op jit(solution)/shard_map/psum | solution.py:58
  173.9 372.6 %all-reduce.7.cloned.1.call-start = ((), (), s32[]{:S(2)}) async-start(), calls=%async_computation.5 | async-start | bytes 2097152 | tf_op jit(solution)/shard_map/psum | solution.py:61
  683.6 4.0 copy-start.2
  717.2 102.7 %all-to-all-start.2 = ((bf16[32,128,512]{2,1,0:T(8,128)(2,1)}), bf16[32,128,512]{2,1,0:T(8,128)(2,1)}, u32[]{:S(2)}, u32[]{:S(2)}) async-start(bf16[32,128,512]{2,1,0:T(8,128)(2,1)} %select_convert_fusion), calls=%async_computation.2 | async-start | bytes 8388608 | tf_op jit(solution)/shard_map/all_to_all | solution.py:68
  725.8 218.9 %reduce-scatter.4.cloned.1.call-start = ((), (), s32[]{:S(2)}) async-start(), calls=%async_computation.6 | async-start | bytes 4718592
  857.8 91.7 %copy-start.1 = (bf16[2048,512]{1,0:T(8,128)(2,1)S(1)}, bf16[2048,512]{1,0:T(8,128)(2,1)}, u32[]{:S(2)}) copy-start(bf16[2048,512]{1,0:T(8,128)(2,1)} %param.9) | copy-start | bytes 6291460
Sparse Core Ops, SparseCore 0:
  174.0 113.3 all-reduce.4
  293.4 253.0 all-reduce.6
  858.0 86.7 reduce-scatter.3
where the time goes:
time: 961 us; the launch traced here: 956 us
  waiting for transfers between devices  559 us (58%)
  other arithmetic  195 us (20%)
  blocking collectives  82.7 us (9%)
  local copies, waits for them, and re-layouts  55.7 us (6%)
  starting transfers between devices  29.1 us (3%)
  between operations  18.1 us (2%)
  matrix products  17.3 us (2%)
    psum x1, waiting for transfers between devices, shards(): gram = lax.psum(gram_part, ('dp', 'cols'))  256 us
    psum x1, waiting for transfers between devices, shards(): summed = lax.psum(partial_sketch, 'dp')  112 us
    all_to_all x1, waiting for transfers between devices, shards(): lax.all_to_all(sketch_rows, 'cols', split_axis=0, concat_axis=0, tiled=True)  94 us
    all_to_all x1, waiting for transfers between devices, shards(): lax.all_to_all(q_rows, 'cols', split_axis=0, concat_axis=0, tiled=True)  93.7 us
    psum x1, blocking collectives, shards(): total_weight, live_rows = lax.psum((own_total, own_rows), ('dp', 'cols'))  82.7 us
    another operation x14, other arithmetic, basis_from(): lower = jnp.linalg.cholesky(gram)  78.8 us
    another operation x3, other arithmetic, basis_from(): jax.scipy.linalg.solve_triangular(lower, identity, lower=True)  40.3 us
    scatter-add x1, other arithmetic, shards(): partial_sketch = jnp.zeros((block, width), jnp.float32).at[prefix_local]....  27.8 us
  transfers between devices with their start and end apart: 6, of which 5 were waited for; matrix products, arithmetic and copies ran while one was open for 3% of the time, Pallas kernels for 0%

commit v1 on v0

v1 whole, which is shorter than its diff:
```python
import functools
import math

import jax
import jax.numpy as jnp
from jax import lax
from jax.experimental import pallas as pl
from jax.experimental.pallas import tpu as pltpu
from jax.sharding import PartitionSpec as P

HIGHEST = lax.Precision.HIGHEST


def dot_exact(a, b, dims):
    return lax.dot_general(
        a, b, (dims, ((), ())), precision=HIGHEST, preferred_element_type=jnp.float32
    )


def one_hot(ids, size):
    rows = lax.broadcasted_iota(jnp.int32, (size, ids.shape[1]), 0)
    return jnp.where(rows == ids, 1.0, 0.0).astype(jnp.bfloat16)


def move_block(table, take, put, weight, width):
    size = table.shape[1]
    groups = table.shape[0] // width
    shift = size.bit_length() - 1
    beside = functools.partial(jnp.concatenate, axis=1)
    picked = jnp.dot(
        table,
        beside([one_hot(ids & (size - 1), size) for ids in take]),
        preferred_element_type=jnp.float32,
    )
    take_group = beside([lax.shift_right_logical(ids, shift) for ids in take])
    put_group = beside([lax.shift_right_logical(ids, shift) for ids in put])
    row = picked[:width]
    for g in range(1, groups):
        row = jnp.where(take_group == g, picked[g * width : (g + 1) * width], row)
    row = beside(weight) * row
    placed = jnp.concatenate(
        [jnp.where(put_group == g, row, 0.0).astype(jnp.bfloat16) for g in range(groups)], axis=0
    )
    spots = beside([one_hot(ids & (size - 1), size) for ids in put])
    return lax.dot_general(
        placed, spots, (((1,), (1,)), ((), ())), preferred_element_type=jnp.float32
    )


def move_kernel(width, table_ref, take_ref, put_ref, weight_ref, total_ref):
    @pl.when(pl.program_id(0) == 0)
    def _():
        total_ref[...] = jnp.zeros_like(total_ref)

    rows = range(take_ref.shape[1])
    total_ref[...] += move_block(
        table_ref[0],
        [take_ref[0, r : r + 1, :] for r in rows],
        [put_ref[0, r : r + 1, :] for r in rows],
        [weight_ref[0, r : r + 1, :] for r in rows],
        width,
    )


def move(name, tables, take, put, weight, width):
    blocks, stacked, size = tables.shape
    _, parts, slots = take.shape
    records = pl.BlockSpec((1, parts, slots), lambda i: (i, 0, 0))
    return pl.pallas_call(
        functools.partial(move_kernel, width),
        out_shape=jax.ShapeDtypeStruct((stacked, size), jnp.float32),
        grid=(blocks,),
        in_specs=[pl.BlockSpec((1, stacked, size), lambda i: (i, 0, 0)), records, records, records],
        out_specs=pl.BlockSpec((stacked, size), lambda i: (0, 0)),
        compiler_params=pltpu.CompilerParams(vmem_limit_bytes=40 * 2**20),
        name=name,
    )(tables, take, put, weight)


def shards(prefix_ids, suffix_ids, weights, counts, omega):
    ncols = lax.axis_size("cols")
    ndata = lax.axis_size("dp")
    block, width = omega.shape
    slots = prefix_ids.shape[-1]
    chunk = width // ndata
    size = block // ndata
    data_at = lax.axis_index("dp")

    live = lax.broadcasted_iota(jnp.int32, (ncols, slots), 1) < counts.reshape(ncols, 1)
    live_weights = jnp.where(live, weights.reshape(ncols, slots), 0.0)
    prefix_local = prefix_ids.reshape(ncols, slots) & (block - 1)
    suffix_local = suffix_ids.reshape(ncols, slots) & (block - 1)
    packed = prefix_local * block + suffix_local

    own = (packed, live_weights)
    here = [lax.all_to_all(x, "cols", split_axis=0, concat_axis=0, tiled=True) for x in own]
    here_ids, here_weights = [lax.all_gather(x, "dp", axis=1) for x in here]
    mine_ids, mine_weights = [lax.all_gather(x, "dp", axis=1) for x in own]
    live_rows, total_weight = lax.psum(
        (jnp.sum(live.astype(jnp.float32)), jnp.sum(live_weights)), ("dp", "cols")
    )

    part = lax.dynamic_slice_in_dim(omega, data_at * chunk, chunk, 1)
    part = part.reshape(ndata, size, chunk).swapaxes(1, 2).reshape(ndata * chunk, size)
    tables = lax.all_gather(part, "cols", axis=0)
    shift = block.bit_length() - 1
    sketch = move(
        "sketch", tables, here_ids & (block - 1), here_ids >> shift, here_weights, chunk
    )
    sketch_rows = lax.all_to_all(
        sketch.reshape(ndata, chunk, size), "dp", split_axis=0, concat_axis=0, tiled=True
    ).reshape(width, size)
    gram = lax.psum(dot_exact(sketch_rows, sketch_rows, ((1,), (1,))), ("dp", "cols"))
    lower = jnp.linalg.cholesky(gram)
    identity = jnp.eye(width, dtype=jnp.float32)
    inverse_factor = jax.scipy.linalg.solve_triangular(lower, identity, lower=True)
    q_part = dot_exact(inverse_factor, sketch_rows, ((1,), (0,)))
    scale = math.sqrt(block * ncols)
    basis = lax.all_gather(scale * q_part.T, "dp", axis=0, tiled=True)

    q_half = q_part.astype(jnp.bfloat16).reshape(ndata, chunk, size)
    q_chunk = lax.all_to_all(q_half, "dp", split_axis=0, concat_axis=0, tiled=True)
    q_tables = lax.all_gather(q_chunk.reshape(width, size), "cols", axis=0)
    sums = move(
        "project", q_tables, mine_ids >> shift, mine_ids & (block - 1), mine_weights, chunk
    )
    sums = sums.reshape(ndata, chunk, size).swapaxes(0, 1).reshape(chunk, block)
    coefficients = (scale * live_rows / total_weight) * sums
    return (basis, coefficients)


def solution(mesh):
    placed = (
        P("dp", "cols", None, None),
        P("dp", "cols", None, None),
        P("dp", "cols", None, None),
        P("dp", "cols", None),
        P("cols", None),
    )
    return jax.shard_map(
        shards,
        mesh=mesh,
        in_specs=placed,
        out_specs=(P("cols", None), P("dp", "cols")),
        check_vma=False,
    )
```

time: 961 us -> 781 us (0.81)
  waiting for transfers between devices: 559 us -> 272 us
  blocking collectives: 82.7 us -> 219 us
  other arithmetic: 195 us -> 130 us
  Pallas kernels: 0 us -> 61.1 us
  local copies, waits for them, and re-layouts: 55.7 us -> 34.2 us
  starting transfers between devices: 29.1 us -> 15.9 us
    all_to_all x3 -> x2, waiting for transfers between devices: 188 us -> 6.51 us  [shards(): lax.all_to_all(x, 'cols', split_axis=0, concat_axis=0, tiled=True)]
    all_gather x0 -> x4, blocking collectives: none -> 114 us  [the longest x2 57.4 us: shards(): here_ids, here_weights = [lax.all_gather(x, 'dp', axis=1) for x in here]]
    psum x2 -> x1, waiting for transfers between devices: 368 us -> 263 us  [shards(): lax.psum(dot_exact(sketch_rows, sketch_rows, ((1,), (1,))), ('dp', 'cols'))]
    pallas_call x0 -> x2, Pallas kernels: none -> 61.1 us  [move(): pl.pallas_call(functools.partial(move_kernel, width), out_shape=jax.Shape...]
    scatter-add x2 -> x0, other arithmetic: 55.2 us -> none  [the longest x1 27.8 us: shards(): partial_sketch = jnp.zeros((block, width), jnp.float32).at[prefix_local]....]
    gather x2 -> x0, local copies, waits for them, and re-layouts: 34.6 us -> none  [the longest x1 17.3 us: shards(): omega_rows = jnp.take(omega, suffix_local, axis=0).astype(jnp.float32)]
    all_to_all x0 -> x2, blocking collectives: none -> 28.1 us  [the longest x1 14.3 us: shards(): lax.all_to_all(sketch.reshape(ndata, chunk, size), 'dp', split_axis=0, co...]
    all_to_all x3 -> x2, starting transfers between devices: 28.2 us -> 15.2 us  [shards(): lax.all_to_all(x, 'cols', split_axis=0, concat_axis=0, tiled=True)]
  transfers between devices with their start and end apart: 6 -> 6, of which waited for: 5 -> 3; matrix products, arithmetic and copies ran while one was open for 3% -> 1% of each run, Pallas kernels for 0% -> 0%
where the time goes in v1:
time: 781 us; the launch traced here: 767 us
  waiting for transfers between devices  272 us (35%)
  blocking collectives  219 us (28%)
  other arithmetic  130 us (17%)
  Pallas kernels  61.1 us (8%)
  local copies, waits for them, and re-layouts  34.2 us (4%)
  between operations  18.1 us (2%)
  matrix products  17.6 us (2%)
  starting transfers between devices  15.9 us (2%)
    psum x1, waiting for transfers between devices, shards(): lax.psum(dot_exact(sketch_rows, sketch_rows, ((1,), (1,))), ('dp', 'cols'))  263 us
    another operation x14, other arithmetic, shards(): lower = jnp.linalg.cholesky(gram)  80.5 us
    psum x1, blocking collectives, shards(): lax.psum((jnp.sum(live.astype(jnp.float32)), jnp.sum(live_weights)), ('dp...  76.7 us
    pallas_call x2, Pallas kernels, move(): pl.pallas_call(functools.partial(move_kernel, width), out_shape=jax.Shape...  61.1 us
    all_gather x2, blocking collectives, shards(): here_ids, here_weights = [lax.all_gather(x, 'dp', axis=1) for x in here]  57.4 us
    all_gather x2, blocking collectives, shards(): mine_ids, mine_weights = [lax.all_gather(x, 'dp', axis=1) for x in own]  57 us
    another operation x3, other arithmetic, shards(): jax.scipy.linalg.solve_triangular(lower, identity, lower=True)  42.5 us
  transfers between devices with their start and end apart: 6, of which 3 were waited for; matrix products, arithmetic and copies ran while one was open for 1% of the time, Pallas kernels for 0%

profile of v1, /device:TPU:1, one launch (start us, length us, event | category | flops | bytes accessed | tf_op | source)
XLA Modules:
  0.0 767.3 jit_solution(12904396416596907235)
XLA Ops:
  7.2 1.5 copy-done
  9.0 0.9 copy.37
  9.9 1.4 compare_select_fusion
  11.3 11.1 %all-to-all-start.1 = ((f32[32,1,128]{2,1,0:T(1,128)}), f32[32,1,128]{2,1,0:T(1,128)S(1)}, u32[]{:S(2)}, u32[]{:S(2)}) async-start(f32[32,1,128]{2,1,0:T(1,128)} %compare_select_fusion), calls=%async_computation.1 | async-start | bytes 32768 | tf_op jit(solution)/shard_map/all_to_all | solution.py:96
  22.5 1.3 and_add_fusion
  23.8 6.5 all-to-all-done.1
  30.3 4.1 all-to-all-start
  34.5 28.6 %all_gather.27 = f32[32,8,128]{2,0,1:T(8,128)S(1)} all-gather(f32[32,1,128]{2,0,1:T(8,128)S(1)} %bitcast.98), channel_id=1, replica_groups=mesh['dp'=8,'cols'=32] {'dp'}, dimensions={1}, use_global_device_ids=true | all-gather | bytes 147456 | tf_op jit(solution)/shard_map/all_gather | solution.py:97
  63.2 28.8 %all_gather.26 = s32[32,8,128]{2,0,1:T(8,128)S(1)} all-gather(s32[32,1,128]{2,0,1:T(8,128)S(1)} %bitcast.99), channel_id=1, replica_groups=mesh['dp'=8,'cols'=32] {'dp'}, dimensions={1}, use_global_device_ids=true | all-gather | bytes 147456 | tf_op jit(solution)/shard_map/all_gather | solution.py:97
  92.1 3.4 copy-done.2
  95.5 30.5 %sketch.1 = f32[512,256]{1,0:T(8,128)S(1)} custom-call(bf16[32,512,256]{2,1,0:T(8,128)(2,1)S(1)} %copy-done.2, s32[32,8,128]{2,1,0:T(8,128)S(1)} %get-tuple-element.39.take_ref, s32[32,8,128]{2,1,0:T(8,128)S(1)} %get-tuple-element.38.put_ref, f32[32,8,128]{2,1,0:T(8,128)S(1)} %copy.42.weight_ref), custom_call_target="tpu_custom_call" | custom-call | tf_op jit(solution)/shard_map/sketch/pallas_call | solution.py:69
  126.0 14.3 %all_to_all.22 = f32[8,64,256]{2,1,0:T(8,128)S(1)} all-to-all(f32[8,64,256]{2,1,0:T(8,128)S(1)} %bitcast.87), channel_id=1, replica_groups=mesh['dp'=8,'cols'=32] {'dp'}, dimensions={0} | all-to-all | bytes 1048576 | tf_op jit(solution)/shard_map/all_to_all | solution.py:110
  140.3 2.0 fusion.45
  142.3 0.5 all-gather.7.cloned.1.call-start
  142.9 1.1 fusion.17
  144.1 262.8 %all-reduce.4.cloned.1.call-done = f32[512,512]{0,1:T(8,128)} async-done(((f32[512,512]{0,1:T(8,128)}), f32[512,512]{0,1:T(8,128)}) %all-reduce.4.cloned.1.call-update) | async-done | bytes 1048592 | tf_op jit(solution)/shard_map/psum | solution.py:113
  406.9 2.5 copy.44
  409.4 1.8 fusion.8
  411.2 1.0 copy-done.3
  412.2 11.7 %cholesky.104 = f32[128,128]{1,0:T(8,128)S(1)} custom-call(f32[128,128]{1,0:T(8,128)S(1)} %cholesky.266), custom_call_target="Cholesky" | custom-call | tf_op jit(solution)/shard_map/jit(cholesky)/cholesky | solution.py:114
  424.0 9.8 %custom-call.31 = f32[1,128,128]{1,2,0:T(8,128)S(1)} custom-call(f32[1,128,128]{2,1,0:T(8,128)S(1)} %get-tuple-element.49), custom_call_target="InvertDiagBlocksLowerTriangular" | custom-call | tf_op jit(solution)/shard_map/jit(cholesky)/cholesky | solution.py:114
  433.8 1.1 cholesky.224
  434.9 1.9 constant_dynamic-update-slice_fusion.3
  436.8 1.2 convolution_subtract_fusion.3
  438.1 11.7 %cholesky.217 = f32[128,128]{1,0:T(8,128)S(1)} custom-call(f32[128,128]{1,0:T(8,128)S(1)} %cholesky.270), custom_call_target="Cholesky" | custom-call | tf_op jit(solution)/shard_map/jit(cholesky)/cholesky | solution.py:114
  449.8 0.6 select_reduce_fusion.2
  450.4 10.0 %custom-call.32 = f32[1,128,128]{1,2,0:T(8,128)S(1)} custom-call(f32[1,128,128]{2,1,0:T(8,128)S(1)} %get-tuple-element.46), custom_call_target="InvertDiagBlocksLowerTriangular" | custom-call | tf_op jit(solution)/shard_map/jit(cholesky)/cholesky | solution.py:114
  460.4 0.9 convolution_dynamic-update-slice_fusion
  461.3 1.4 convolution_subtract_fusion.4
  462.8 11.7 %cholesky.238 = f32[128,128]{1,0:T(8,128)S(1)} custom-call(f32[128,128]{1,0:T(8,128)S(1)} %cholesky.275), custom_call_target="Cholesky" | custom-call | tf_op jit(solution)/shard_map/jit(cholesky)/cholesky | solution.py:114
  474.5 0.6 select_reduce_fusion.1
  475.1 0.6 compare_reduce_fusion.1
  475.8 9.8 %custom-call.33 = f32[1,128,128]{1,2,0:T(8,128)S(1)} custom-call(f32[1,128,128]{2,1,0:T(8,128)S(1)} %get-tuple-element.43), custom_call_target="InvertDiagBlocksLowerTriangular" | custom-call | tf_op jit(solution)/shard_map/jit(cholesky)/cholesky | solution.py:114
  485.6 0.8 convolution_dynamic-update-slice_fusion.1
  486.4 1.4 convolution_subtract_fusion.5
  487.8 11.7 %cholesky.255 = f32[128,128]{1,0:T(8,128)S(1)} custom-call(f32[128,128]{1,0:T(8,128)S(1)} %convolution_subtract_fusion.5), custom_call_target="Cholesky" | custom-call | tf_op jit(solution)/shard_map/jit(cholesky)/cholesky | solution.py:114
  499.5 0.6 select_reduce_fusion
  500.2 0.8 compare_reduce_fusion
  501.0 0.6 compare_reduce_fusion.2
  504.0 2.3 select_select_fusion
  506.4 13.7 %while.1 = (s32[]{:T(128)}, f32[512,512]{1,0:T(8,128)}, s32[4,2]{0,1:T(2,128)S(1)}, f32[4,128,128]{2,1,0:T(8,128)}, s32[]{:T(128)}) while((s32[]{:T(128)}, f32[512,512]{1,0:T(8,128)}, s32[4,2]{0,1:T(2,128)S(1)}, f32[4,128,128]{2,1,0:T(8,128)}, s32[]{:T(128)}) %tuple.40), condition=%wide.while_cond, body=%wide.while_body.sunk | while | flops 2 | bytes 132705 | solution.py:116
  506.4 0.5 fusion.55
  507.0 2.8 bitcast_dynamic-update-slice_fusion.2
  509.9 0.5 fusion.55
  510.4 2.8 bitcast_dynamic-update-slice_fusion.2
  513.3 0.5 fusion.55
  513.8 2.8 bitcast_dynamic-update-slice_fusion.2
  516.8 0.5 fusion.55
  517.3 2.8 bitcast_dynamic-update-slice_fusion.2
  520.1 40.1 %custom-call.34 = f32[4,128,128]{1,2,0:T(8,128)S(1)} custom-call(f32[4,128,128]{2,1,0:T(8,128)} %get-tuple-element.9), custom_call_target="InvertDiagBlocksLowerTriangular" | custom-call | tf_op jit(solution)/shard_map/jit(_solve_triangular)/triangular_solve | solution.py:116
  560.5 1.4 convolution_subtract_fusion.1
  562.3 1.4 convolution_subtract_fusion
  564.2 1.7 convolution_subtract_fusion.2
  566.3 1.8 fusion.42
  568.2 13.8 %all_to_all.23 = bf16[8,64,256]{2,1,0:T(8,128)(2,1)} all-to-all(bf16[8,64,256]{2,1,0:T(8,128)(2,1)S(1)} %bitcast.95), channel_id=1, replica_groups=mesh['dp'=8,'cols'=32] {'dp'}, dimensions={0} | all-to-all | bytes 524288 | tf_op jit(solution)/shard_map/all_to_all | solution.py:122
  582.1 0.7 fusion.37
  582.8 76.7 %all-reduce.1 = (f32[]{:T(128)}, f32[]{:T(128)}) all-reduce(f32[]{:T(128)} %get-tuple-element.21, f32[]{:T(128)} %get-tuple-element.20), channel_id=1, replica_groups=mesh['dp'=8,'cols'=32] {'dp','cols'}, use_global_device_ids=true, to_apply=%region_10.11 | all-reduce | flops 2 | bytes 16 | tf_op jit(solution)/shard_map/psum | solution.py:99
  659.5 28.5 %all-gather = s32[1,1,32,1024]{3,2,1,0:T(8,128)S(1)} all-gather(s32[1,1,32,128]{3,2,1,0:T(8,128)} %and_add_fusion), channel_id=2, replica_groups=mesh['dp'=8,'cols'=32] {'dp'}, dimensions={3}, use_global_device_ids=true | all-gather | bytes 147456 | tf_op jit(solution)/shard_map/all_gather | solution.py:98
  688.1 28.4 %all_gather.31 = f32[32,8,128]{2,0,1:T(8,128)S(1)} all-gather(f32[32,1,128]{2,0,1:T(8,128)} %bitcast.26), channel_id=1, replica_groups=mesh['dp'=8,'cols'=32] {'dp'}, dimensions={1}, use_global_device_ids=true | all-gather | bytes 147456 | tf_op jit(solution)/shard_map/all_gather | solution.py:98
  718.1 5.3 copy.48
  723.4 2.3 all-gather.9.cloned.1.call-done.table_ref
  725.7 3.4 copy-done.1
  729.1 30.5 %project.1 = f32[512,256]{1,0:T(8,128)S(1)} custom-call(bf16[32,512,256]{2,1,0:T(8,128)(2,1)S(1)} %copy-done.1, s32[32,8,128]{2,1,0:T(8,128)S(1)} %bitcast.88, s32[32,8,128]{2,1,0:T(8,128)S(1)} %bitcast.89, f32[32,8,128]{2,1,0:T(8,128)S(1)} %copy.46.weight_ref), custom_call_target="tpu_custom_call" | custom-call | tf_op jit(solution)/shard_map/project/pallas_call | solution.py:69
  759.7 0.8 copy.52
  (42 shorter events, 2.8 us)
Async XLA Ops:
  7.2 1.6 copy-start
  7.2 84.9 %all-gather.5.cloned.1.call-start = ((), (), s32[]{:S(2)}) async-start(), calls=%async_computation.4 | async-start | bytes 8650752 | tf_op jit(solution)/shard_map/all_gather | solution.py:105
  11.3 19.0 %all-to-all-start.1 = ((f32[32,1,128]{2,1,0:T(1,128)}), f32[32,1,128]{2,1,0:T(1,128)S(1)}, u32[]{:S(2)}, u32[]{:S(2)}) async-start(f32[32,1,128]{2,1,0:T(1,128)} %compare_select_fusion), calls=%async_computation.1 | async-start | bytes 32768 | tf_op jit(solution)/shard_map/all_to_all | solution.py:96
  30.3 32.9 %all-to-all-start = ((s32[32,1,128]{2,1,0:T(1,128)}), s32[32,1,128]{2,1,0:T(1,128)S(1)}, u32[]{:S(2)}, u32[]{:S(2)}) async-start(s32[32,1,128]{2,1,0:T(1,128)} %bitcast.4), calls=%async_computation | async-start | bytes 32768 | tf_op jit(solution)/shard_map/all_to_all | solution.py:96
  34.4 372.5 %all-reduce.4.cloned.1.call-start = ((), (), s32[]{:S(2)}) async-start(), calls=%async_computation.5 | async-start | bytes 2097152 | tf_op jit(solution)/shard_map/psum | solution.py:113
  92.1 3.4 copy-start.2
  142.3 575.8 %all-gather.7.cloned.1.call-start = ((), (), s32[]{:S(2)}) async-start(), calls=%async_computation.6 | async-start | bytes 4718592 | tf_op jit(solution)/shard_map/all_gather | solution.py:119
  411.2 1.0 copy-start.3
  561.9 20.2 %copy-start.4 = (f32[1,1,32,128]{3,2,1,0:T(8,128)S(1)}, f32[1,1,32,128]{3,2,1,0:T(8,128)}, u32[]{:S(2)}) copy-start(f32[1,1,32,128]{3,2,1,0:T(8,128)} %param.7) | copy-start | bytes 49156
  561.9 20.2 %copy-start.5 = (s32[1,1,32]{2,1,0:T(1,128)S(1)}, s32[1,1,32]{2,1,0:T(1,128)}, u32[]{:S(2)}) copy-start(s32[1,1,32]{2,1,0:T(1,128)} %param.8) | copy-start | bytes 388
  568.1 157.6 %all-gather.9.cloned.1.call-start = ((), (), s32[]{:S(2)}) async-start(), calls=%async_computation.7 | async-start | bytes 8650752 | tf_op jit(solution)/shard_map/all_gather | solution.py:123
  725.7 3.4 copy-start.1
Sparse Core Ops, SparseCore 0:
  10.4 77.0 all-gather.4
  142.4 264.4 all-reduce.3
  568.3 82.8 all-gather.6
  653.0 72.6 all-gather.8

commit v2 on v1

--- a/solution.py
+++ b/solution.py
@@ -77,6 +77,343 @@
     )(tables, take, put, weight)
 
 
+def vmem():
+    return pl.BlockSpec(memory_space=pltpu.VMEM)
+
+
+def put_copy(src, dst, send, recv, axis, peer):
+    return pltpu.make_async_remote_copy(
+        src_ref=src,
+        dst_ref=dst,
+        send_sem=send,
+        recv_sem=recv,
+        device_id={axis: peer},
+        device_id_type=pl.DeviceIdType.MESH,
+    )
+
+
+def over_peers(axis, act):
+    count = lax.axis_size(axis)
+    me = lax.axis_index(axis)
+
+    def one(offset, carry):
+        act(offset, lax.rem(me + offset, count))
+        return carry
+
+    lax.fori_loop(1, count, one, 0)
+
+
+def greet(*axes):
+    barrier = pltpu.get_barrier_semaphore()
+    for axis in axes:
+        over_peers(
+            axis,
+            lambda offset, peer, axis=axis: pl.semaphore_signal(
+                barrier, inc=1, device_id={axis: peer}, device_id_type=pl.DeviceIdType.MESH
+            ),
+        )
+    pl.semaphore_wait(barrier, sum(lax.axis_size(axis) - 1 for axis in axes))
+
+
+def exchange(axis, make):
+    over_peers(axis, lambda offset, peer: make(offset, peer).start())
+    over_peers(axis, lambda offset, peer: make(offset, peer).wait())
+
+
+def records_kernel(own_ref, here_ref, mine_ref, col_sems, here_sems, mine_sems):
+    data_at, col_at = lax.axis_index("dp"), lax.axis_index("cols")
+    greet("cols", "dp")
+
+    def to_col(offset, peer):
+        return put_copy(
+            own_ref.at[peer],
+            here_ref.at[data_at, col_at],
+            col_sems.at[0, offset],
+            col_sems.at[1, offset],
+            "cols",
+            peer,
+        )
+
+    def own_to_data(offset, peer):
+        return put_copy(
+            own_ref,
+            mine_ref.at[data_at],
+            mine_sems.at[0, offset],
+            mine_sems.at[1, offset],
+            "dp",
+            peer,
+        )
+
+    def here_to_data(offset, peer):
+        return put_copy(
+            here_ref.at[data_at],
+            here_ref.at[data_at],
+            here_sems.at[0, offset],
+            here_sems.at[1, offset],
+            "dp",
+            peer,
+        )
+
+    over_peers("cols", lambda offset, peer: to_col(offset, peer).start())
+    over_peers("dp", lambda offset, peer: own_to_data(offset, peer).start())
+    here_ref[data_at, col_at] = own_ref[col_at]
+    mine_ref[data_at] = own_ref[...]
+    over_peers("cols", lambda offset, peer: to_col(offset, peer).wait())
+    exchange("dp", here_to_data)
+    over_peers("dp", lambda offset, peer: own_to_data(offset, peer).wait())
+
+
+def exchange_records(own):
+    ndata, ncols = lax.axis_size("dp"), lax.axis_size("cols")
+    gathered = jax.ShapeDtypeStruct((ndata, *own.shape), own.dtype)
+    return pl.pallas_call(
+        records_kernel,
+        out_shape=(gathered, gathered),
+        in_specs=[vmem()],
+        out_specs=(vmem(), vmem()),
+        scratch_shapes=[
+            pltpu.SemaphoreType.DMA((2, ncols)),
+            pltpu.SemaphoreType.DMA((2, ndata)),
+            pltpu.SemaphoreType.DMA((2, ndata)),
+        ],
+        compiler_params=pltpu.CompilerParams(collective_id=0, has_side_effects=True),
+        name="records",
+    )(own)
+
+
+def gram_kernel(
+    sketch_ref,
+    weight_ref,
+    rows_ref,
+    gram_ref,
+    totals_ref,
+    part_ref,
+    got_ref,
+    piece_ref,
+    arrived_ref,
+    shared_ref,
+    rows_sems,
+    part_sems,
+    piece_sems,
+    shared_sems,
+    gram_sems,
+):
+    data_at, col_at = lax.axis_index("dp"), lax.axis_index("cols")
+    ndata, chunk, size = sketch_ref.shape
+    width = ndata * chunk
+    lanes = piece_ref.shape[2]
+    across = width // lanes
+    greet("cols", "dp")
+
+    def rows_copy(offset, peer):
+        return put_copy(
+            sketch_ref.at[peer],
+            rows_ref.at[data_at],
+            rows_sems.at[0, offset],
+            rows_sems.at[1, offset],
+            "dp",
+            peer,
+        )
+
+    over_peers("dp", lambda offset, peer: rows_copy(offset, peer).start())
+    rows_ref[data_at] = sketch_ref[data_at]
+    over_peers("dp", lambda offset, peer: rows_copy(offset, peer).wait())
+    rows = rows_ref[...].reshape(width, size)
+    part_ref[...] = dot_exact(rows, rows, ((1,), (1,))).reshape(part_ref.shape)
+
+    def part_copy(offset, peer):
+        return put_copy(
+            part_ref.at[peer],
+            got_ref.at[data_at],
+            part_sems.at[0, offset],
+            part_sems.at[1, offset],
+            "dp",
+            peer,
+        )
+
+    over_peers("dp", lambda offset, peer: part_copy(offset, peer).start())
+    got_ref[data_at] = part_ref[data_at]
+    over_peers("dp", lambda offset, peer: part_copy(offset, peer).wait())
+    summed = got_ref[0]
+    for d in range(1, ndata):
+        summed = summed + got_ref[d]
+    for at in range(piece_ref.shape[0]):
+        r, l = divmod(at, across)
+        piece_ref[at] = summed[8 * r : 8 * r + 8, lanes * l : lanes * (l + 1)]
+
+    def piece_copy(offset, peer):
+        return put_copy(
+            piece_ref.at[peer],
+            arrived_ref.at[col_at],
+            piece_sems.at[0, offset],
+            piece_sems.at[1, offset],
+            "cols",
+            peer,
+        )
+
+    over_peers("cols", lambda offset, peer: piece_copy(offset, peer).start())
+    arrived_ref[col_at] = piece_ref[col_at]
+    weight = weight_ref[...]
+    shared_ref[col_at, 1] = jnp.sum(weight, axis=0)
+    shared_ref[col_at, 2] = jnp.sum((weight > 0.0).astype(jnp.float32), axis=0)
+    over_peers("cols", lambda offset, peer: piece_copy(offset, peer).wait())
+    shared_ref[col_at, 0] = jnp.sum(arrived_ref[...], axis=0)
+
+    def shared_copy(offset, peer):
+        return put_copy(
+            shared_ref.at[col_at],
+            shared_ref.at[col_at],
+            shared_sems.at[0, offset],
+            shared_sems.at[1, offset],
+            "cols",
+            peer,
+        )
+
+    exchange("cols", shared_copy)
+    for r in range(chunk // 8):
+        row = [shared_ref[r * across + l, 0] for l in range(across)]
+        gram_ref[data_at, pl.ds(8 * r, 8), :] = jnp.concatenate(row, axis=1)
+
+    def gram_copy(offset, peer):
+        return put_copy(
+            gram_ref.at[data_at],
+            gram_ref.at[data_at],
+            gram_sems.at[0, offset],
+            gram_sems.at[1, offset],
+            "dp",
+            peer,
+        )
+
+    over_peers("dp", lambda offset, peer: gram_copy(offset, peer).start())
+    totals_ref[0] = jnp.sum(shared_ref[:, 1], axis=0)
+    totals_ref[1] = jnp.sum(shared_ref[:, 2], axis=0)
+    over_peers("dp", lambda offset, peer: gram_copy(offset, peer).wait())
+
+
+def sum_gram(sketch, weights):
+    ndata, chunk, size = sketch.shape
+    ncols = lax.axis_size("cols")
+    width = ndata * chunk
+    f32 = jnp.float32
+    tile = weights.shape[1:]
+    assert ncols * tile[0] * tile[1] == chunk * width
+    dma = pltpu.SemaphoreType.DMA
+    return pl.pallas_call(
+        gram_kernel,
+        out_shape=(
+            jax.ShapeDtypeStruct((ndata, chunk, size), f32),
+            jax.ShapeDtypeStruct((ndata, chunk, width), f32),
+            jax.ShapeDtypeStruct((2, *tile), f32),
+        ),
+        in_specs=[vmem(), vmem()],
+        out_specs=(vmem(), vmem(), vmem()),
+        scratch_shapes=[
+            pltpu.VMEM((ndata, chunk, width), f32),
+            pltpu.VMEM((ndata, chunk, width), f32),
+            pltpu.VMEM((ncols, *tile), f32),
+            pltpu.VMEM((ncols, *tile), f32),
+            pltpu.VMEM((ncols, 3, *tile), f32),
+            dma((2, ndata)),
+            dma((2, ndata)),
+            dma((2, ncols)),
+            dma((2, ncols)),
+            dma((2, ndata)),
+        ],
+        compiler_params=pltpu.CompilerParams(
+            collective_id=1, has_side_effects=True, vmem_limit_bytes=24 * 2**20
+        ),
+        name="gram",
+    )(sketch, weights)
+
+
+def corner_inverse(tile, pivots=8):
+    n = tile.shape[0]
+    blocks = n // pivots
+
+    def full(x):
+        return jnp.broadcast_to(x, (pivots, n))
+
+    work = [tile[pivots * i : pivots * (i + 1), :] for i in range(blocks)]
+    lane = lax.broadcasted_iota(jnp.int32, (pivots, n), 1)
+    sub = lax.broadcasted_iota(jnp.int32, (pivots, n), 0)
+    done = []
+    for at in range(blocks):
+        start = at * pivots
+        group = (lane >= start) & (lane < start + pivots)
+        cols = [full(work[at][:, start + c : start + c + 1]) for c in range(pivots)]
+        left = [[full(cols[c][r : r + 1, :]) for c in range(r + 1)] for r in range(pivots)]
+        rows = [
+            jnp.where(group, jnp.where(lane == start + r, 1.0, 0.0), full(work[at][r : r + 1, :]))
+            for r in range(pivots)
+        ]
+        recip = [None] * pivots
+        low = [[None] * pivots for _ in range(pivots)]
+        for c in range(pivots):
+            recip[c] = 1.0 / left[c][c]
+            for r in range(c + 1, pivots):
+                low[r][c] = left[r][c] * recip[c]
+                for e in range(c + 1, r + 1):
+                    left[r][e] = left[r][e] - low[r][c] * left[e][c]
+        for r in range(pivots):
+            for c in range(r):
+                rows[r] = rows[r] - low[r][c] * rows[c]
+        result = jnp.zeros((pivots, n), jnp.float32)
+        for r in range(pivots):
+            result = jnp.where(sub == r, rows[r] * lax.rsqrt(left[r][r]), result)
+        done.append(jnp.where(lane <= sub + start, result, 0.0))
+        back = [rows[r] * recip[r] for r in range(pivots)]
+        for r in range(pivots - 1, -1, -1):
+            for c in range(r):
+                back[c] = back[c] - low[r][c] * back[r]
+        for i in range(at + 1, blocks):
+            rest = jnp.where(group, 0.0, work[i])
+            for c in range(pivots):
+                rest = rest - full(work[i][:, start + c : start + c + 1]) * back[c]
+            work[i] = rest
+    return jnp.concatenate(done, axis=0)
+
+
+def factor_kernel(scale, corner_size, gram_ref, rows_ref, basis_ref, half_ref, work_ref, inverse_ref):
+    n = gram_ref.shape[0]
+    work_ref[...] = gram_ref[...]
+    row_at = lax.broadcasted_iota(jnp.int32, (n, n), 0)
+    col_at = lax.broadcasted_iota(jnp.int32, (n, n), 1)
+    inverse_ref[...] = jnp.where(row_at == col_at, 1.0, 0.0)
+
+    def step(k, carry):
+        at = pl.ds(pl.multiple_of(k * corner_size, corner_size), corner_size)
+        corner = corner_inverse(work_ref[at, at])
+        row = dot_exact(corner, inverse_ref[at, :], ((1,), (0,)))
+        low = dot_exact(work_ref[:, at], corner, ((1,), (1,)))
+        below = lax.broadcasted_iota(jnp.int32, low.shape, 0) >= (k + 1) * corner_size
+        low = jnp.where(below, low, 0.0)
+        work_ref[...] -= dot_exact(low, low, ((1,), (1,)))
+        inverse_ref[...] -= dot_exact(low, row, ((1,), (0,)))
+        inverse_ref[at, :] = row
+        return carry
+
+    lax.fori_loop(0, n // corner_size, step, 0)
+    q = dot_exact(inverse_ref[...], rows_ref[...], ((1,), (0,)))
+    half_ref[...] = q.astype(jnp.bfloat16)
+    basis_ref[...] = scale * q.T
+
+
+def factor_and_q(gram, rows, scale):
+    width, size = rows.shape
+    return pl.pallas_call(
+        functools.partial(factor_kernel, scale, 128),
+        out_shape=(
+            jax.ShapeDtypeStruct((size, width), jnp.float32),
+            jax.ShapeDtypeStruct((width, size), jnp.bfloat16),
+        ),
+        in_specs=[vmem(), vmem()],
+        out_specs=(vmem(), vmem()),
+        scratch_shapes=[pltpu.VMEM((width, width), jnp.float32)] * 2,
+        compiler_params=pltpu.CompilerParams(vmem_limit_bytes=24 * 2**20),
+        name="factor",
+    )(gram, rows)
+
+
 def shards(prefix_ids, suffix_ids, weights, counts, omega):
     ncols = lax.axis_size("cols")
     ndata = lax.axis_size("dp")
@@ -91,14 +428,10 @@
     prefix_local = prefix_ids.reshape(ncols, slots) & (block - 1)
     suffix_local = suffix_ids.reshape(ncols, slots) & (block - 1)
     packed = prefix_local * block + suffix_local
-
-    own = (packed, live_weights)
-    here = [lax.all_to_all(x, "cols", split_axis=0, concat_axis=0, tiled=True) for x in own]
-    here_ids, here_weights = [lax.all_gather(x, "dp", axis=1) for x in here]
-    mine_ids, mine_weights = [lax.all_gather(x, "dp", axis=1) for x in own]
-    live_rows, total_weight = lax.psum(
-        (jnp.sum(live.astype(jnp.float32)), jnp.sum(live_weights)), ("dp", "cols")
-    )
+    own = jnp.stack([packed.astype(jnp.float32), live_weights], axis=1)
+    here, mine = exchange_records(own)
+    here_ids, here_weights = here[:, :, 0].astype(jnp.int32).swapaxes(0, 1), here[:, :, 1].swapaxes(0, 1)
+    mine_ids, mine_weights = mine[:, :, 0].astype(jnp.int32).swapaxes(0, 1), mine[:, :, 1].swapaxes(0, 1)
 
     part = lax.dynamic_slice_in_dim(omega, data_at * chunk, chunk, 1)
     part = part.reshape(ndata, size, chunk).swapaxes(1, 2).reshape(ndata * chunk, size)
@@ -107,25 +440,19 @@
     sketch = move(
         "sketch", tables, here_ids & (block - 1), here_ids >> shift, here_weights, chunk
     )
-    sketch_rows = lax.all_to_all(
-        sketch.reshape(ndata, chunk, size), "dp", split_axis=0, concat_axis=0, tiled=True
-    ).reshape(width, size)
-    gram = lax.psum(dot_exact(sketch_rows, sketch_rows, ((1,), (1,))), ("dp", "cols"))
-    lower = jnp.linalg.cholesky(gram)
-    identity = jnp.eye(width, dtype=jnp.float32)
-    inverse_factor = jax.scipy.linalg.solve_triangular(lower, identity, lower=True)
-    q_part = dot_exact(inverse_factor, sketch_rows, ((1,), (0,)))
+    rows, gram, totals = sum_gram(sketch.reshape(ndata, chunk, size), mine_weights)
     scale = math.sqrt(block * ncols)
-    basis = lax.all_gather(scale * q_part.T, "dp", axis=0, tiled=True)
-
-    q_half = q_part.astype(jnp.bfloat16).reshape(ndata, chunk, size)
+    basis_part, q_half = factor_and_q(gram.reshape(width, width), rows.reshape(width, size), scale)
+    basis = lax.all_gather(basis_part, "dp", axis=0, tiled=True)
+
+    q_half = q_half.reshape(ndata, chunk, size)
     q_chunk = lax.all_to_all(q_half, "dp", split_axis=0, concat_axis=0, tiled=True)
     q_tables = lax.all_gather(q_chunk.reshape(width, size), "cols", axis=0)
     sums = move(
         "project", q_tables, mine_ids >> shift, mine_ids & (block - 1), mine_weights, chunk
     )
     sums = sums.reshape(ndata, chunk, size).swapaxes(0, 1).reshape(chunk, block)
-    coefficients = (scale * live_rows / total_weight) * sums
+    coefficients = (scale * jnp.sum(totals[1]) / jnp.sum(totals[0])) * sums
     return (basis, coefficients)
 
 

time: 781 us -> 410 us (0.52); the launches traced: 767 us -> 409 us
  blocking collectives: 219 us -> 12.1 us
  other arithmetic: 130 us -> 2.89 us
  Pallas kernels: 61.1 us -> 184 us
  waiting for transfers between devices: 272 us -> 181 us
  local copies, waits for them, and re-layouts: 34.2 us -> 14.5 us
  matrix products: 17.6 us -> 0 us
  starting transfers between devices: 15.9 us -> 0.12 us
    psum x1 -> x0, waiting for transfers between devices: 263 us -> none  [shards(): lax.psum(dot_exact(sketch_rows, sketch_rows, ((1,), (1,))), ('dp', 'cols'))]
    pallas_call x0 -> x3, Pallas kernels: none -> 123 us  [the longest x1 65.7 us: sum_gram(): pl.pallas_call(gram_kernel, out_shape=(jax.ShapeDtypeStruct((ndata, chunk...]
    another operation x17 -> x1, other arithmetic: 123 us -> 0.65 us  [shards(): own = jnp.stack([packed.astype(jnp.float32), live_weights], axis=1)]
    all_gather x4 -> x0, blocking collectives: 114 us -> none  [the longest x2 57.4 us: shards(): here_ids, here_weights = [lax.all_gather(x, 'dp', axis=1) for x in here]]
    psum x1 -> x0, blocking collectives: 76.7 us -> none  [shards(): lax.psum((jnp.sum(live.astype(jnp.float32)), jnp.sum(live_weights)), ('dp...]
    all_gather x1, waiting for transfers between devices: 2.29 us -> 73 us  [shards(): q_tables = lax.all_gather(q_chunk.reshape(width, size), 'cols', axis=0)]
    all_gather x1, waiting for transfers between devices: 0.02 us -> 58.6 us  [shards(): basis = lax.all_gather(basis_part, 'dp', axis=0, tiled=True)]
    all_gather x1, waiting for transfers between devices: 0.02 us -> 49 us  [shards(): tables = lax.all_gather(part, 'cols', axis=0)]
  transfers between devices with their start and end apart: 6 -> 3, of which waited for: 3 -> 3; matrix products, arithmetic and copies ran while one was open for 1% -> 1% of each run, Pallas kernels for 0% -> 6%
where the time goes in v2:
time: 410 us; the launch traced here: 409 us
  Pallas kernels  184 us (45%)
  waiting for transfers between devices  181 us (44%)
  between operations  15.1 us (4%)
  local copies, waits for them, and re-layouts  14.5 us (4%)
  blocking collectives  12.1 us (3%)
    all_gather x1, waiting for transfers between devices, shards(): q_tables = lax.all_gather(q_chunk.reshape(width, size), 'cols', axis=0)  73 us
    pallas_call x1, Pallas kernels, sum_gram(): pl.pallas_call(gram_kernel, out_shape=(jax.ShapeDtypeStruct((ndata, chunk...  65.7 us
    pallas_call x2, Pallas kernels, move(): pl.pallas_call(functools.partial(move_kernel, width), out_shape=jax.Shape...  61.1 us
    all_gather x1, waiting for transfers between devices, shards(): basis = lax.all_gather(basis_part, 'dp', axis=0, tiled=True)  58.6 us
    all_gather x1, waiting for transfers between devices, shards(): tables = lax.all_gather(part, 'cols', axis=0)  49 us
    pallas_call x1, Pallas kernels, factor_and_q(): pl.pallas_call(functools.partial(factor_kernel, scale, 128), out_shape=(j...  32.6 us
    pallas_call x1, Pallas kernels, exchange_records(): pl.pallas_call(records_kernel, out_shape=(gathered, gathered), in_specs=[...  24.7 us
    all_to_all x1, blocking collectives, shards(): lax.all_to_all(q_half, 'dp', split_axis=0, concat_axis=0, tiled=True)  12.1 us
  transfers between devices with their start and end apart: 3, of which 3 were waited for; matrix products, arithmetic and copies ran while one was open for 1% of the time, Pallas kernels for 6%

profile of v2, /device:TPU:1, one launch (start us, length us, event | category | flops | bytes accessed | tf_op | source)
XLA Modules:
  0.0 409.4 jit_solution(2630320284142001610)
XLA Ops:
  7.2 0.0 copy-start
  7.2 0.0 all-gather.4.cloned.1.call-start
  7.2 1.5 copy-done
  8.8 0.2 constant_dynamic-slice_fusion
  9.0 0.9 copy.26
  9.9 0.0 all-gather.4.cloned.1.call-update
  9.9 0.0 all-gather.6.cloned.1.call-start
  9.9 0.8 compare_select_fusion
  10.8 0.7 add_convert_fusion
  11.5 0.6 pad_maximum_fusion.own_ref
  12.2 24.7 %records.1 = (f32[8,32,2,128]{3,2,1,0:T(2,128)}, f32[8,32,2,128]{3,2,1,0:T(2,128)}) custom-call(f32[32,2,128]{2,1,0:T(2,128)} %pad_maximum_fusion.own_ref), custom_call_target="tpu_custom_call" | custom-call | tf_op jit(solution)/shard_map/records/pallas_call | solution.py:169
  36.9 1.1 copy.27
  38.0 1.1 copy.29
  39.2 49.0 %all-gather.4.cloned.1.call-done.table_ref = bf16[32,512,256]{2,1,0:T(8,128)(2,1)} async-done(((bf16[1,512,256]{2,1,0:T(8,128)(2,1)}), bf16[32,512,256]{2,1,0:T(8,128)(2,1)}) %all-gather.4.cloned.1.call-update) | async-done | bytes 8388624 | tf_op jit(solution)/shard_map/all_gather | solution.py:438
  88.2 0.0 copy-start.1
  88.2 3.4 copy-done.1
  91.6 30.5 %sketch.1 = f32[512,256]{1,0:T(8,128)S(1)} custom-call(bf16[32,512,256]{2,1,0:T(8,128)(2,1)S(1)} %copy-done.1, s32[32,8,128]{2,1,0:T(8,128)S(1)} %get-tuple-element.21.take_ref, s32[32,8,128]{2,1,0:T(8,128)S(1)} %get-tuple-element.20.put_ref, f32[32,8,128]{2,1,0:T(8,128)S(1)} %slice_bitcast_fusion.1.weight_ref), custom_call_target="tpu_custom_call" | custom-call | tf_op jit(solution)/shard_map/sketch/pallas_call | solution.py:69
  122.2 65.7 %gram.1 = (f32[8,64,256]{2,1,0:T(8,128)S(1)}, f32[8,64,512]{2,1,0:T(8,128)S(1)}, f32[2,8,128]{2,1,0:T(8,128)S(1)}) custom-call(f32[8,64,256]{2,1,0:T(8,128)S(1)} %bitcast.42, f32[32,8,128]{2,1,0:T(8,128)S(1)} %slice_bitcast_fusion.weight_ref), custom_call_target="tpu_custom_call" | custom-call | tf_op jit(solution)/shard_map/gram/pallas_call | solution.py:301
  187.8 32.6 %factor.1 = (f32[256,512]{1,0:T(8,128)}, bf16[512,256]{1,0:T(8,128)(2,1)S(1)}) custom-call(f32[512,512]{1,0:T(8,128)S(1)} %bitcast.43, f32[512,256]{1,0:T(8,128)S(1)} %bitcast.44), custom_call_target="tpu_custom_call" | custom-call | tf_op jit(solution)/shard_map/factor/pallas_call | solution.py:403
  220.5 0.0 all-gather.6.cloned.1.call-update
  220.5 0.0 all-gather.8.cloned.1.call-start
  220.5 12.1 %all_to_all.5 = bf16[8,64,256]{2,1,0:T(8,128)(2,1)} all-to-all(bf16[8,64,256]{2,1,0:T(8,128)(2,1)S(1)} %bitcast.45), channel_id=1, replica_groups=mesh['dp'=8,'cols'=32] {'dp'}, dimensions={0} | all-to-all | bytes 524288 | tf_op jit(solution)/shard_map/all_to_all | solution.py:449
  232.6 0.0 all-gather.8.cloned.1.call-update
  232.7 0.6 slice_reduce_fusion
  234.5 58.6 %all-gather.6.cloned.1.call-done = f32[2048,512]{1,0:T(8,128)} async-done(((f32[256,512]{1,0:T(8,128)}), f32[2048,512]{1,0:T(8,128)}) %all-gather.6.cloned.1.call-update) | async-done | bytes 4194320 | tf_op jit(solution)/shard_map/all_gather | solution.py:446
  293.1 73.0 %all-gather.8.cloned.1.call-done.table_ref = bf16[32,512,256]{2,1,0:T(8,128)(2,1)} async-done(((bf16[1,512,256]{2,1,0:T(8,128)(2,1)}), bf16[32,512,256]{2,1,0:T(8,128)(2,1)}) %all-gather.8.cloned.1.call-update) | async-done | bytes 8388624 | tf_op jit(solution)/shard_map/all_gather | solution.py:450
  366.1 0.0 copy-start.2
  366.1 3.4 copy-done.2
  369.5 0.0 copy-start.3
  369.5 30.5 %project.1 = f32[512,256]{1,0:T(8,128)S(1)} custom-call(bf16[32,512,256]{2,1,0:T(8,128)(2,1)S(1)} %copy-done.2, s32[32,8,128]{2,1,0:T(8,128)S(1)} %get-tuple-element.19.take_ref, s32[32,8,128]{2,1,0:T(8,128)S(1)} %get-tuple-element.18.put_ref, f32[32,8,128]{2,1,0:T(8,128)S(1)} %slice_bitcast_fusion.weight_ref), custom_call_target="tpu_custom_call" | custom-call | tf_op jit(solution)/shard_map/project/pallas_call | solution.py:69
  400.1 0.8 copy.34
  400.9 0.0 copy-done.3
  400.9 2.0 copy.36
  (5 shorter events, 0.1 us)
Async XLA Ops:
  7.2 1.6 copy-start
  7.2 81.1 %all-gather.4.cloned.1.call-start = ((), (), s32[]{:S(2)}) async-start(), calls=%async_computation.1 | async-start | bytes 8650752 | tf_op jit(solution)/shard_map/all_gather | solution.py:438
  9.9 283.2 %all-gather.6.cloned.1.call-start = ((), (), s32[]{:S(2)}) async-start(), calls=%async_computation.2 | async-start | bytes 4718592 | tf_op jit(solution)/shard_map/all_gather | solution.py:446
  88.2 3.4 copy-start.1
  220.5 145.6 %all-gather.8.cloned.1.call-start = ((), (), s32[]{:S(2)}) async-start(), calls=%async_computation.3 | async-start | bytes 8650752 | tf_op jit(solution)/shard_map/all_gather | solution.py:450
  366.1 3.4 copy-start.2
  369.5 31.4 %copy-start.3 = (f32[2048,512]{1,0:T(8,128)S(1)}, f32[2048,512]{1,0:T(8,128)}, u32[]{:S(2)}) copy-start(f32[2048,512]{1,0:T(8,128)} %all-gather.6.cloned.1.call-done) | copy-start | bytes 12582916
Sparse Core Ops, SparseCore 0:
  10.4 77.7 all-gather.3
  220.6 72.4 all-gather.5
  295.0 71.0 all-gather.7

commit v3 on v2

--- a/solution.py
+++ b/solution.py
@@ -47,36 +47,6 @@
     )
 
 
-def move_kernel(width, table_ref, take_ref, put_ref, weight_ref, total_ref):
-    @pl.when(pl.program_id(0) == 0)
-    def _():
-        total_ref[...] = jnp.zeros_like(total_ref)
-
-    rows = range(take_ref.shape[1])
-    total_ref[...] += move_block(
-        table_ref[0],
-        [take_ref[0, r : r + 1, :] for r in rows],
-        [put_ref[0, r : r + 1, :] for r in rows],
-        [weight_ref[0, r : r + 1, :] for r in rows],
-        width,
-    )
-
-
-def move(name, tables, take, put, weight, width):
-    blocks, stacked, size = tables.shape
-    _, parts, slots = take.shape
-    records = pl.BlockSpec((1, parts, slots), lambda i: (i, 0, 0))
-    return pl.pallas_call(
-        functools.partial(move_kernel, width),
-        out_shape=jax.ShapeDtypeStruct((stacked, size), jnp.float32),
-        grid=(blocks,),
-        in_specs=[pl.BlockSpec((1, stacked, size), lambda i: (i, 0, 0)), records, records, records],
-        out_specs=pl.BlockSpec((stacked, size), lambda i: (0, 0)),
-        compiler_params=pltpu.CompilerParams(vmem_limit_bytes=40 * 2**20),
-        name=name,
-    )(tables, take, put, weight)
-
-
 def vmem():
     return pl.BlockSpec(memory_space=pltpu.VMEM)
 
@@ -183,7 +153,7 @@
 
 def gram_kernel(
     sketch_ref,
-    weight_ref,
+    mine_ref,
     rows_ref,
     gram_ref,
     totals_ref,
@@ -253,9 +223,10 @@
 
     over_peers("cols", lambda offset, peer: piece_copy(offset, peer).start())
     arrived_ref[col_at] = piece_ref[col_at]
-    weight = weight_ref[...]
-    shared_ref[col_at, 1] = jnp.sum(weight, axis=0)
-    shared_ref[col_at, 2] = jnp.sum((weight > 0.0).astype(jnp.float32), axis=0)
+    weight = mine_ref[:, :, 1, :]
+    for at, term in ((1, weight), (2, (weight > 0.0).astype(jnp.float32))):
+        term = jnp.sum(term, axis=0).reshape(-1, *shared_ref.shape[2:])
+        shared_ref[col_at, at] = jnp.sum(term, axis=0)
     over_peers("cols", lambda offset, peer: piece_copy(offset, peer).wait())
     shared_ref[col_at, 0] = jnp.sum(arrived_ref[...], axis=0)
 
@@ -290,12 +261,12 @@
     over_peers("dp", lambda offset, peer: gram_copy(offset, peer).wait())
 
 
-def sum_gram(sketch, weights):
+def sum_gram(sketch, mine):
     ndata, chunk, size = sketch.shape
     ncols = lax.axis_size("cols")
     width = ndata * chunk
     f32 = jnp.float32
-    tile = weights.shape[1:]
+    tile = (8, mine.shape[-1])
     assert ncols * tile[0] * tile[1] == chunk * width
     dma = pltpu.SemaphoreType.DMA
     return pl.pallas_call(
@@ -323,7 +294,7 @@
             collective_id=1, has_side_effects=True, vmem_limit_bytes=24 * 2**20
         ),
         name="gram",
-    )(sketch, weights)
+    )(sketch, mine)
 
 
 def corner_inverse(tile, pivots=8):
@@ -373,7 +344,7 @@
     return jnp.concatenate(done, axis=0)
 
 
-def factor_kernel(scale, corner_size, gram_ref, rows_ref, basis_ref, half_ref, work_ref, inverse_ref):
+def factor_kernel(corner_size, gram_ref, rows_ref, basis_ref, half_ref, work_ref, inverse_ref):
     n = gram_ref.shape[0]
     work_ref[...] = gram_ref[...]
     row_at = lax.broadcasted_iota(jnp.int32, (n, n), 0)
@@ -395,15 +366,15 @@
     lax.fori_loop(0, n // corner_size, step, 0)
     q = dot_exact(inverse_ref[...], rows_ref[...], ((1,), (0,)))
     half_ref[...] = q.astype(jnp.bfloat16)
-    basis_ref[...] = scale * q.T
-
-
-def factor_and_q(gram, rows, scale):
+    basis_ref[...] = q.T.astype(jnp.bfloat16)
+
+
+def factor_and_q(gram, rows):
     width, size = rows.shape
     return pl.pallas_call(
-        functools.partial(factor_kernel, scale, 128),
+        functools.partial(factor_kernel, 128),
         out_shape=(
-            jax.ShapeDtypeStruct((size, width), jnp.float32),
+            jax.ShapeDtypeStruct((size, width), jnp.bfloat16),
             jax.ShapeDtypeStruct((width, size), jnp.bfloat16),
         ),
         in_specs=[vmem(), vmem()],
@@ -414,6 +385,246 @@
     )(gram, rows)
 
 
+class Ring:
+    def __init__(self, all_ref, got_sems, ring_sems, pair_sems, across_sem):
+        self.all_ref, self.got_sems = all_ref, got_sems
+        self.ring_sems, self.pair_sems, self.across_sem = ring_sems, pair_sems, across_sem
+        at = lax.axis_index("cols")
+        self.length = lax.axis_size("cols") // 4
+        self.z, quad = at // 4, lax.rem(at, 4)
+        self.y, self.core = quad // 2, lax.rem(quad, 2)
+        self.way = 1 - 2 * self.core
+        self.pair = self.device(self.z, self.y, 1 - self.core)
+        self.across = self.device(self.z, 1 - self.y, self.core)
+        self.after = self.device(self.z + self.way, self.y, self.core)
+        self.before = self.device(self.z - self.way, self.y, self.core)
+
+    def device(self, z, y, core):
+        z = lax.rem(z + self.length, self.length)
+        return z * 4 + y * 2 + core
+
+    def quad_slot(self, z, turn, core):
+        y = lax.rem(self.y + lax.rem(turn, 2), 2)
+        return self.device(z, y, lax.rem(core + turn // 2, 2))
+
+    def greet(self, others=()):
+        barrier = pltpu.get_barrier_semaphore()
+        for peer in (self.pair, self.across, self.after, self.before):
+            pl.semaphore_signal(
+                barrier, inc=1, device_id={"cols": peer}, device_id_type=pl.DeviceIdType.MESH
+            )
+        for axis in others:
+            over_peers(
+                axis,
+                lambda offset, peer, axis=axis: pl.semaphore_signal(
+                    barrier, inc=1, device_id={axis: peer}, device_id_type=pl.DeviceIdType.MESH
+                ),
+            )
+        pl.semaphore_wait(barrier, 4 + sum(lax.axis_size(axis) - 1 for axis in others))
+
+    def copy(self, slot, send, peer):
+        part = self.all_ref.at[slot]
+        return put_copy(part, part, send, self.got_sems.at[slot], "cols", peer)
+
+    def arrived(self, slot):
+        self.copy(slot, self.across_sem.at[0], self.pair).wait_recv()
+
+    def run(self, work, begun=None):
+        steps = 4 * (self.length // 2) - 2
+
+        def near(turn, carry):
+            slot = self.quad_slot(self.z, turn, self.core)
+
+            @pl.when(turn > 0)
+            def _():
+                self.arrived(slot)
+
+            self.copy(slot, self.ring_sems.at[turn], self.after).start()
+
+            @pl.when(turn < 2)
+            def _():
+                self.copy(slot, self.pair_sems.at[turn], self.pair).start()
+
+            @pl.when(turn == 0)
+            def _():
+                self.copy(slot, self.across_sem.at[0], self.across).start()
+
+            work(slot)
+            return carry
+
+        lax.fori_loop(0, 4, near, 0)
+        if begun is not None:
+            begun()
+
+        def far(step, carry):
+            turn, away = lax.rem(step, 4), step // 4 + 1
+            slot = self.quad_slot(self.z - self.way * away, turn, self.core)
+            self.arrived(slot)
+
+            @pl.when(step < steps - 4)
+            def _():
+                self.copy(slot, self.ring_sems.at[step + 4], self.after).start()
+
+            self.copy(slot, self.pair_sems.at[step + 2], self.pair).start()
+            work(slot)
+            slot = self.quad_slot(self.z + self.way * away, turn, 1 - self.core)
+            self.arrived(slot)
+            work(slot)
+            return carry
+
+        lax.fori_loop(0, steps, far, 0)
+        own = self.device(self.z, self.y, self.core)
+
+        def sent(sems):
+            def one(at, carry):
+                self.copy(own, sems.at[at], self.pair).wait_send()
+                return carry
+
+            lax.fori_loop(0, sems.shape[0], one, 0)
+
+        sent(self.ring_sems)
+        sent(self.pair_sems)
+        sent(self.across_sem)
+
+
+def ring_scratch(table):
+    ncols = lax.axis_size("cols")
+    moved = 4 * (ncols // 8) - 2
+    dma = pltpu.SemaphoreType.DMA
+    return [
+        pltpu.VMEM((ncols, *table), jnp.bfloat16),
+        dma((ncols,)),
+        dma((moved,)),
+        dma((moved + 2,)),
+        dma((1,)),
+    ]
+
+
+def block_sums(table, records_ref, slot, block, width, by_prefix):
+    shift = block.bit_length() - 1
+    rows = range(records_ref.shape[0])
+    packed = [records_ref[d, slot, 0:1, :].astype(jnp.int32) for d in rows]
+    weight = [records_ref[d, slot, 1:2, :] for d in rows]
+    prefix = [lax.shift_right_logical(ids, shift) for ids in packed]
+    suffix = [ids & (block - 1) for ids in packed]
+    take, put = (prefix, suffix) if by_prefix else (suffix, prefix)
+    return move_block(table, take, put, weight, width)
+
+
+def sketch_kernel(block, width, part_ref, here_ref, total_ref, all_ref, *sems):
+    ring = Ring(all_ref, *sems)
+    ring.greet()
+    all_ref[lax.axis_index("cols")] = part_ref[...]
+    total_ref[...] = jnp.zeros_like(total_ref)
+
+    def work(slot):
+        total_ref[...] += block_sums(all_ref[slot], here_ref, slot, block, width, False)
+
+    ring.run(work)
+
+
+def sketch_sums(part, here, block, width):
+    return pl.pallas_call(
+        functools.partial(sketch_kernel, block, width),
+        out_shape=jax.ShapeDtypeStruct(part.shape, jnp.float32),
+        in_specs=[vmem(), vmem()],
+        out_specs=vmem(),
+        scratch_shapes=ring_scratch(part.shape),
+        compiler_params=pltpu.CompilerParams(
+            collective_id=2, has_side_effects=True, vmem_limit_bytes=40 * 2**20
+        ),
+        name="sketch",
+    )(part, here)
+
+
+def project_kernel(
+    scale,
+    block,
+    width,
+    half_ref,
+    basis_ref,
+    mine_ref,
+    totals_ref,
+    coef_ref,
+    whole_ref,
+    total_ref,
+    half_sems,
+    basis_sems,
+    own_sem,
+    all_ref,
+    *sems,
+):
+    ring = Ring(all_ref, *sems)
+    ring.greet(["dp"])
+    data_at, col_at = lax.axis_index("dp"), lax.axis_index("cols")
+    size = basis_ref.shape[0]
+    own_rows = pl.ds(pl.multiple_of(data_at * width, width), width)
+
+    def half_copy(offset, peer):
+        return put_copy(
+            half_ref.at[pl.ds(pl.multiple_of(peer * width, width), width), :],
+            all_ref.at[col_at, own_rows, :],
+            half_sems.at[0, offset],
+            half_sems.at[1, offset],
+            "dp",
+            peer,
+        )
+
+    own_basis = whole_ref.at[pl.ds(pl.multiple_of(data_at * size, size), size), :]
+
+    def basis_copy(offset, peer):
+        return put_copy(
+            basis_ref, own_basis, basis_sems.at[0, offset], basis_sems.at[1, offset], "dp", peer
+        )
+
+    own_copy = pltpu.make_async_copy(basis_ref, own_basis, own_sem)
+
+    def begun():
+        over_peers("dp", lambda offset, peer: basis_copy(offset, peer).start())
+        own_copy.start()
+
+    def work(slot):
+        total_ref[...] += block_sums(all_ref[slot], mine_ref, slot, block, width, True)
+
+    over_peers("dp", lambda offset, peer: half_copy(offset, peer).start())
+    all_ref[col_at, own_rows, :] = half_ref[own_rows, :]
+    total_ref[...] = jnp.zeros_like(total_ref)
+    over_peers("dp", lambda offset, peer: half_copy(offset, peer).wait())
+    ring.run(work, begun)
+    factor = scale * jnp.sum(totals_ref[1]) / jnp.sum(totals_ref[0])
+    for g in range(total_ref.shape[0] // width):
+        coef_ref[:, g * size : (g + 1) * size] = factor * total_ref[g * width : (g + 1) * width, :]
+    over_peers("dp", lambda offset, peer: basis_copy(offset, peer).wait())
+    own_copy.wait()
+
+
+def project(half, basis_part, mine, totals, scale, block, width):
+    ndata = lax.axis_size("dp")
+    size, whole = basis_part.shape
+    dma = pltpu.SemaphoreType.DMA
+    anywhere = pl.BlockSpec(memory_space=pl.ANY)
+    return pl.pallas_call(
+        functools.partial(project_kernel, scale, block, width),
+        out_shape=(
+            jax.ShapeDtypeStruct((width, block), jnp.float32),
+            jax.ShapeDtypeStruct((size * ndata, whole), jnp.bfloat16),
+        ),
+        in_specs=[vmem(), anywhere, vmem(), vmem()],
+        out_specs=(vmem(), anywhere),
+        scratch_shapes=[
+            pltpu.VMEM(half.shape, jnp.float32),
+            dma((2, ndata)),
+            dma((2, ndata)),
+            dma,
+            *ring_scratch(half.shape),
+        ],
+        compiler_params=pltpu.CompilerParams(
+            collective_id=3, has_side_effects=True, vmem_limit_bytes=40 * 2**20
+        ),
+        name="project",
+    )(half, basis_part, mine, totals)
+
+
 def shards(prefix_ids, suffix_ids, weights, counts, omega):
     ncols = lax.axis_size("cols")
     ndata = lax.axis_size("dp")
@@ -430,29 +641,14 @@
     packed = prefix_local * block + suffix_local
     own = jnp.stack([packed.astype(jnp.float32), live_weights], axis=1)
     here, mine = exchange_records(own)
-    here_ids, here_weights = here[:, :, 0].astype(jnp.int32).swapaxes(0, 1), here[:, :, 1].swapaxes(0, 1)
-    mine_ids, mine_weights = mine[:, :, 0].astype(jnp.int32).swapaxes(0, 1), mine[:, :, 1].swapaxes(0, 1)
-
     part = lax.dynamic_slice_in_dim(omega, data_at * chunk, chunk, 1)
     part = part.reshape(ndata, size, chunk).swapaxes(1, 2).reshape(ndata * chunk, size)
-    tables = lax.all_gather(part, "cols", axis=0)
-    shift = block.bit_length() - 1
-    sketch = move(
-        "sketch", tables, here_ids & (block - 1), here_ids >> shift, here_weights, chunk
-    )
-    rows, gram, totals = sum_gram(sketch.reshape(ndata, chunk, size), mine_weights)
+    sketch = sketch_sums(part, here, block, chunk)
+    rows, gram, totals = sum_gram(sketch.reshape(ndata, chunk, size), mine)
+    basis_part, q_half = factor_and_q(gram.reshape(width, width), rows.reshape(width, size))
     scale = math.sqrt(block * ncols)
-    basis_part, q_half = factor_and_q(gram.reshape(width, width), rows.reshape(width, size), scale)
-    basis = lax.all_gather(basis_part, "dp", axis=0, tiled=True)
-
-    q_half = q_half.reshape(ndata, chunk, size)
-    q_chunk = lax.all_to_all(q_half, "dp", split_axis=0, concat_axis=0, tiled=True)
-    q_tables = lax.all_gather(q_chunk.reshape(width, size), "cols", axis=0)
-    sums = move(
-        "project", q_tables, mine_ids >> shift, mine_ids & (block - 1), mine_weights, chunk
-    )
-    sums = sums.reshape(ndata, chunk, size).swapaxes(0, 1).reshape(chunk, block)
-    coefficients = (scale * jnp.sum(totals[1]) / jnp.sum(totals[0])) * sums
+    coefficients, q_block = project(q_half, basis_part, mine, totals, scale, block, chunk)
+    basis = scale * q_block.astype(jnp.float32)
     return (basis, coefficients)
 
 

time: 410 us -> 239 us (0.58)
  waiting for transfers between devices: 181 us -> 0 us
  Pallas kernels: 184 us -> 230 us
  between operations: 15.1 us -> 0.74 us
  blocking collectives: 12.1 us -> 0 us
  local copies, waits for them, and re-layouts: 14.5 us -> 3.1 us
    all_gather x3 -> x0, waiting for transfers between devices: 181 us -> none  [the longest x1 73 us: shards(): q_tables = lax.all_gather(q_chunk.reshape(width, size), 'cols', axis=0)]
    pallas_call x3, Pallas kernels: 93.7 us -> 141 us  [the longest x1 56.8 us: project(): pl.pallas_call(functools.partial(project_kernel, scale, block, width), ou...]
    all_to_all x1 -> x0, blocking collectives: 12.1 us -> none  [shards(): lax.all_to_all(q_half, 'dp', split_axis=0, concat_axis=0, tiled=True)]
    unnamed x9, local copies, waits for them, and re-layouts: 10.3 us -> 2.69 us
  transfers between devices with their start and end apart: 3 -> 0, of which waited for: 3 -> 0; matrix products, arithmetic and copies ran while one was open for 1% -> 0% of each run, Pallas kernels for 6% -> 0%
where the time goes in v3:
time: 239 us
  Pallas kernels  230 us (96%)
  other arithmetic  4.96 us (2%)
  local copies, waits for them, and re-layouts  3.1 us (1%)
    pallas_call x1, Pallas kernels, sum_gram(): pl.pallas_call(gram_kernel, out_shape=(jax.ShapeDtypeStruct((ndata, chunk...  66 us
    pallas_call x1, Pallas kernels, project(): pl.pallas_call(functools.partial(project_kernel, scale, block, width), ou...  56.8 us
    pallas_call x1, Pallas kernels, sketch_sums(): pl.pallas_call(functools.partial(sketch_kernel, block, width), out_shape=...  52.6 us
    pallas_call x1, Pallas kernels, factor_and_q(): pl.pallas_call(functools.partial(factor_kernel, 128), out_shape=(jax.Shap...  32 us
    pallas_call x1, Pallas kernels, exchange_records(): pl.pallas_call(records_kernel, out_shape=(gathered, gathered), in_specs=[...  22.9 us

profile of v3, /device:TPU:1, one launch (start us, length us, event | category | flops | bytes accessed | tf_op | source)
XLA Modules:
  0.0 239.1 jit_solution(3777562176550140197)
XLA Ops:
  0.6 0.0 copy-start
  0.7 0.9 add_convert_fusion
  1.5 0.8 compare_select_fusion
  2.4 0.6 pad_maximum_fusion.own_ref
  3.0 22.9 %records.1 = (f32[8,32,2,128]{3,2,1,0:T(2,128)}, f32[8,32,2,128]{3,2,1,0:T(2,128)}) custom-call(f32[32,2,128]{2,1,0:T(2,128)} %pad_maximum_fusion.own_ref), custom_call_target="tpu_custom_call" | custom-call | tf_op jit(solution)/shard_map/records/pallas_call | solution.py:139
  25.9 0.0 copy-start.2
  25.9 0.0 copy-done
  25.9 0.2 constant_dynamic-slice_fusion
  26.2 0.2 copy.8
  26.4 0.0 copy-start.3
  26.4 0.9 copy-done.3
  27.3 52.6 %sketch.1 = f32[512,256]{1,0:T(8,128)S(1)} custom-call(bf16[512,256]{1,0:T(8,128)(2,1)S(1)} %bitcast.13, f32[8,32,2,128]{3,2,1,0:T(2,128)S(1)} %copy-done.3), custom_call_target="tpu_custom_call" | custom-call | tf_op jit(solution)/shard_map/sketch/pallas_call | solution.py:527
  80.0 0.0 copy-start.1
  80.0 0.9 copy-done.1
  80.9 66.0 %gram.1 = (f32[8,64,256]{2,1,0:T(8,128)S(1)}, f32[8,64,512]{2,1,0:T(8,128)S(1)}, f32[2,8,128]{2,1,0:T(8,128)S(1)}) custom-call(f32[8,64,256]{2,1,0:T(8,128)S(1)} %bitcast.11, f32[8,32,2,128]{3,2,1,0:T(2,128)S(1)} %copy-done.1), custom_call_target="tpu_custom_call" | custom-call | tf_op jit(solution)/shard_map/gram/pallas_call | solution.py:272
  146.9 32.0 %factor.1 = (bf16[256,512]{1,0:T(8,128)(2,1)S(1)}, bf16[512,256]{1,0:T(8,128)(2,1)S(1)}) custom-call(f32[512,512]{1,0:T(8,128)S(1)} %bitcast.12, f32[512,256]{1,0:T(8,128)S(1)} %bitcast.14), custom_call_target="tpu_custom_call" | custom-call | tf_op jit(solution)/shard_map/factor/pallas_call | solution.py:374
  178.9 0.0 copy-done.2
  178.9 56.8 %project.1 = (f32[64,2048]{1,0:T(8,128)S(1)}, bf16[2048,512]{1,0:T(8,128)(2,1)S(1)}) custom-call(bf16[512,256]{1,0:T(8,128)(2,1)S(1)} %get-tuple-element.15.half_ref, bf16[256,512]{1,0:T(8,128)(2,1)S(1)} %get-tuple-element.16.basis_ref, f32[8,32,2,128]{3,2,1,0:T(2,128)S(1)} %copy-done.2, f32[2,8,128]{2,1,0:T(8,128)S(1)} %get-tuple-element.17.totals_ref), custom_call_target="tpu_custom_call" | custom-call | tf_op jit(solution)/shard_map/project/pallas_call | solution.py:606
  235.7 2.6 %convert_multiply_fusion = f32[2048,512]{1,0:T(8,128)} fusion(bf16[2048,512]{1,0:T(8,128)(2,1)S(1)} %get-tuple-element.18), kind=kLoop, calls=%fused_computation | loop fusion | flops 2097152 | bytes 6291456 | tf_op jit(solution)/shard_map/mul | solution.py:651
  238.3 0.8 copy.12
Async XLA Ops:
  0.6 25.3 %copy-start = (bf16[2048,512]{1,0:T(8,128)(2,1)S(1)}, bf16[2048,512]{1,0:T(8,128)(2,1)}, u32[]{:S(2)}) copy-start(bf16[2048,512]{1,0:T(8,128)(2,1)} %param.9) | copy-start | bytes 6291460
  25.9 153.0 %copy-start.2 = (f32[8,32,2,128]{3,2,1,0:T(2,128)S(1)}, f32[8,32,2,128]{3,2,1,0:T(2,128)}, u32[]{:S(2)}) copy-start(f32[8,32,2,128]{3,2,1,0:T(2,128)} %get-tuple-element.12.mine_ref) | copy-start | bytes 786436
  26.4 1.0 copy-start.3
  80.0 1.0 copy-start.1

commit v4 on v3

--- a/solution.py
+++ b/solution.py
@@ -62,27 +62,31 @@
     )
 
 
-def over_peers(axis, act):
+def over_peers(axis, act, stride=1):
     count = lax.axis_size(axis)
     me = lax.axis_index(axis)
 
     def one(offset, carry):
-        act(offset, lax.rem(me + offset, count))
+        act(offset, lax.rem(me + stride * offset, count))
         return carry
 
-    lax.fori_loop(1, count, one, 0)
-
-
-def greet(*axes):
+    lax.fori_loop(1, count // stride, one, 0)
+
+
+def signal(barrier, axis, peer):
+    pl.semaphore_signal(
+        barrier, inc=1, device_id={axis: peer}, device_id_type=pl.DeviceIdType.MESH
+    )
+
+
+def greet(*groups, near=()):
     barrier = pltpu.get_barrier_semaphore()
-    for axis in axes:
-        over_peers(
-            axis,
-            lambda offset, peer, axis=axis: pl.semaphore_signal(
-                barrier, inc=1, device_id={axis: peer}, device_id_type=pl.DeviceIdType.MESH
-            ),
-        )
-    pl.semaphore_wait(barrier, sum(lax.axis_size(axis) - 1 for axis in axes))
+    for peer in near:
+        signal(barrier, "cols", peer)
+    for axis, stride in groups:
+        over_peers(axis, lambda offset, peer, axis=axis: signal(barrier, axis, peer), stride)
+    count = sum(lax.axis_size(axis) // stride - 1 for axis, stride in groups)
+    pl.semaphore_wait(barrier, count + len(near))
 
 
 def exchange(axis, make):
@@ -92,7 +96,7 @@
 
 def records_kernel(own_ref, here_ref, mine_ref, col_sems, here_sems, mine_sems):
     data_at, col_at = lax.axis_index("dp"), lax.axis_index("cols")
-    greet("cols", "dp")
+    greet(("cols", 1), ("dp", 1))
 
     def to_col(offset, peer):
         return put_copy(
@@ -151,6 +155,10 @@
     )(own)
 
 
+def lower_blocks(width, lanes):
+    return [(i, j) for i in range(width // lanes) for j in range(i + 1)]
+
+
 def gram_kernel(
     sketch_ref,
     mine_ref,
@@ -158,22 +166,36 @@
     gram_ref,
     totals_ref,
     part_ref,
+    half_ref,
+    other_ref,
     got_ref,
     piece_ref,
     arrived_ref,
     shared_ref,
+    own_ref,
+    sum_ref,
     rows_sems,
+    pair_sems,
     part_sems,
     piece_sems,
     shared_sems,
     gram_sems,
 ):
     data_at, col_at = lax.axis_index("dp"), lax.axis_index("cols")
+    core, chip = lax.rem(col_at, 2), col_at // 2
+    pair = col_at + 1 - 2 * core
     ndata, chunk, size = sketch_ref.shape
     width = ndata * chunk
-    lanes = piece_ref.shape[2]
-    across = width // lanes
-    greet("cols", "dp")
+    lanes = part_ref.shape[1]
+    half = half_ref.shape[0]
+    share = half // ndata
+    chips = piece_ref.shape[0]
+    few = share // chips
+
+    def rows_at(start, count):
+        return pl.ds(pl.multiple_of(start, 8), count)
+
+    greet(("dp", 1), ("cols", 2), near=(pair,))
 
     def rows_copy(offset, peer):
         return put_copy(
@@ -187,13 +209,41 @@
 
     over_peers("dp", lambda offset, peer: rows_copy(offset, peer).start())
     rows_ref[data_at] = sketch_ref[data_at]
+    weight = mine_ref[:, :, 1, :]
+    for at, term in ((0, weight), (1, (weight > 0.0).astype(jnp.float32))):
+        term = jnp.sum(term, axis=0).reshape(-1, *totals_ref.shape[1:])
+        sum_ref[0, at] = jnp.sum(term, axis=0)
+    sums_copy = put_copy(
+        sum_ref.at[0], sum_ref.at[1], pair_sems.at[0, 0], pair_sems.at[1, 0], "cols", pair
+    )
+    sums_copy.start()
+    piece_ref[...] = jnp.zeros_like(piece_ref)
     over_peers("dp", lambda offset, peer: rows_copy(offset, peer).wait())
     rows = rows_ref[...].reshape(width, size)
-    part_ref[...] = dot_exact(rows, rows, ((1,), (1,))).reshape(part_ref.shape)
+    gram = dot_exact(rows, rows, ((1,), (1,)))
+    for at, (i, j) in enumerate(lower_blocks(width, lanes)):
+        part_ref[lanes * at : lanes * (at + 1), :] = gram[
+            lanes * i : lanes * (i + 1), lanes * j : lanes * (j + 1)
+        ]
+
+    pair_copy = put_copy(
+        part_ref.at[rows_at((1 - core) * half, half), :],
+        other_ref,
+        pair_sems.at[0, 1],
+        pair_sems.at[1, 1],
+        "cols",
+        pair,
+    )
+    pair_copy.start()
+    sums_copy.wait()
+    shared_ref[chip, 1] = sum_ref[0, 0] + sum_ref[1, 0]
+    shared_ref[chip, 2] = sum_ref[0, 1] + sum_ref[1, 1]
+    pair_copy.wait()
+    half_ref[...] = part_ref[rows_at(core * half, half), :] + other_ref[...]
 
     def part_copy(offset, peer):
         return put_copy(
-            part_ref.at[peer],
+            half_ref.at[rows_at(peer * share, share), :],
             got_ref.at[data_at],
             part_sems.at[0, offset],
             part_sems.at[1, offset],
@@ -202,53 +252,47 @@
         )
 
     over_peers("dp", lambda offset, peer: part_copy(offset, peer).start())
-    got_ref[data_at] = part_ref[data_at]
+    got_ref[data_at] = half_ref[rows_at(data_at * share, share), :]
     over_peers("dp", lambda offset, peer: part_copy(offset, peer).wait())
-    summed = got_ref[0]
-    for d in range(1, ndata):
-        summed = summed + got_ref[d]
-    for at in range(piece_ref.shape[0]):
-        r, l = divmod(at, across)
-        piece_ref[at] = summed[8 * r : 8 * r + 8, lanes * l : lanes * (l + 1)]
+    summed = jnp.sum(got_ref[...], axis=0)
+    for at in range(chips):
+        piece_ref[at, :few] = summed[few * at : few * (at + 1)]
 
     def piece_copy(offset, peer):
         return put_copy(
-            piece_ref.at[peer],
-            arrived_ref.at[col_at],
+            piece_ref.at[peer // 2],
+            arrived_ref.at[chip],
             piece_sems.at[0, offset],
             piece_sems.at[1, offset],
             "cols",
             peer,
         )
 
-    over_peers("cols", lambda offset, peer: piece_copy(offset, peer).start())
-    arrived_ref[col_at] = piece_ref[col_at]
-    weight = mine_ref[:, :, 1, :]
-    for at, term in ((1, weight), (2, (weight > 0.0).astype(jnp.float32))):
-        term = jnp.sum(term, axis=0).reshape(-1, *shared_ref.shape[2:])
-        shared_ref[col_at, at] = jnp.sum(term, axis=0)
-    over_peers("cols", lambda offset, peer: piece_copy(offset, peer).wait())
-    shared_ref[col_at, 0] = jnp.sum(arrived_ref[...], axis=0)
+    over_peers("cols", lambda offset, peer: piece_copy(offset, peer).start(), 2)
+    arrived_ref[chip] = piece_ref[chip]
+    over_peers("cols", lambda offset, peer: piece_copy(offset, peer).wait(), 2)
+    shared_ref[chip, 0] = jnp.sum(arrived_ref[...], axis=0)
 
     def shared_copy(offset, peer):
         return put_copy(
-            shared_ref.at[col_at],
-            shared_ref.at[col_at],
+            shared_ref.at[chip],
+            shared_ref.at[chip],
             shared_sems.at[0, offset],
             shared_sems.at[1, offset],
             "cols",
             peer,
         )
 
-    exchange("cols", shared_copy)
-    for r in range(chunk // 8):
-        row = [shared_ref[r * across + l, 0] for l in range(across)]
-        gram_ref[data_at, pl.ds(8 * r, 8), :] = jnp.concatenate(row, axis=1)
+    over_peers("cols", lambda offset, peer: shared_copy(offset, peer).start(), 2)
+    over_peers("cols", lambda offset, peer: shared_copy(offset, peer).wait(), 2)
+    for at in range(chips):
+        own_ref[few * at : few * (at + 1), :] = shared_ref[at, 0, :few, :]
+    own_rows = rows_at((core * ndata + data_at) * share, share)
 
     def gram_copy(offset, peer):
         return put_copy(
-            gram_ref.at[data_at],
-            gram_ref.at[data_at],
+            own_ref,
+            gram_ref.at[own_rows, :],
             gram_sems.at[0, offset],
             gram_sems.at[1, offset],
             "dp",
@@ -256,38 +300,54 @@
         )
 
     over_peers("dp", lambda offset, peer: gram_copy(offset, peer).start())
+    gram_ref[own_rows, :] = own_ref[...]
     totals_ref[0] = jnp.sum(shared_ref[:, 1], axis=0)
     totals_ref[1] = jnp.sum(shared_ref[:, 2], axis=0)
     over_peers("dp", lambda offset, peer: gram_copy(offset, peer).wait())
+    own_half = gram_ref.at[rows_at(core * half, half), :]
+    last_copy = put_copy(
+        own_half, own_half, pair_sems.at[0, 2], pair_sems.at[1, 2], "cols", pair
+    )
+    last_copy.start()
+    last_copy.wait()
 
 
 def sum_gram(sketch, mine):
     ndata, chunk, size = sketch.shape
-    ncols = lax.axis_size("cols")
+    chips = lax.axis_size("cols") // 2
     width = ndata * chunk
+    lanes = mine.shape[-1]
     f32 = jnp.float32
-    tile = (8, mine.shape[-1])
-    assert ncols * tile[0] * tile[1] == chunk * width
+    packed = len(lower_blocks(width, lanes)) * lanes
+    half = packed // 2
+    share = half // ndata
+    tile = (8, lanes)
+    assert share % 8 == 0 and share % chips == 0 and share // chips <= 8
     dma = pltpu.SemaphoreType.DMA
     return pl.pallas_call(
         gram_kernel,
         out_shape=(
             jax.ShapeDtypeStruct((ndata, chunk, size), f32),
-            jax.ShapeDtypeStruct((ndata, chunk, width), f32),
+            jax.ShapeDtypeStruct((packed, lanes), f32),
             jax.ShapeDtypeStruct((2, *tile), f32),
         ),
         in_specs=[vmem(), vmem()],
         out_specs=(vmem(), vmem(), vmem()),
         scratch_shapes=[
-            pltpu.VMEM((ndata, chunk, width), f32),
-            pltpu.VMEM((ndata, chunk, width), f32),
-            pltpu.VMEM((ncols, *tile), f32),
-            pltpu.VMEM((ncols, *tile), f32),
-            pltpu.VMEM((ncols, 3, *tile), f32),
+            pltpu.VMEM((packed, lanes), f32),
+            pltpu.VMEM((half, lanes), f32),
+            pltpu.VMEM((half, lanes), f32),
+            pltpu.VMEM((ndata, share, lanes), f32),
+            pltpu.VMEM((chips, *tile), f32),
+            pltpu.VMEM((chips, *tile), f32),
+            pltpu.VMEM((chips, 3, *tile), f32),
+            pltpu.VMEM((share, lanes), f32),
+            pltpu.VMEM((2, 2, *tile), f32),
             dma((2, ndata)),
+            dma((2, 3)),
             dma((2, ndata)),
-            dma((2, ncols)),
-            dma((2, ncols)),
+            dma((2, chips)),
+            dma((2, chips)),
             dma((2, ndata)),
         ],
         compiler_params=pltpu.CompilerParams(
@@ -344,35 +404,40 @@
     return jnp.concatenate(done, axis=0)
 
 
-def factor_kernel(corner_size, gram_ref, rows_ref, basis_ref, half_ref, work_ref, inverse_ref):
-    n = gram_ref.shape[0]
-    work_ref[...] = gram_ref[...]
-    row_at = lax.broadcasted_iota(jnp.int32, (n, n), 0)
-    col_at = lax.broadcasted_iota(jnp.int32, (n, n), 1)
-    inverse_ref[...] = jnp.where(row_at == col_at, 1.0, 0.0)
-
-    def step(k, carry):
-        at = pl.ds(pl.multiple_of(k * corner_size, corner_size), corner_size)
-        corner = corner_inverse(work_ref[at, at])
-        row = dot_exact(corner, inverse_ref[at, :], ((1,), (0,)))
-        low = dot_exact(work_ref[:, at], corner, ((1,), (1,)))
-        below = lax.broadcasted_iota(jnp.int32, low.shape, 0) >= (k + 1) * corner_size
-        low = jnp.where(below, low, 0.0)
-        work_ref[...] -= dot_exact(low, low, ((1,), (1,)))
-        inverse_ref[...] -= dot_exact(low, row, ((1,), (0,)))
-        inverse_ref[at, :] = row
-        return carry
-
-    lax.fori_loop(0, n // corner_size, step, 0)
-    q = dot_exact(inverse_ref[...], rows_ref[...], ((1,), (0,)))
-    half_ref[...] = q.astype(jnp.bfloat16)
-    basis_ref[...] = q.T.astype(jnp.bfloat16)
+def factor_kernel(gram_ref, rows_ref, basis_ref, half_ref, work_ref, inverse_ref):
+    n = work_ref.shape[0]
+    size = gram_ref.shape[1]
+    for at, (i, j) in enumerate(lower_blocks(n, size)):
+        work_ref[size * i : size * (i + 1), size * j : size * (j + 1)] = gram_ref[
+            size * at : size * (at + 1), :
+        ]
+    for start in range(0, n, size):
+        end = start + size
+        corner = corner_inverse(work_ref[start:end, start:end])
+        if start:
+            inverse_ref[start:end, :start] = dot_exact(
+                corner, inverse_ref[start:end, :start], ((1,), (0,))
+            )
+        inverse_ref[start:end, start:end] = corner
+        if end < n:
+            low = dot_exact(work_ref[end:, start:end], corner, ((1,), (1,)))
+            work_ref[end:, end:] -= dot_exact(low, low, ((1,), (1,)))
+            if start:
+                inverse_ref[end:, :start] -= dot_exact(
+                    low, inverse_ref[start:end, :start], ((1,), (0,))
+                )
+            inverse_ref[end:, start:end] = -dot_exact(low, corner, ((1,), (0,)))
+    for start in range(0, n, size):
+        end = start + size
+        q = dot_exact(inverse_ref[start:end, :end], rows_ref[:end, :], ((1,), (0,)))
+        half_ref[start:end, :] = q.astype(jnp.bfloat16)
+        basis_ref[:, start:end] = q.T.astype(jnp.bfloat16)
 
 
 def factor_and_q(gram, rows):
     width, size = rows.shape
     return pl.pallas_call(
-        functools.partial(factor_kernel, 128),
+        factor_kernel,
         out_shape=(
             jax.ShapeDtypeStruct((size, width), jnp.bfloat16),
             jax.ShapeDtypeStruct((width, size), jnp.bfloat16),
@@ -407,20 +472,8 @@
         y = lax.rem(self.y + lax.rem(turn, 2), 2)
         return self.device(z, y, lax.rem(core + turn // 2, 2))
 
-    def greet(self, others=()):
-        barrier = pltpu.get_barrier_semaphore()
-        for peer in (self.pair, self.across, self.after, self.before):
-            pl.semaphore_signal(
-                barrier, inc=1, device_id={"cols": peer}, device_id_type=pl.DeviceIdType.MESH
-            )
-        for axis in others:
-            over_peers(
-                axis,
-                lambda offset, peer, axis=axis: pl.semaphore_signal(
-                    barrier, inc=1, device_id={axis: peer}, device_id_type=pl.DeviceIdType.MESH
-                ),
-            )
-        pl.semaphore_wait(barrier, 4 + sum(lax.axis_size(axis) - 1 for axis in others))
+    def greet(self, *groups):
+        greet(*groups, near=(self.pair, self.across, self.after, self.before))
 
     def copy(self, slot, send, peer):
         part = self.all_ref.at[slot]
@@ -555,7 +608,7 @@
     *sems,
 ):
     ring = Ring(all_ref, *sems)
-    ring.greet(["dp"])
+    ring.greet(("dp", 1))
     data_at, col_at = lax.axis_index("dp"), lax.axis_index("cols")
     size = basis_ref.shape[0]
     own_rows = pl.ds(pl.multiple_of(data_at * width, width), width)
@@ -645,7 +698,7 @@
     part = part.reshape(ndata, size, chunk).swapaxes(1, 2).reshape(ndata * chunk, size)
     sketch = sketch_sums(part, here, block, chunk)
     rows, gram, totals = sum_gram(sketch.reshape(ndata, chunk, size), mine)
-    basis_part, q_half = factor_and_q(gram.reshape(width, width), rows.reshape(width, size))
+    basis_part, q_half = factor_and_q(gram, rows.reshape(width, size))
     scale = math.sqrt(block * ncols)
     coefficients, q_block = project(q_half, basis_part, mine, totals, scale, block, chunk)
     basis = scale * q_block.astype(jnp.float32)

time: 239 us -> 210 us (0.88)
  Pallas kernels: 230 us -> 201 us
    pallas_call x1, Pallas kernels: 66 us -> 43.9 us  [sum_gram(): pl.pallas_call(gram_kernel, out_shape=(jax.ShapeDtypeStruct((ndata, chunk...]
    pallas_call x1, Pallas kernels: 32 us -> 24.1 us  [factor_and_q(): pl.pallas_call(factor_kernel, out_shape=(jax.ShapeDtypeStruct((size, widt...]
where the time goes in v4:
time: 210 us
  Pallas kernels  201 us (96%)
  other arithmetic  4.96 us (2%)
  local copies, waits for them, and re-layouts  3.1 us (1%)
    pallas_call x1, Pallas kernels, project(): pl.pallas_call(functools.partial(project_kernel, scale, block, width), ou...  57.8 us
    pallas_call x1, Pallas kernels, sketch_sums(): pl.pallas_call(functools.partial(sketch_kernel, block, width), out_shape=...  52.6 us
    pallas_call x1, Pallas kernels, sum_gram(): pl.pallas_call(gram_kernel, out_shape=(jax.ShapeDtypeStruct((ndata, chunk...  43.9 us
    pallas_call x1, Pallas kernels, factor_and_q(): pl.pallas_call(factor_kernel, out_shape=(jax.ShapeDtypeStruct((size, widt...  24.1 us
    pallas_call x1, Pallas kernels, exchange_records(): pl.pallas_call(records_kernel, out_shape=(gathered, gathered), in_specs=[...  22.9 us

profile of v4, /device:TPU:1, one launch (start us, length us, event | category | flops | bytes accessed | tf_op | source)
XLA Modules:
  0.0 210.1 jit_solution(5605730488047661485)
XLA Ops:
  0.6 0.0 copy-start
  0.7 0.9 add_convert_fusion
  1.5 0.8 compare_select_fusion
  2.4 0.6 pad_maximum_fusion.own_ref
  3.0 22.9 %records.1 = (f32[8,32,2,128]{3,2,1,0:T(2,128)}, f32[8,32,2,128]{3,2,1,0:T(2,128)}) custom-call(f32[32,2,128]{2,1,0:T(2,128)} %pad_maximum_fusion.own_ref), custom_call_target="tpu_custom_call" | custom-call | tf_op jit(solution)/shard_map/records/pallas_call | solution.py:143
  25.9 0.0 copy-start.2
  25.9 0.0 copy-done
  25.9 0.2 constant_dynamic-slice_fusion
  26.2 0.2 copy.8
  26.4 0.0 copy-start.3
  26.4 0.9 copy-done.3
  27.3 52.6 %sketch.1 = f32[512,256]{1,0:T(8,128)S(1)} custom-call(bf16[512,256]{1,0:T(8,128)(2,1)S(1)} %bitcast.11, f32[8,32,2,128]{3,2,1,0:T(2,128)S(1)} %copy-done.3), custom_call_target="tpu_custom_call" | custom-call | tf_op jit(solution)/shard_map/sketch/pallas_call | solution.py:580
  80.0 0.0 copy-start.1
  80.0 0.9 copy-done.1
  80.9 43.9 %gram.1 = (f32[8,64,256]{2,1,0:T(8,128)S(1)}, f32[1280,128]{1,0:T(8,128)S(1)}, f32[2,8,128]{2,1,0:T(8,128)S(1)}) custom-call(f32[8,64,256]{2,1,0:T(8,128)S(1)} %bitcast.10, f32[8,32,2,128]{3,2,1,0:T(2,128)S(1)} %copy-done.1), custom_call_target="tpu_custom_call" | custom-call | tf_op jit(solution)/shard_map/gram/pallas_call | solution.py:327
  124.8 24.1 %factor.1 = (bf16[256,512]{1,0:T(8,128)(2,1)S(1)}, bf16[512,256]{1,0:T(8,128)(2,1)S(1)}) custom-call(f32[1280,128]{1,0:T(8,128)S(1)} %get-tuple-element.13.gram_ref, f32[512,256]{1,0:T(8,128)S(1)} %bitcast.12), custom_call_target="tpu_custom_call" | custom-call | tf_op jit(solution)/shard_map/factor/pallas_call | solution.py:439
  148.9 0.0 copy-done.2
  148.9 57.8 %project.1 = (f32[64,2048]{1,0:T(8,128)S(1)}, bf16[2048,512]{1,0:T(8,128)(2,1)S(1)}) custom-call(bf16[512,256]{1,0:T(8,128)(2,1)S(1)} %get-tuple-element.15.half_ref, bf16[256,512]{1,0:T(8,128)(2,1)S(1)} %get-tuple-element.16.basis_ref, f32[8,32,2,128]{3,2,1,0:T(2,128)S(1)} %copy-done.2, f32[2,8,128]{2,1,0:T(8,128)S(1)} %get-tuple-element.17.totals_ref), custom_call_target="tpu_custom_call" | custom-call | tf_op jit(solution)/shard_map/project/pallas_call | solution.py:659
  206.7 2.6 %convert_multiply_fusion = f32[2048,512]{1,0:T(8,128)} fusion(bf16[2048,512]{1,0:T(8,128)(2,1)S(1)} %get-tuple-element.18), kind=kLoop, calls=%fused_computation | loop fusion | flops 2097152 | bytes 6291456 | tf_op jit(solution)/shard_map/mul | solution.py:704
  209.3 0.8 copy.12
Async XLA Ops:
  0.6 25.3 %copy-start = (bf16[2048,512]{1,0:T(8,128)(2,1)S(1)}, bf16[2048,512]{1,0:T(8,128)(2,1)}, u32[]{:S(2)}) copy-start(bf16[2048,512]{1,0:T(8,128)(2,1)} %param.9) | copy-start | bytes 6291460
  25.9 122.9 %copy-start.2 = (f32[8,32,2,128]{3,2,1,0:T(2,128)S(1)}, f32[8,32,2,128]{3,2,1,0:T(2,128)}, u32[]{:S(2)}) copy-start(f32[8,32,2,128]{3,2,1,0:T(2,128)} %get-tuple-element.12.mine_ref) | copy-start | bytes 786436
  26.4 1.0 copy-start.3
  80.0 1.0 copy-start.1

commit v5 on v4

--- a/solution.py
+++ b/solution.py
@@ -22,7 +22,7 @@
     return jnp.where(rows == ids, 1.0, 0.0).astype(jnp.bfloat16)
 
 
-def move_block(table, take, put, weight, width):
+def weighted_rows(table, take, put, weight, width):
     size = table.shape[1]
     groups = table.shape[0] // width
     shift = size.bit_length() - 1
@@ -41,10 +41,7 @@
     placed = jnp.concatenate(
         [jnp.where(put_group == g, row, 0.0).astype(jnp.bfloat16) for g in range(groups)], axis=0
     )
-    spots = beside([one_hot(ids & (size - 1), size) for ids in put])
-    return lax.dot_general(
-        placed, spots, (((1,), (1,)), ((), ())), preferred_element_type=jnp.float32
-    )
+    return placed, beside([one_hot(ids & (size - 1), size) for ids in put])
 
 
 def vmem():
@@ -451,26 +448,40 @@
 
 
 class Ring:
-    def __init__(self, all_ref, got_sems, ring_sems, pair_sems, across_sem):
+    ARRIVALS = 15
+    RING = (0, 1, 3, 4, 5, 7, 8)
+    CROSS = (1, 5, 9, 12)
+
+    def __init__(self, all_ref, got_sems, ring_sems, pair_sems, cross_sems):
         self.all_ref, self.got_sems = all_ref, got_sems
-        self.ring_sems, self.pair_sems, self.across_sem = ring_sems, pair_sems, across_sem
+        self.ring_sems, self.pair_sems, self.cross_sems = ring_sems, pair_sems, cross_sems
         at = lax.axis_index("cols")
         self.length = lax.axis_size("cols") // 4
+        assert self.length == 8
         self.z, quad = at // 4, lax.rem(at, 4)
         self.y, self.core = quad // 2, lax.rem(quad, 2)
         self.way = 1 - 2 * self.core
-        self.pair = self.device(self.z, self.y, 1 - self.core)
-        self.across = self.device(self.z, 1 - self.y, self.core)
-        self.after = self.device(self.z + self.way, self.y, self.core)
-        self.before = self.device(self.z - self.way, self.y, self.core)
-
-    def device(self, z, y, core):
-        z = lax.rem(z + self.length, self.length)
+        self.own = at
+        self.pair = self.device(0, 0, 1)
+        self.across = self.device(0, 1, 0)
+        self.after = self.device(-1, 0, 0)
+        self.before = self.device(1, 0, 0)
+        self.diagonal = self.device(0, 1, 1)
+
+    def device(self, away, row, core, mirror=False):
+        way = -self.way if mirror else self.way
+        z = lax.rem(self.z - way * away + self.length, self.length)
+        y = lax.rem(self.y + row, 2)
+        core = lax.rem(self.core + core + (1 if mirror else 0), 2)
         return z * 4 + y * 2 + core
 
-    def quad_slot(self, z, turn, core):
-        y = lax.rem(self.y + lax.rem(turn, 2), 2)
-        return self.device(z, y, lax.rem(core + turn // 2, 2))
+    def place(self, n):
+        return n + n // 13
+
+    def slot(self, m, mirror=False):
+        turn = lax.rem(m, 4)
+        away = m // 4 + 1 - (turn // 2 - turn // 3)
+        return self.device(away, turn // 2, lax.rem((turn + 1) // 2, 2), mirror)
 
     def greet(self, *groups):
         greet(*groups, near=(self.pair, self.across, self.after, self.before))
@@ -480,100 +491,139 @@
         return put_copy(part, part, send, self.got_sems.at[slot], "cols", peer)
 
     def arrived(self, slot):
-        self.copy(slot, self.across_sem.at[0], self.pair).wait_recv()
-
-    def run(self, work, begun=None):
-        steps = 4 * (self.length // 2) - 2
-
-        def near(turn, carry):
-            slot = self.quad_slot(self.z, turn, self.core)
-
-            @pl.when(turn > 0)
+        self.copy(slot, self.cross_sems.at[0], self.pair).wait_recv()
+
+    def to_ring(self, slot, at):
+        self.copy(slot, self.ring_sems.at[at], self.after).start()
+
+    def to_pair(self, slot, at):
+        self.copy(slot, self.pair_sems.at[at], self.pair).start()
+
+    def to_across(self, slot, at):
+        self.copy(slot, self.cross_sems.at[at], self.across).start()
+
+    def hand_on(self, n):
+        m = self.place(n)
+        slot = self.slot(m)
+        self.arrived(slot)
+        turn, step = lax.rem(m, 4), m // 4 + 1
+
+        @pl.when((turn == 0) & (step < 4))
+        def _():
+            self.to_ring(slot, m + 3)
+
+        @pl.when((turn == 1) & (step < 3))
+        def _():
+            self.to_ring(slot, m + 3)
+
+        @pl.when(m == 3)
+        def _():
+            self.to_ring(slot, m + 3)
+
+        @pl.when(m == 8)
+        def _():
+            self.to_ring(self.slot(7), 7 + 3)
+
+        @pl.when((turn == 1) | (m == 12))
+        def _():
+            self.to_across(slot, m)
+
+        @pl.when(m != 2)
+        def _():
+            self.to_pair(slot, n + 1)
+
+    def begin(self):
+        self.to_pair(self.own, 0)
+        self.to_ring(self.own, 0)
+        self.to_across(self.own, 0)
+        self.arrived(self.pair)
+        self.to_ring(self.pair, 1)
+        self.arrived(self.across)
+        self.to_ring(self.across, 2)
+        self.to_pair(self.across, 3)
+        self.hand_on(0)
+
+    def run(self, work, also):
+        work([self.own, self.pair])
+        last = self.ARRIVALS - 1
+
+        def one(n, carry):
+            for at, act in also.items():
+                pl.when(n == at)(act)
+
+            @pl.when(n < last)
             def _():
-                self.arrived(slot)
-
-            self.copy(slot, self.ring_sems.at[turn], self.after).start()
-
-            @pl.when(turn < 2)
+                ahead = n + 1
+                swap = ahead // 11 - 2 * (ahead // 12) + ahead // 13
+                self.hand_on(ahead + swap)
+
+            m = self.place(n)
+            mirrored = self.slot(m, mirror=True)
+
+            @pl.when(m != 2)
             def _():
-                self.copy(slot, self.pair_sems.at[turn], self.pair).start()
-
-            @pl.when(turn == 0)
-            def _():
-                self.copy(slot, self.across_sem.at[0], self.across).start()
-
-            work(slot)
+                self.arrived(mirrored)
+
+            work([self.slot(m), mirrored])
             return carry
 
-        lax.fori_loop(0, 4, near, 0)
-        if begun is not None:
-            begun()
-
-        def far(step, carry):
-            turn, away = lax.rem(step, 4), step // 4 + 1
-            slot = self.quad_slot(self.z - self.way * away, turn, self.core)
-            self.arrived(slot)
-
-            @pl.when(step < steps - 4)
-            def _():
-                self.copy(slot, self.ring_sems.at[step + 4], self.after).start()
-
-            self.copy(slot, self.pair_sems.at[step + 2], self.pair).start()
-            work(slot)
-            slot = self.quad_slot(self.z + self.way * away, turn, 1 - self.core)
-            self.arrived(slot)
-            work(slot)
+        lax.fori_loop(0, self.ARRIVALS, one, 0)
+        for at in [0, 1, 2, *(m + 3 for m in self.RING)]:
+            self.copy(self.own, self.ring_sems.at[at], self.after).wait_send()
+        for at in [0, *self.CROSS]:
+            self.copy(self.own, self.cross_sems.at[at], self.across).wait_send()
+
+        def sent(at, carry):
+            self.copy(self.own, self.pair_sems.at[at], self.pair).wait_send()
             return carry
 
-        lax.fori_loop(0, steps, far, 0)
-        own = self.device(self.z, self.y, self.core)
-
-        def sent(sems):
-            def one(at, carry):
-                self.copy(own, sems.at[at], self.pair).wait_send()
-                return carry
-
-            lax.fori_loop(0, sems.shape[0], one, 0)
-
-        sent(self.ring_sems)
-        sent(self.pair_sems)
-        sent(self.across_sem)
+        lax.fori_loop(0, self.ARRIVALS + 1, sent, 0)
 
 
 def ring_scratch(table):
+    dma = pltpu.SemaphoreType.DMA
     ncols = lax.axis_size("cols")
-    moved = 4 * (ncols // 8) - 2
-    dma = pltpu.SemaphoreType.DMA
     return [
         pltpu.VMEM((ncols, *table), jnp.bfloat16),
         dma((ncols,)),
-        dma((moved,)),
-        dma((moved + 2,)),
-        dma((1,)),
+        dma((Ring.RING[-1] + 4,)),
+        dma((Ring.ARRIVALS + 1,)),
+        dma((Ring.CROSS[-1] + 1,)),
     ]
 
 
-def block_sums(table, records_ref, slot, block, width, by_prefix):
+def block_sums(all_ref, records_ref, slots, block, width, by_prefix):
     shift = block.bit_length() - 1
     rows = range(records_ref.shape[0])
-    packed = [records_ref[d, slot, 0:1, :].astype(jnp.int32) for d in rows]
-    weight = [records_ref[d, slot, 1:2, :] for d in rows]
-    prefix = [lax.shift_right_logical(ids, shift) for ids in packed]
-    suffix = [ids & (block - 1) for ids in packed]
-    take, put = (prefix, suffix) if by_prefix else (suffix, prefix)
-    return move_block(table, take, put, weight, width)
+    placed, spots = [], []
+    for slot in slots:
+        packed = [records_ref[d, slot, 0:1, :].astype(jnp.int32) for d in rows]
+        weight = [records_ref[d, slot, 1:2, :] for d in rows]
+        prefix = [lax.shift_right_logical(ids, shift) for ids in packed]
+        suffix = [ids & (block - 1) for ids in packed]
+        take, put = (prefix, suffix) if by_prefix else (suffix, prefix)
+        one, spot = weighted_rows(all_ref[slot], take, put, weight, width)
+        placed.append(one)
+        spots.append(spot)
+    return lax.dot_general(
+        jnp.concatenate(placed, axis=1),
+        jnp.concatenate(spots, axis=1),
+        (((1,), (1,)), ((), ())),
+        preferred_element_type=jnp.float32,
+    )
 
 
 def sketch_kernel(block, width, part_ref, here_ref, total_ref, all_ref, *sems):
     ring = Ring(all_ref, *sems)
     ring.greet()
-    all_ref[lax.axis_index("cols")] = part_ref[...]
+    all_ref[ring.own] = part_ref[...]
+    ring.begin()
     total_ref[...] = jnp.zeros_like(total_ref)
 
-    def work(slot):
-        total_ref[...] += block_sums(all_ref[slot], here_ref, slot, block, width, False)
-
-    ring.run(work)
+    def work(slots):
+        total_ref[...] += block_sums(all_ref, here_ref, slots, block, width, False)
+
+    ring.run(work, {})
 
 
 def sketch_sums(part, here, block, width):
@@ -611,6 +661,7 @@
     ring.greet(("dp", 1))
     data_at, col_at = lax.axis_index("dp"), lax.axis_index("cols")
     size = basis_ref.shape[0]
+    ndata = whole_ref.shape[0] // size
     own_rows = pl.ds(pl.multiple_of(data_at * width, width), width)
 
     def half_copy(offset, peer):
@@ -623,31 +674,58 @@
             peer,
         )
 
-    own_basis = whole_ref.at[pl.ds(pl.multiple_of(data_at * size, size), size), :]
-
-    def basis_copy(offset, peer):
-        return put_copy(
-            basis_ref, own_basis, basis_sems.at[0, offset], basis_sems.at[1, offset], "dp", peer
-        )
-
-    own_copy = pltpu.make_async_copy(basis_ref, own_basis, own_sem)
+    along = ndata // 2
+    other = lax.rem(data_at + along, ndata)
+
+    def basis_rows(owner):
+        return whole_ref.at[pl.ds(pl.multiple_of(owner * size, size), size), :]
+
+    def basis_copy(offset, rows, source, peer):
+        return put_copy(
+            source, rows, basis_sems.at[0, offset], basis_sems.at[1, offset], "dp", peer
+        )
+
+    def x_copy(offset, owner, source):
+        peer = data_at // along * along + lax.rem(data_at + offset, along)
+        at = offset if source is basis_ref else along + offset
+        return basis_copy(at, basis_rows(owner), source, peer)
+
+    def own_x_copy(offset):
+        return x_copy(offset, data_at, basis_ref)
+
+    def other_x_copy(offset):
+        return x_copy(offset, other, basis_rows(other))
+
+    own_copy = pltpu.make_async_copy(basis_ref, basis_rows(data_at), own_sem)
+    other_copy = basis_copy(0, basis_rows(data_at), basis_ref, other)
 
     def begun():
-        over_peers("dp", lambda offset, peer: basis_copy(offset, peer).start())
+        other_copy.start()
+        for offset in range(1, along):
+            own_x_copy(offset).start()
         own_copy.start()
 
-    def work(slot):
-        total_ref[...] += block_sums(all_ref[slot], mine_ref, slot, block, width, True)
+    def later():
+        other_copy.wait_recv()
+        for offset in range(1, along):
+            other_x_copy(offset).start()
+
+    def work(slots):
+        total_ref[...] += block_sums(all_ref, mine_ref, slots, block, width, True)
 
     over_peers("dp", lambda offset, peer: half_copy(offset, peer).start())
     all_ref[col_at, own_rows, :] = half_ref[own_rows, :]
     total_ref[...] = jnp.zeros_like(total_ref)
     over_peers("dp", lambda offset, peer: half_copy(offset, peer).wait())
-    ring.run(work, begun)
+    ring.begin()
+    ring.run(work, {0: begun, 6: later})
     factor = scale * jnp.sum(totals_ref[1]) / jnp.sum(totals_ref[0])
     for g in range(total_ref.shape[0] // width):
         coef_ref[:, g * size : (g + 1) * size] = factor * total_ref[g * width : (g + 1) * width, :]
-    over_peers("dp", lambda offset, peer: basis_copy(offset, peer).wait())
+    other_copy.wait_send()
+    for offset in range(1, along):
+        own_x_copy(offset).wait()
+        other_x_copy(offset).wait()
     own_copy.wait()
 
 

time: 210 us -> 197 us (0.938)
  Pallas kernels: 201 us -> 188 us
    pallas_call x1, Pallas kernels: 52.6 us -> 44.8 us  [sketch_sums(): pl.pallas_call(functools.partial(sketch_kernel, block, width), out_shape=...]
    pallas_call x1, Pallas kernels: 57.8 us -> 53.3 us  [project(): pl.pallas_call(functools.partial(project_kernel, scale, block, width), ou...]
where the time goes in v5:
time: 197 us
  Pallas kernels  188 us (95%)
  other arithmetic  4.96 us (3%)
  local copies, waits for them, and re-layouts  3.1 us (2%)
    pallas_call x1, Pallas kernels, project(): pl.pallas_call(functools.partial(project_kernel, scale, block, width), ou...  53.3 us
    pallas_call x1, Pallas kernels, sketch_sums(): pl.pallas_call(functools.partial(sketch_kernel, block, width), out_shape=...  44.8 us
    pallas_call x1, Pallas kernels, sum_gram(): pl.pallas_call(gram_kernel, out_shape=(jax.ShapeDtypeStruct((ndata, chunk...  42.5 us
    pallas_call x1, Pallas kernels, factor_and_q(): pl.pallas_call(factor_kernel, out_shape=(jax.ShapeDtypeStruct((size, widt...  24.1 us
    pallas_call x1, Pallas kernels, exchange_records(): pl.pallas_call(records_kernel, out_shape=(gathered, gathered), in_specs=[...  22.9 us

profile of v5, /device:TPU:1, one launch (start us, length us, event | category | flops | bytes accessed | tf_op | source)
XLA Modules:
  0.0 196.5 jit_solution(4257050503907215791)
XLA Ops:
  0.6 0.0 copy-start
  0.7 0.9 add_convert_fusion
  1.5 0.8 compare_select_fusion
  2.4 0.6 pad_maximum_fusion.own_ref
  3.0 22.9 %records.1 = (f32[8,32,2,128]{3,2,1,0:T(2,128)}, f32[8,32,2,128]{3,2,1,0:T(2,128)}) custom-call(f32[32,2,128]{2,1,0:T(2,128)} %pad_maximum_fusion.own_ref), custom_call_target="tpu_custom_call" | custom-call | tf_op jit(solution)/shard_map/records/pallas_call | solution.py:140
  25.9 0.0 copy-start.2
  25.9 0.0 copy-done
  25.9 0.2 constant_dynamic-slice_fusion
  26.2 0.2 copy.8
  26.4 0.0 copy-start.3
  26.4 0.9 copy-done.3
  27.3 44.8 %sketch.1 = f32[512,256]{1,0:T(8,128)S(1)} custom-call(bf16[512,256]{1,0:T(8,128)(2,1)S(1)} %bitcast.11, f32[8,32,2,128]{3,2,1,0:T(2,128)S(1)} %copy-done.3), custom_call_target="tpu_custom_call" | custom-call | tf_op jit(solution)/shard_map/sketch/pallas_call | solution.py:630
  72.1 0.0 copy-start.1
  72.2 0.9 copy-done.1
  73.1 42.5 %gram.1 = (f32[8,64,256]{2,1,0:T(8,128)S(1)}, f32[1280,128]{1,0:T(8,128)S(1)}, f32[2,8,128]{2,1,0:T(8,128)S(1)}) custom-call(f32[8,64,256]{2,1,0:T(8,128)S(1)} %bitcast.10, f32[8,32,2,128]{3,2,1,0:T(2,128)S(1)} %copy-done.1), custom_call_target="tpu_custom_call" | custom-call | tf_op jit(solution)/shard_map/gram/pallas_call | solution.py:324
  115.7 24.1 %factor.1 = (bf16[256,512]{1,0:T(8,128)(2,1)S(1)}, bf16[512,256]{1,0:T(8,128)(2,1)S(1)}) custom-call(f32[1280,128]{1,0:T(8,128)S(1)} %get-tuple-element.13.gram_ref, f32[512,256]{1,0:T(8,128)S(1)} %bitcast.12), custom_call_target="tpu_custom_call" | custom-call | tf_op jit(solution)/shard_map/factor/pallas_call | solution.py:436
  139.8 0.0 copy-done.2
  139.8 53.3 %project.1 = (f32[64,2048]{1,0:T(8,128)S(1)}, bf16[2048,512]{1,0:T(8,128)(2,1)S(1)}) custom-call(bf16[512,256]{1,0:T(8,128)(2,1)S(1)} %get-tuple-element.15.half_ref, bf16[256,512]{1,0:T(8,128)(2,1)S(1)} %get-tuple-element.16.basis_ref, f32[8,32,2,128]{3,2,1,0:T(2,128)S(1)} %copy-done.2, f32[2,8,128]{2,1,0:T(8,128)S(1)} %get-tuple-element.17.totals_ref), custom_call_target="tpu_custom_call" | custom-call | tf_op jit(solution)/shard_map/project/pallas_call | solution.py:737
  193.1 2.6 %convert_multiply_fusion = f32[2048,512]{1,0:T(8,128)} fusion(bf16[2048,512]{1,0:T(8,128)(2,1)S(1)} %get-tuple-element.18), kind=kLoop, calls=%fused_computation | loop fusion | flops 2097152 | bytes 6291456 | tf_op jit(solution)/shard_map/mul | solution.py:782
  195.7 0.8 copy.12
Async XLA Ops:
  0.6 25.3 %copy-start = (bf16[2048,512]{1,0:T(8,128)(2,1)S(1)}, bf16[2048,512]{1,0:T(8,128)(2,1)}, u32[]{:S(2)}) copy-start(bf16[2048,512]{1,0:T(8,128)(2,1)} %param.9) | copy-start | bytes 6291460
  25.9 113.8 %copy-start.2 = (f32[8,32,2,128]{3,2,1,0:T(2,128)S(1)}, f32[8,32,2,128]{3,2,1,0:T(2,128)}, u32[]{:S(2)}) copy-start(f32[8,32,2,128]{3,2,1,0:T(2,128)} %get-tuple-element.12.mine_ref) | copy-start | bytes 786436
  26.4 1.0 copy-start.3
  72.1 1.0 copy-start.1

commit v6 on v5

--- a/solution.py
+++ b/solution.py
@@ -86,78 +86,16 @@
     pl.semaphore_wait(barrier, count + len(near))
 
 
-def exchange(axis, make):
-    over_peers(axis, lambda offset, peer: make(offset, peer).start())
-    over_peers(axis, lambda offset, peer: make(offset, peer).wait())
-
-
-def records_kernel(own_ref, here_ref, mine_ref, col_sems, here_sems, mine_sems):
-    data_at, col_at = lax.axis_index("dp"), lax.axis_index("cols")
-    greet(("cols", 1), ("dp", 1))
-
-    def to_col(offset, peer):
-        return put_copy(
-            own_ref.at[peer],
-            here_ref.at[data_at, col_at],
-            col_sems.at[0, offset],
-            col_sems.at[1, offset],
-            "cols",
-            peer,
-        )
-
-    def own_to_data(offset, peer):
-        return put_copy(
-            own_ref,
-            mine_ref.at[data_at],
-            mine_sems.at[0, offset],
-            mine_sems.at[1, offset],
-            "dp",
-            peer,
-        )
-
-    def here_to_data(offset, peer):
-        return put_copy(
-            here_ref.at[data_at],
-            here_ref.at[data_at],
-            here_sems.at[0, offset],
-            here_sems.at[1, offset],
-            "dp",
-            peer,
-        )
-
-    over_peers("cols", lambda offset, peer: to_col(offset, peer).start())
-    over_peers("dp", lambda offset, peer: own_to_data(offset, peer).start())
-    here_ref[data_at, col_at] = own_ref[col_at]
-    mine_ref[data_at] = own_ref[...]
-    over_peers("cols", lambda offset, peer: to_col(offset, peer).wait())
-    exchange("dp", here_to_data)
-    over_peers("dp", lambda offset, peer: own_to_data(offset, peer).wait())
-
-
-def exchange_records(own):
-    ndata, ncols = lax.axis_size("dp"), lax.axis_size("cols")
-    gathered = jax.ShapeDtypeStruct((ndata, *own.shape), own.dtype)
-    return pl.pallas_call(
-        records_kernel,
-        out_shape=(gathered, gathered),
-        in_specs=[vmem()],
-        out_specs=(vmem(), vmem()),
-        scratch_shapes=[
-            pltpu.SemaphoreType.DMA((2, ncols)),
-            pltpu.SemaphoreType.DMA((2, ndata)),
-            pltpu.SemaphoreType.DMA((2, ndata)),
-        ],
-        compiler_params=pltpu.CompilerParams(collective_id=0, has_side_effects=True),
-        name="records",
-    )(own)
-
-
 def lower_blocks(width, lanes):
     return [(i, j) for i in range(width // lanes) for j in range(i + 1)]
 
 
-def gram_kernel(
-    sketch_ref,
+def rows_at(start, count):
+    return pl.ds(pl.multiple_of(start, 8), count)
+
+
+def gram_steps(
+    total_ref,
     mine_ref,
     rows_ref,
     gram_ref,
@@ -181,7 +119,7 @@
     data_at, col_at = lax.axis_index("dp"), lax.axis_index("cols")
     core, chip = lax.rem(col_at, 2), col_at // 2
     pair = col_at + 1 - 2 * core
-    ndata, chunk, size = sketch_ref.shape
+    ndata, chunk, size = rows_ref.shape
     width = ndata * chunk
     lanes = part_ref.shape[1]
     half = half_ref.shape[0]
@@ -189,14 +127,9 @@
     chips = piece_ref.shape[0]
     few = share // chips
 
-    def rows_at(start, count):
-        return pl.ds(pl.multiple_of(start, 8), count)
-
-    greet(("dp", 1), ("cols", 2), near=(pair,))
-
     def rows_copy(offset, peer):
         return put_copy(
-            sketch_ref.at[peer],
+            total_ref.at[rows_at(peer * chunk, chunk), :],
             rows_ref.at[data_at],
             rows_sems.at[0, offset],
             rows_sems.at[1, offset],
@@ -205,7 +138,7 @@
         )
 
     over_peers("dp", lambda offset, peer: rows_copy(offset, peer).start())
-    rows_ref[data_at] = sketch_ref[data_at]
+    rows_ref[data_at] = total_ref[rows_at(data_at * chunk, chunk), :]
     weight = mine_ref[:, :, 1, :]
     for at, term in ((0, weight), (1, (weight > 0.0).astype(jnp.float32))):
         term = jnp.sum(term, axis=0).reshape(-1, *totals_ref.shape[1:])
@@ -307,51 +240,6 @@
     )
     last_copy.start()
     last_copy.wait()
-
-
-def sum_gram(sketch, mine):
-    ndata, chunk, size = sketch.shape
-    chips = lax.axis_size("cols") // 2
-    width = ndata * chunk
-    lanes = mine.shape[-1]
-    f32 = jnp.float32
-    packed = len(lower_blocks(width, lanes)) * lanes
-    half = packed // 2
-    share = half // ndata
-    tile = (8, lanes)
-    assert share % 8 == 0 and share % chips == 0 and share // chips <= 8
-    dma = pltpu.SemaphoreType.DMA
-    return pl.pallas_call(
-        gram_kernel,
-        out_shape=(
-            jax.ShapeDtypeStruct((ndata, chunk, size), f32),
-            jax.ShapeDtypeStruct((packed, lanes), f32),
-            jax.ShapeDtypeStruct((2, *tile), f32),
-        ),
-        in_specs=[vmem(), vmem()],
-        out_specs=(vmem(), vmem(), vmem()),
-        scratch_shapes=[
-            pltpu.VMEM((packed, lanes), f32),
-            pltpu.VMEM((half, lanes), f32),
-            pltpu.VMEM((half, lanes), f32),
-            pltpu.VMEM((ndata, share, lanes), f32),
-            pltpu.VMEM((chips, *tile), f32),
-            pltpu.VMEM((chips, *tile), f32),
-            pltpu.VMEM((chips, 3, *tile), f32),
-            pltpu.VMEM((share, lanes), f32),
-            pltpu.VMEM((2, 2, *tile), f32),
-            dma((2, ndata)),
-            dma((2, 3)),
-            dma((2, ndata)),
-            dma((2, chips)),
-            dma((2, chips)),
-            dma((2, ndata)),
-        ],
-        compiler_params=pltpu.CompilerParams(
-            collective_id=1, has_side_effects=True, vmem_limit_bytes=24 * 2**20
-        ),
-        name="gram",
-    )(sketch, mine)
 
 
 def corner_inverse(tile, pivots=8):
@@ -452,7 +340,8 @@
     RING = (0, 1, 3, 4, 5, 7, 8)
     CROSS = (1, 5, 9, 12)
 
-    def __init__(self, all_ref, got_sems, ring_sems, pair_sems, cross_sems):
+    def __init__(self, lead, all_ref, got_sems, ring_sems, pair_sems, cross_sems):
+        self.lead = lead
         self.all_ref, self.got_sems = all_ref, got_sems
         self.ring_sems, self.pair_sems, self.cross_sems = ring_sems, pair_sems, cross_sems
         at = lax.axis_index("cols")
@@ -532,16 +421,26 @@
         def _():
             self.to_pair(slot, n + 1)
 
-    def begin(self):
+    def begin(self, first=None, second=None):
         self.to_pair(self.own, 0)
         self.to_ring(self.own, 0)
         self.to_across(self.own, 0)
+        if first is not None:
+            first()
         self.arrived(self.pair)
         self.to_ring(self.pair, 1)
         self.arrived(self.across)
         self.to_ring(self.across, 2)
         self.to_pair(self.across, 3)
         self.hand_on(0)
+        if second is not None:
+            second()
+
+        def early(n, carry):
+            self.hand_on(n)
+            return carry
+
+        lax.fori_loop(1, self.lead, early, 0)
 
     def run(self, work, also):
         work([self.own, self.pair])
@@ -551,9 +450,9 @@
             for at, act in also.items():
                 pl.when(n == at)(act)
 
-            @pl.when(n < last)
+            @pl.when(n + self.lead <= last)
             def _():
-                ahead = n + 1
+                ahead = n + self.lead
                 swap = ahead // 11 - 2 * (ahead // 12) + ahead // 13
                 self.hand_on(ahead + swap)
 
@@ -613,31 +512,116 @@
     )
 
 
-def sketch_kernel(block, width, part_ref, here_ref, total_ref, all_ref, *sems):
-    ring = Ring(all_ref, *sems)
-    ring.greet()
+def sketch_kernel(block, width, own_ref, part_ref, mine_ref, rows_ref, gram_ref, totals_ref, *scratch):
+    here_ref, total_ref, col_sems, here_sems, mine_sems, *scratch = scratch
+    ring = Ring(5, *scratch[:5])
+    data_at, col_at = lax.axis_index("dp"), lax.axis_index("cols")
+    greet(("cols", 1), ("dp", 1))
+
+    def to_col(offset, peer):
+        return put_copy(
+            own_ref.at[peer],
+            here_ref.at[data_at, col_at],
+            col_sems.at[0, offset],
+            col_sems.at[1, offset],
+            "cols",
+            peer,
+        )
+
+    def mine_to_data(offset, peer):
+        return put_copy(
+            own_ref,
+            mine_ref.at[data_at],
+            mine_sems.at[0, offset],
+            mine_sems.at[1, offset],
+            "dp",
+            peer,
+        )
+
+    def here_to_data(offset, peer):
+        return put_copy(
+            here_ref.at[data_at],
+            here_ref.at[data_at],
+            here_sems.at[0, offset],
+            here_sems.at[1, offset],
+            "dp",
+            peer,
+        )
+
+    def first():
+        over_peers("cols", lambda offset, peer: to_col(offset, peer).start())
+        here_ref[data_at, col_at] = own_ref[col_at]
+        mine_ref[data_at] = own_ref[...]
+
+    def second():
+        over_peers("cols", lambda offset, peer: to_col(offset, peer).wait())
+        over_peers("dp", lambda offset, peer: here_to_data(offset, peer).start())
+        over_peers("dp", lambda offset, peer: mine_to_data(offset, peer).start())
+
+    all_ref = scratch[0]
     all_ref[ring.own] = part_ref[...]
-    ring.begin()
+    ring.begin(first, second)
     total_ref[...] = jnp.zeros_like(total_ref)
+    over_peers("dp", lambda offset, peer: here_to_data(offset, peer).wait())
 
     def work(slots):
         total_ref[...] += block_sums(all_ref, here_ref, slots, block, width, False)
 
     ring.run(work, {})
-
-
-def sketch_sums(part, here, block, width):
+    over_peers("dp", lambda offset, peer: mine_to_data(offset, peer).wait())
+    gram_steps(total_ref, mine_ref, rows_ref, gram_ref, totals_ref, *scratch[5:])
+
+
+def sketch_and_gram(own, part, block, width):
+    ndata, ncols = lax.axis_size("dp"), lax.axis_size("cols")
+    whole, size = part.shape
+    chips = ncols // 2
+    lanes = own.shape[-1]
+    f32 = jnp.float32
+    packed = len(lower_blocks(whole, lanes)) * lanes
+    half = packed // 2
+    share = half // ndata
+    tile = (8, lanes)
+    assert share % 8 == 0 and share % chips == 0 and share // chips <= 8
+    dma = pltpu.SemaphoreType.DMA
     return pl.pallas_call(
         functools.partial(sketch_kernel, block, width),
-        out_shape=jax.ShapeDtypeStruct(part.shape, jnp.float32),
+        out_shape=(
+            jax.ShapeDtypeStruct((ndata, *own.shape), f32),
+            jax.ShapeDtypeStruct((ndata, width, size), f32),
+            jax.ShapeDtypeStruct((packed, lanes), f32),
+            jax.ShapeDtypeStruct((2, *tile), f32),
+        ),
         in_specs=[vmem(), vmem()],
-        out_specs=vmem(),
-        scratch_shapes=ring_scratch(part.shape),
+        out_specs=(vmem(), vmem(), vmem(), vmem()),
+        scratch_shapes=[
+            pltpu.VMEM((ndata, *own.shape), f32),
+            pltpu.VMEM((whole, size), f32),
+            dma((2, ncols)),
+            dma((2, ndata)),
+            dma((2, ndata)),
+            *ring_scratch(part.shape),
+            pltpu.VMEM((packed, lanes), f32),
+            pltpu.VMEM((half, lanes), f32),
+            pltpu.VMEM((half, lanes), f32),
+            pltpu.VMEM((ndata, share, lanes), f32),
+            pltpu.VMEM((chips, *tile), f32),
+            pltpu.VMEM((chips, *tile), f32),
+            pltpu.VMEM((chips, 3, *tile), f32),
+            pltpu.VMEM((share, lanes), f32),
+            pltpu.VMEM((2, 2, *tile), f32),
+            dma((2, ndata)),
+            dma((2, 3)),
+            dma((2, ndata)),
+            dma((2, chips)),
+            dma((2, chips)),
+            dma((2, ndata)),
+        ],
         compiler_params=pltpu.CompilerParams(
-            collective_id=2, has_side_effects=True, vmem_limit_bytes=40 * 2**20
+            collective_id=0, has_side_effects=True, vmem_limit_bytes=40 * 2**20
         ),
         name="sketch",
-    )(part, here)
+    )(own, part)
 
 
 def project_kernel(
@@ -657,7 +641,7 @@
     all_ref,
     *sems,
 ):
-    ring = Ring(all_ref, *sems)
+    ring = Ring(1, all_ref, *sems)
     ring.greet(("dp", 1))
     data_at, col_at = lax.axis_index("dp"), lax.axis_index("cols")
     size = basis_ref.shape[0]
@@ -750,7 +734,7 @@
             *ring_scratch(half.shape),
         ],
         compiler_params=pltpu.CompilerParams(
-            collective_id=3, has_side_effects=True, vmem_limit_bytes=40 * 2**20
+            collective_id=1, has_side_effects=True, vmem_limit_bytes=40 * 2**20
         ),
         name="project",
     )(half, basis_part, mine, totals)
@@ -771,11 +755,9 @@
     suffix_local = suffix_ids.reshape(ncols, slots) & (block - 1)
     packed = prefix_local * block + suffix_local
     own = jnp.stack([packed.astype(jnp.float32), live_weights], axis=1)
-    here, mine = exchange_records(own)
     part = lax.dynamic_slice_in_dim(omega, data_at * chunk, chunk, 1)
     part = part.reshape(ndata, size, chunk).swapaxes(1, 2).reshape(ndata * chunk, size)
-    sketch = sketch_sums(part, here, block, chunk)
-    rows, gram, totals = sum_gram(sketch.reshape(ndata, chunk, size), mine)
+    mine, rows, gram, totals = sketch_and_gram(own, part, block, chunk)
     basis_part, q_half = factor_and_q(gram, rows.reshape(width, size))
     scale = math.sqrt(block * ncols)
     coefficients, q_block = project(q_half, basis_part, mine, totals, scale, block, chunk)

time: 197 us -> 184 us (0.934)
  Pallas kernels: 188 us -> 177 us
    pallas_call x3 -> x1, Pallas kernels: 110 us -> 100 us  [sketch_and_gram(): pl.pallas_call(functools.partial(sketch_kernel, block, width), out_shape=...]
where the time goes in v6:
time: 184 us
  Pallas kernels  177 us (96%)
  other arithmetic  4.35 us (2%)
    pallas_call x1, Pallas kernels, sketch_and_gram(): pl.pallas_call(functools.partial(sketch_kernel, block, width), out_shape=...  100 us
    pallas_call x1, Pallas kernels, project(): pl.pallas_call(functools.partial(project_kernel, scale, block, width), ou...  53.2 us
    pallas_call x1, Pallas kernels, factor_and_q(): pl.pallas_call(factor_kernel, out_shape=(jax.ShapeDtypeStruct((size, widt...  24.1 us

profile of v6, /device:TPU:1, one launch (start us, length us, event | category | flops | bytes accessed | tf_op | source)
XLA Modules:
  0.0 183.6 jit_solution(13602206243587448288)
XLA Ops:
  0.6 0.0 copy-start
  0.7 0.9 add_convert_fusion
  1.5 0.8 compare_select_fusion
  2.4 0.0 copy-done
  2.4 0.2 constant_dynamic-slice_fusion
  2.6 0.2 copy.8
  2.8 100.0 %sketch.1 = (f32[8,32,2,128]{3,2,1,0:T(2,128)S(1)}, f32[8,64,256]{2,1,0:T(8,128)S(1)}, f32[1280,128]{1,0:T(8,128)S(1)}, f32[2,8,128]{2,1,0:T(8,128)S(1)}) custom-call(f32[32,2,128]{2,1,0:T(2,128)S(1)} %pad_maximum_fusion.own_ref, bf16[512,256]{1,0:T(8,128)(2,1)S(1)} %bitcast.9), custom_call_target="tpu_custom_call" | custom-call | tf_op jit(solution)/shard_map/sketch/pallas_call | solution.py:587
  102.8 24.1 %factor.1 = (bf16[256,512]{1,0:T(8,128)(2,1)S(1)}, bf16[512,256]{1,0:T(8,128)(2,1)S(1)}) custom-call(f32[1280,128]{1,0:T(8,128)S(1)} %get-tuple-element.10.gram_ref, f32[512,256]{1,0:T(8,128)S(1)} %bitcast.10), custom_call_target="tpu_custom_call" | custom-call | tf_op jit(solution)/shard_map/factor/pallas_call | solution.py:324
  127.0 53.2 %project.1 = (f32[64,2048]{1,0:T(8,128)S(1)}, bf16[2048,512]{1,0:T(8,128)(2,1)S(1)}) custom-call(bf16[512,256]{1,0:T(8,128)(2,1)S(1)} %get-tuple-element.12.half_ref, bf16[256,512]{1,0:T(8,128)(2,1)S(1)} %get-tuple-element.13.basis_ref, f32[8,32,2,128]{3,2,1,0:T(2,128)S(1)} %get-tuple-element.14.mine_ref, f32[2,8,128]{2,1,0:T(8,128)S(1)} %get-tuple-element.15.totals_ref), custom_call_target="tpu_custom_call" | custom-call | tf_op jit(solution)/shard_map/project/pallas_call | solution.py:721
  180.2 2.6 %convert_multiply_fusion = f32[2048,512]{1,0:T(8,128)} fusion(bf16[2048,512]{1,0:T(8,128)(2,1)S(1)} %get-tuple-element.16), kind=kLoop, calls=%fused_computation | loop fusion | flops 2097152 | bytes 6291456 | tf_op jit(solution)/shard_map/mul | solution.py:764
  182.8 0.8 copy.12
  (1 shorter events, 0.0 us)
Async XLA Ops:
  0.6 1.8 copy-start

commit v7 on v6

--- a/solution.py
+++ b/solution.py
@@ -337,8 +337,8 @@
 
 class Ring:
     ARRIVALS = 15
-    RING = (0, 1, 3, 4, 5, 7, 8)
-    CROSS = (1, 5, 9, 12)
+    RING = (0, 1, 3, 4, 5, 7, 8, 11)
+    CROSS = (1, 5, 9)
 
     def __init__(self, lead, all_ref, got_sems, ring_sems, pair_sems, cross_sems):
         self.lead = lead
@@ -397,23 +397,11 @@
         self.arrived(slot)
         turn, step = lax.rem(m, 4), m // 4 + 1
 
-        @pl.when((turn == 0) & (step < 4))
+        @pl.when(((turn == 1) & (step < 3)) | ((turn != 1) & (turn != 2) & (step < 4)))
         def _():
             self.to_ring(slot, m + 3)
 
-        @pl.when((turn == 1) & (step < 3))
-        def _():
-            self.to_ring(slot, m + 3)
-
-        @pl.when(m == 3)
-        def _():
-            self.to_ring(slot, m + 3)
-
-        @pl.when(m == 8)
-        def _():
-            self.to_ring(self.slot(7), 7 + 3)
-
-        @pl.when((turn == 1) | (m == 12))
+        @pl.when(turn == 1)
         def _():
             self.to_across(slot, m)
 
@@ -421,20 +409,20 @@
         def _():
             self.to_pair(slot, n + 1)
 
-    def begin(self, first=None, second=None):
+    def begin(self, *between):
+        first, second, third = between or [lambda: None] * 3
         self.to_pair(self.own, 0)
         self.to_ring(self.own, 0)
         self.to_across(self.own, 0)
-        if first is not None:
-            first()
+        first()
         self.arrived(self.pair)
         self.to_ring(self.pair, 1)
+        second()
         self.arrived(self.across)
         self.to_ring(self.across, 2)
         self.to_pair(self.across, 3)
         self.hand_on(0)
-        if second is not None:
-            second()
+        third()
 
         def early(n, carry):
             self.hand_on(n)
@@ -452,9 +440,7 @@
 
             @pl.when(n + self.lead <= last)
             def _():
-                ahead = n + self.lead
-                swap = ahead // 11 - 2 * (ahead // 12) + ahead // 13
-                self.hand_on(ahead + swap)
+                self.hand_on(n + self.lead)
 
             m = self.place(n)
             mirrored = self.slot(m, mirror=True)
@@ -491,13 +477,13 @@
     ]
 
 
-def block_sums(all_ref, records_ref, slots, block, width, by_prefix):
+def block_sums(all_ref, records_ref, slots, places, block, width, by_prefix):
     shift = block.bit_length() - 1
     rows = range(records_ref.shape[0])
     placed, spots = [], []
-    for slot in slots:
-        packed = [records_ref[d, slot, 0:1, :].astype(jnp.int32) for d in rows]
-        weight = [records_ref[d, slot, 1:2, :] for d in rows]
+    for slot, place in zip(slots, places):
+        packed = [records_ref[d, place, 0:1, :].astype(jnp.int32) for d in rows]
+        weight = [records_ref[d, place, 1:2, :] for d in rows]
         prefix = [lax.shift_right_logical(ids, shift) for ids in packed]
         suffix = [ids & (block - 1) for ids in packed]
         take, put = (prefix, suffix) if by_prefix else (suffix, prefix)
@@ -514,19 +500,49 @@
 
 def sketch_kernel(block, width, own_ref, part_ref, mine_ref, rows_ref, gram_ref, totals_ref, *scratch):
     here_ref, total_ref, col_sems, here_sems, mine_sems, *scratch = scratch
-    ring = Ring(5, *scratch[:5])
+    ring = Ring(2, *scratch[:5])
     data_at, col_at = lax.axis_index("dp"), lax.axis_index("cols")
     greet(("cols", 1), ("dp", 1))
 
-    def to_col(offset, peer):
+    ncols = lax.axis_size("cols")
+    near = 12
+
+    def place_at(slot, device):
+        return lax.rem(slot - device // 4 * 4 + 4 + ncols, ncols)
+
+    own_place = place_at(col_at, col_at)
+
+    def peer_at(place):
+        return lax.rem(col_at // 4 * 4 - 4 + place + ncols, ncols)
+
+    def to_col(place):
+        peer = peer_at(place)
+        there = place_at(col_at, peer)
         return put_copy(
             own_ref.at[peer],
-            here_ref.at[data_at, col_at],
-            col_sems.at[0, offset],
-            col_sems.at[1, offset],
+            here_ref.at[data_at, there],
+            col_sems.at[0, place],
+            col_sems.at[1, there],
             "cols",
             peer,
         )
+
+    def from_col(place):
+        return put_copy(
+            own_ref.at[peer_at(place)],
+            here_ref.at[data_at, place],
+            col_sems.at[0, place],
+            col_sems.at[1, place],
+            "cols",
+            peer_at(place),
+        )
+
+    def others(start, end, act):
+        def one(place, carry):
+            pl.when(place != own_place)(lambda: act(place))
+            return carry
+
+        lax.fori_loop(start, end, one, 0)
 
     def mine_to_data(offset, peer):
         return put_copy(
@@ -538,36 +554,54 @@
             peer,
         )
 
-    def here_to_data(offset, peer):
-        return put_copy(
-            here_ref.at[data_at],
-            here_ref.at[data_at],
-            here_sems.at[0, offset],
-            here_sems.at[1, offset],
-            "dp",
-            peer,
-        )
+    def here_to_data(group):
+        places = pl.ds(0, near) if group == 0 else pl.ds(near, ncols - near)
+
+        def make(offset, peer):
+            return put_copy(
+                here_ref.at[data_at, places],
+                here_ref.at[data_at, places],
+                here_sems.at[0, group, offset],
+                here_sems.at[1, group, offset],
+                "dp",
+                peer,
+            )
+
+        return make
+
+    def begin_data(group):
+        over_peers("dp", lambda offset, peer: here_to_data(group)(offset, peer).start())
+
+    def end_data(group):
+        over_peers("dp", lambda offset, peer: here_to_data(group)(offset, peer).wait())
 
     def first():
-        over_peers("cols", lambda offset, peer: to_col(offset, peer).start())
-        here_ref[data_at, col_at] = own_ref[col_at]
+        others(0, ncols, lambda place: to_col(place).start())
+        here_ref[data_at, own_place] = own_ref[col_at]
+
+    def second():
+        others(0, near, lambda place: from_col(place).wait())
+        begin_data(0)
         mine_ref[data_at] = own_ref[...]
 
-    def second():
-        over_peers("cols", lambda offset, peer: to_col(offset, peer).wait())
-        over_peers("dp", lambda offset, peer: here_to_data(offset, peer).start())
-        over_peers("dp", lambda offset, peer: mine_to_data(offset, peer).start())
+    def third():
+        others(near, ncols, lambda place: from_col(place).wait())
+        begin_data(1)
 
     all_ref = scratch[0]
     all_ref[ring.own] = part_ref[...]
-    ring.begin(first, second)
+    ring.begin(first, second, third)
     total_ref[...] = jnp.zeros_like(total_ref)
-    over_peers("dp", lambda offset, peer: here_to_data(offset, peer).wait())
+    end_data(0)
 
     def work(slots):
-        total_ref[...] += block_sums(all_ref, here_ref, slots, block, width, False)
-
-    ring.run(work, {})
+        places = [place_at(slot, col_at) for slot in slots]
+        total_ref[...] += block_sums(all_ref, here_ref, slots, places, block, width, False)
+
+    def begin_mine():
+        over_peers("dp", lambda offset, peer: mine_to_data(offset, peer).start())
+
+    ring.run(work, {0: begin_mine, 4: lambda: end_data(1)})
     over_peers("dp", lambda offset, peer: mine_to_data(offset, peer).wait())
     gram_steps(total_ref, mine_ref, rows_ref, gram_ref, totals_ref, *scratch[5:])
 
@@ -598,7 +632,7 @@
             pltpu.VMEM((ndata, *own.shape), f32),
             pltpu.VMEM((whole, size), f32),
             dma((2, ncols)),
-            dma((2, ndata)),
+            dma((2, 2, ndata)),
             dma((2, ndata)),
             *ring_scratch(part.shape),
             pltpu.VMEM((packed, lanes), f32),
@@ -695,7 +729,7 @@
             other_x_copy(offset).start()
 
     def work(slots):
-        total_ref[...] += block_sums(all_ref, mine_ref, slots, block, width, True)
+        total_ref[...] += block_sums(all_ref, mine_ref, slots, slots, block, width, True)
 
     over_peers("dp", lambda offset, peer: half_copy(offset, peer).start())
     all_ref[col_at, own_rows, :] = half_ref[own_rows, :]

time: 184 us -> 173 us (0.940)
  Pallas kernels: 177 us -> 166 us
    pallas_call x1, Pallas kernels: 100 us -> 92.9 us  [sketch_and_gram(): pl.pallas_call(functools.partial(sketch_kernel, block, width), out_shape=...]
    pallas_call x1, Pallas kernels: 53.2 us -> 49.2 us  [project(): pl.pallas_call(functools.partial(project_kernel, scale, block, width), ou...]
where the time goes in v7:
time: 173 us; the launch traced here: 172 us
  Pallas kernels  166 us (96%)
  other arithmetic  4.35 us (3%)
    pallas_call x1, Pallas kernels, sketch_and_gram(): pl.pallas_call(functools.partial(sketch_kernel, block, width), out_shape=...  92.9 us
    pallas_call x1, Pallas kernels, project(): pl.pallas_call(functools.partial(project_kernel, scale, block, width), ou...  49.2 us
    pallas_call x1, Pallas kernels, factor_and_q(): pl.pallas_call(factor_kernel, out_shape=(jax.ShapeDtypeStruct((size, widt...  24.1 us

profile of v7, /device:TPU:1, one launch (start us, length us, event | category | flops | bytes accessed | tf_op | source)
XLA Modules:
  0.0 172.4 jit_solution(9152083960069714955)
XLA Ops:
  0.6 0.0 copy-start
  0.7 0.9 add_convert_fusion
  1.5 0.8 compare_select_fusion
  2.4 0.0 copy-done
  2.4 0.2 constant_dynamic-slice_fusion
  2.6 0.2 copy.8
  2.8 92.9 %sketch.1 = (f32[8,32,2,128]{3,2,1,0:T(2,128)S(1)}, f32[8,64,256]{2,1,0:T(8,128)S(1)}, f32[1280,128]{1,0:T(8,128)S(1)}, f32[2,8,128]{2,1,0:T(8,128)S(1)}) custom-call(f32[32,2,128]{2,1,0:T(2,128)S(1)} %pad_maximum_fusion.own_ref, bf16[512,256]{1,0:T(8,128)(2,1)S(1)} %bitcast.9), custom_call_target="tpu_custom_call" | custom-call | tf_op jit(solution)/shard_map/sketch/pallas_call | solution.py:621
  95.7 24.1 %factor.1 = (bf16[256,512]{1,0:T(8,128)(2,1)S(1)}, bf16[512,256]{1,0:T(8,128)(2,1)S(1)}) custom-call(f32[1280,128]{1,0:T(8,128)S(1)} %get-tuple-element.10.gram_ref, f32[512,256]{1,0:T(8,128)S(1)} %bitcast.10), custom_call_target="tpu_custom_call" | custom-call | tf_op jit(solution)/shard_map/factor/pallas_call | solution.py:324
  119.8 49.2 %project.1 = (f32[64,2048]{1,0:T(8,128)S(1)}, bf16[2048,512]{1,0:T(8,128)(2,1)S(1)}) custom-call(bf16[512,256]{1,0:T(8,128)(2,1)S(1)} %get-tuple-element.12.half_ref, bf16[256,512]{1,0:T(8,128)(2,1)S(1)} %get-tuple-element.13.basis_ref, f32[8,32,2,128]{3,2,1,0:T(2,128)S(1)} %get-tuple-element.14.mine_ref, f32[2,8,128]{2,1,0:T(8,128)S(1)} %get-tuple-element.15.totals_ref), custom_call_target="tpu_custom_call" | custom-call | tf_op jit(solution)/shard_map/project/pallas_call | solution.py:755
  169.0 2.6 %convert_multiply_fusion = f32[2048,512]{1,0:T(8,128)} fusion(bf16[2048,512]{1,0:T(8,128)(2,1)S(1)} %get-tuple-element.16), kind=kLoop, calls=%fused_computation | loop fusion | flops 2097152 | bytes 6291456 | tf_op jit(solution)/shard_map/mul | solution.py:798
  171.6 0.8 copy.12
  (1 shorter events, 0.0 us)
Async XLA Ops:
  0.6 1.8 %copy-start = (bf16[2048,512]{1,0:T(8,128)(2,1)S(1)}, bf16[2048,512]{1,0:T(8,128)(2,1)}, u32[]{:S(2)}) copy-start(bf16[2048,512]{1,0:T(8,128)(2,1)} %param.9) | copy-start | bytes 6291460

commit v8 on v7

--- a/solution.py
+++ b/solution.py
@@ -83,7 +83,7 @@
     for axis, stride in groups:
         over_peers(axis, lambda offset, peer, axis=axis: signal(barrier, axis, peer), stride)
     count = sum(lax.axis_size(axis) // stride - 1 for axis, stride in groups)
-    pl.semaphore_wait(barrier, count + len(near))
+    return lambda: pl.semaphore_wait(barrier, count + len(near))
 
 
 def lower_blocks(width, lanes):
@@ -289,7 +289,7 @@
     return jnp.concatenate(done, axis=0)
 
 
-def factor_kernel(gram_ref, rows_ref, basis_ref, half_ref, work_ref, inverse_ref):
+def factor_steps(gram_ref, rows_ref, work_ref, inverse_ref, ready):
     n = work_ref.shape[0]
     size = gram_ref.shape[1]
     for at, (i, j) in enumerate(lower_blocks(n, size)):
@@ -312,27 +312,7 @@
                     low, inverse_ref[start:end, :start], ((1,), (0,))
                 )
             inverse_ref[end:, start:end] = -dot_exact(low, corner, ((1,), (0,)))
-    for start in range(0, n, size):
-        end = start + size
-        q = dot_exact(inverse_ref[start:end, :end], rows_ref[:end, :], ((1,), (0,)))
-        half_ref[start:end, :] = q.astype(jnp.bfloat16)
-        basis_ref[:, start:end] = q.T.astype(jnp.bfloat16)
-
-
-def factor_and_q(gram, rows):
-    width, size = rows.shape
-    return pl.pallas_call(
-        factor_kernel,
-        out_shape=(
-            jax.ShapeDtypeStruct((size, width), jnp.bfloat16),
-            jax.ShapeDtypeStruct((width, size), jnp.bfloat16),
-        ),
-        in_specs=[vmem(), vmem()],
-        out_specs=(vmem(), vmem()),
-        scratch_shapes=[pltpu.VMEM((width, width), jnp.float32)] * 2,
-        compiler_params=pltpu.CompilerParams(vmem_limit_bytes=24 * 2**20),
-        name="factor",
-    )(gram, rows)
+        ready(start, end, dot_exact(inverse_ref[start:end, :end], rows_ref[:end, :], ((1,), (0,))))
 
 
 class Ring:
@@ -373,7 +353,7 @@
         return self.device(away, turn // 2, lax.rem((turn + 1) // 2, 2), mirror)
 
     def greet(self, *groups):
-        greet(*groups, near=(self.pair, self.across, self.after, self.before))
+        return greet(*groups, near=(self.pair, self.across, self.after, self.before))
 
     def copy(self, slot, send, peer):
         part = self.all_ref.at[slot]
@@ -502,7 +482,7 @@
     here_ref, total_ref, col_sems, here_sems, mine_sems, *scratch = scratch
     ring = Ring(2, *scratch[:5])
     data_at, col_at = lax.axis_index("dp"), lax.axis_index("cols")
-    greet(("cols", 1), ("dp", 1))
+    greet(("cols", 1), ("dp", 1))()
 
     ncols = lax.axis_size("cols")
     near = 12
@@ -662,12 +642,16 @@
     scale,
     block,
     width,
-    half_ref,
-    basis_ref,
+    gram_ref,
+    rows_ref,
     mine_ref,
     totals_ref,
     coef_ref,
     whole_ref,
+    work_ref,
+    inverse_ref,
+    half_ref,
+    basis_ref,
     total_ref,
     half_sems,
     basis_sems,
@@ -676,21 +660,29 @@
     *sems,
 ):
     ring = Ring(1, all_ref, *sems)
-    ring.greet(("dp", 1))
+    greeted = ring.greet(("dp", 1))
     data_at, col_at = lax.axis_index("dp"), lax.axis_index("cols")
     size = basis_ref.shape[0]
     ndata = whole_ref.shape[0] // size
     own_rows = pl.ds(pl.multiple_of(data_at * width, width), width)
 
-    def half_copy(offset, peer):
-        return put_copy(
-            half_ref.at[pl.ds(pl.multiple_of(peer * width, width), width), :],
+    def half_copy(peer, sender):
+        return put_copy(
+            half_ref.at[peer * width : (peer + 1) * width, :],
             all_ref.at[col_at, own_rows, :],
-            half_sems.at[0, offset],
-            half_sems.at[1, offset],
+            half_sems.at[0, peer],
+            half_sems.at[1, sender],
             "dp",
             peer,
         )
+
+    def ready(start, end, q):
+        half_ref[start:end, :] = q.astype(jnp.bfloat16)
+        basis_ref[:, start:end] = q.T.astype(jnp.bfloat16)
+        if start == 0:
+            greeted()
+        for peer in range(start // width, end // width):
+            pl.when(peer != data_at)(lambda peer=peer: half_copy(peer, data_at).start())
 
     along = ndata // 2
     other = lax.rem(data_at + along, ndata)
@@ -731,10 +723,11 @@
     def work(slots):
         total_ref[...] += block_sums(all_ref, mine_ref, slots, slots, block, width, True)
 
-    over_peers("dp", lambda offset, peer: half_copy(offset, peer).start())
+    factor_steps(gram_ref, rows_ref, work_ref, inverse_ref, ready)
     all_ref[col_at, own_rows, :] = half_ref[own_rows, :]
     total_ref[...] = jnp.zeros_like(total_ref)
-    over_peers("dp", lambda offset, peer: half_copy(offset, peer).wait())
+    for peer in range(ndata):
+        pl.when(peer != data_at)(lambda peer=peer: half_copy(peer, peer).wait())
     ring.begin()
     ring.run(work, {0: begun, 6: later})
     factor = scale * jnp.sum(totals_ref[1]) / jnp.sum(totals_ref[0])
@@ -747,31 +740,34 @@
     own_copy.wait()
 
 
-def project(half, basis_part, mine, totals, scale, block, width):
+def project(gram, rows, mine, totals, scale, block, width):
     ndata = lax.axis_size("dp")
-    size, whole = basis_part.shape
+    whole, size = rows.shape
     dma = pltpu.SemaphoreType.DMA
-    anywhere = pl.BlockSpec(memory_space=pl.ANY)
     return pl.pallas_call(
         functools.partial(project_kernel, scale, block, width),
         out_shape=(
             jax.ShapeDtypeStruct((width, block), jnp.float32),
             jax.ShapeDtypeStruct((size * ndata, whole), jnp.bfloat16),
         ),
-        in_specs=[vmem(), anywhere, vmem(), vmem()],
-        out_specs=(vmem(), anywhere),
+        in_specs=[vmem(), vmem(), vmem(), vmem()],
+        out_specs=(vmem(), pl.BlockSpec(memory_space=pl.ANY)),
         scratch_shapes=[
-            pltpu.VMEM(half.shape, jnp.float32),
+            pltpu.VMEM((whole, whole), jnp.float32),
+            pltpu.VMEM((whole, whole), jnp.float32),
+            pltpu.VMEM((whole, size), jnp.bfloat16),
+            pltpu.VMEM((size, whole), jnp.bfloat16),
+            pltpu.VMEM((whole, size), jnp.float32),
             dma((2, ndata)),
             dma((2, ndata)),
             dma,
-            *ring_scratch(half.shape),
+            *ring_scratch((whole, size)),
         ],
         compiler_params=pltpu.CompilerParams(
             collective_id=1, has_side_effects=True, vmem_limit_bytes=40 * 2**20
         ),
         name="project",
-    )(half, basis_part, mine, totals)
+    )(gram, rows, mine, totals)
 
 
 def shards(prefix_ids, suffix_ids, weights, counts, omega):
@@ -792,9 +788,9 @@
     part = lax.dynamic_slice_in_dim(omega, data_at * chunk, chunk, 1)
     part = part.reshape(ndata, size, chunk).swapaxes(1, 2).reshape(ndata * chunk, size)
     mine, rows, gram, totals = sketch_and_gram(own, part, block, chunk)
-    basis_part, q_half = factor_and_q(gram, rows.reshape(width, size))
     scale = math.sqrt(block * ncols)
-    coefficients, q_block = project(q_half, basis_part, mine, totals, scale, block, chunk)
+    rows = rows.reshape(width, size)
+    coefficients, q_block = project(gram, rows, mine, totals, scale, block, chunk)
     basis = scale * q_block.astype(jnp.float32)
     return (basis, coefficients)
 

time: 173 us -> 169 us (0.977)
  Pallas kernels: 166 us -> 161 us
    pallas_call x1 -> x0, Pallas kernels: 24.1 us -> none  [factor_and_q(): pl.pallas_call(factor_kernel, out_shape=(jax.ShapeDtypeStruct((size, widt...]
    pallas_call x1, Pallas kernels: 49.2 us -> 68 us  [project(): pl.pallas_call(functools.partial(project_kernel, scale, block, width), ou...]
where the time goes in v8:
time: 169 us; the launch traced here: 167 us
  Pallas kernels  161 us (95%)
  other arithmetic  4.35 us (3%)
    pallas_call x1, Pallas kernels, sketch_and_gram(): pl.pallas_call(functools.partial(sketch_kernel, block, width), out_shape=...  92.7 us
    pallas_call x1, Pallas kernels, project(): pl.pallas_call(functools.partial(project_kernel, scale, block, width), ou...  68 us

profile of v8, /device:TPU:1, one launch (start us, length us, event | category | flops | bytes accessed | tf_op | source)
XLA Modules:
  0.0 167.0 jit_solution(6719564356794303340)
XLA Ops:
  0.6 0.0 copy-start
  0.7 0.9 add_convert_fusion
  1.5 0.8 compare_select_fusion
  2.4 0.0 copy-done
  2.4 0.2 constant_dynamic-slice_fusion
  2.6 0.2 copy.8
  2.8 92.7 %sketch.1 = (f32[8,32,2,128]{3,2,1,0:T(2,128)S(1)}, f32[8,64,256]{2,1,0:T(8,128)S(1)}, f32[1280,128]{1,0:T(8,128)S(1)}, f32[2,8,128]{2,1,0:T(8,128)S(1)}) custom-call(f32[32,2,128]{2,1,0:T(2,128)S(1)} %pad_maximum_fusion.own_ref, bf16[512,256]{1,0:T(8,128)(2,1)S(1)} %bitcast.9), custom_call_target="tpu_custom_call" | custom-call | tf_op jit(solution)/shard_map/sketch/pallas_call | solution.py:601
  95.5 68.0 %project.1 = (f32[64,2048]{1,0:T(8,128)S(1)}, bf16[2048,512]{1,0:T(8,128)(2,1)S(1)}) custom-call(f32[1280,128]{1,0:T(8,128)S(1)} %get-tuple-element.8.gram_ref, f32[512,256]{1,0:T(8,128)S(1)} %bitcast.10, f32[8,32,2,128]{3,2,1,0:T(2,128)S(1)} %get-tuple-element.10.mine_ref, f32[2,8,128]{2,1,0:T(8,128)S(1)} %get-tuple-element.11.totals_ref), custom_call_target="tpu_custom_call" | custom-call | tf_op jit(solution)/shard_map/project/pallas_call | solution.py:747
  163.6 2.6 %convert_multiply_fusion = f32[2048,512]{1,0:T(8,128)} fusion(bf16[2048,512]{1,0:T(8,128)(2,1)S(1)} %get-tuple-element.12), kind=kLoop, calls=%fused_computation | loop fusion | flops 2097152 | bytes 6291456 | tf_op jit(solution)/shard_map/mul | solution.py:794
  166.2 0.8 copy.12
  (1 shorter events, 0.0 us)
Async XLA Ops:
  0.6 1.8 %copy-start = (bf16[2048,512]{1,0:T(8,128)(2,1)S(1)}, bf16[2048,512]{1,0:T(8,128)(2,1)}, u32[]{:S(2)}) copy-start(bf16[2048,512]{1,0:T(8,128)(2,1)} %param.9) | copy-start | bytes 6291460

commit v9 on v8

--- a/solution.py
+++ b/solution.py
@@ -76,14 +76,18 @@
     )
 
 
-def greet(*groups, near=()):
+def greet(*groups, near=(), plane=()):
     barrier = pltpu.get_barrier_semaphore()
     for peer in near:
         signal(barrier, "cols", peer)
     for axis, stride in groups:
         over_peers(axis, lambda offset, peer, axis=axis: signal(barrier, axis, peer), stride)
+    for device in plane:
+        pl.semaphore_signal(
+            barrier, inc=1, device_id=device, device_id_type=pl.DeviceIdType.MESH
+        )
     count = sum(lax.axis_size(axis) // stride - 1 for axis, stride in groups)
-    return lambda: pl.semaphore_wait(barrier, count + len(near))
+    return lambda: pl.semaphore_wait(barrier, count + len(near) + len(plane))
 
 
 def lower_blocks(width, lanes):
@@ -104,28 +108,44 @@
     half_ref,
     other_ref,
     got_ref,
-    piece_ref,
-    arrived_ref,
-    shared_ref,
+    plane_ref,
     own_ref,
     sum_ref,
     rows_sems,
     pair_sems,
     part_sems,
-    piece_sems,
-    shared_sems,
+    plane_sems,
     gram_sems,
 ):
     data_at, col_at = lax.axis_index("dp"), lax.axis_index("cols")
-    core, chip = lax.rem(col_at, 2), col_at // 2
+    core, y, z = lax.rem(col_at, 2), lax.rem(col_at // 2, 2), col_at // 4
     pair = col_at + 1 - 2 * core
+    across = col_at + 2 - 4 * y
     ndata, chunk, size = rows_ref.shape
     width = ndata * chunk
     lanes = part_ref.shape[1]
     half = half_ref.shape[0]
-    share = half // ndata
-    chips = piece_ref.shape[0]
-    few = share // chips
+    share = own_ref.shape[0]
+    spots = 2 * ndata
+    spot = 2 * data_at + y
+
+    def over_plane(act):
+        def one(offset, carry):
+            to = lax.rem(spot + offset, spots)
+            act(offset, to, {"dp": to // 2, "cols": z * 4 + lax.rem(to, 2) * 2 + core})
+            return carry
+
+        lax.fori_loop(1, spots, one, 0)
+
+    def copy_to(src, dst, sems, at, device):
+        return pltpu.make_async_remote_copy(
+            src_ref=src,
+            dst_ref=dst,
+            send_sem=sems.at[0, at],
+            recv_sem=sems.at[1, at],
+            device_id=device,
+            device_id_type=pl.DeviceIdType.MESH,
+        )
 
     def rows_copy(offset, peer):
         return put_copy(
@@ -147,7 +167,6 @@
         sum_ref.at[0], sum_ref.at[1], pair_sems.at[0, 0], pair_sems.at[1, 0], "cols", pair
     )
     sums_copy.start()
-    piece_ref[...] = jnp.zeros_like(piece_ref)
     over_peers("dp", lambda offset, peer: rows_copy(offset, peer).wait())
     rows = rows_ref[...].reshape(width, size)
     gram = dot_exact(rows, rows, ((1,), (1,)))
@@ -166,74 +185,48 @@
     )
     pair_copy.start()
     sums_copy.wait()
-    shared_ref[chip, 1] = sum_ref[0, 0] + sum_ref[1, 0]
-    shared_ref[chip, 2] = sum_ref[0, 1] + sum_ref[1, 1]
+    sum_ref[0] = sum_ref[0] + sum_ref[1]
+    sums_copy = put_copy(
+        sum_ref.at[0], sum_ref.at[2], pair_sems.at[0, 3], pair_sems.at[1, 3], "cols", across
+    )
+    sums_copy.start()
     pair_copy.wait()
     half_ref[...] = part_ref[rows_at(core * half, half), :] + other_ref[...]
 
-    def part_copy(offset, peer):
+    def part_copy(offset, to, device):
+        source = half_ref.at[rows_at(to * share, share), :]
+        return copy_to(source, got_ref.at[spot], part_sems, offset, device)
+
+    over_plane(lambda *at: part_copy(*at).start())
+    got_ref[spot] = half_ref[rows_at(spot * share, share), :]
+    sums_copy.wait()
+    sums = sum_ref[0] + sum_ref[2]
+    over_plane(lambda *at: part_copy(*at).wait())
+    plane_ref[z, :share, :] = jnp.sum(got_ref[...], axis=0)
+    plane_ref[z, share:, :] = sums.reshape(-1, lanes)
+
+    def plane_copy(offset, peer):
         return put_copy(
-            half_ref.at[rows_at(peer * share, share), :],
-            got_ref.at[data_at],
-            part_sems.at[0, offset],
-            part_sems.at[1, offset],
-            "dp",
-            peer,
-        )
-
-    over_peers("dp", lambda offset, peer: part_copy(offset, peer).start())
-    got_ref[data_at] = half_ref[rows_at(data_at * share, share), :]
-    over_peers("dp", lambda offset, peer: part_copy(offset, peer).wait())
-    summed = jnp.sum(got_ref[...], axis=0)
-    for at in range(chips):
-        piece_ref[at, :few] = summed[few * at : few * (at + 1)]
-
-    def piece_copy(offset, peer):
-        return put_copy(
-            piece_ref.at[peer // 2],
-            arrived_ref.at[chip],
-            piece_sems.at[0, offset],
-            piece_sems.at[1, offset],
+            plane_ref.at[z],
+            plane_ref.at[z],
+            plane_sems.at[0, offset],
+            plane_sems.at[1, offset],
             "cols",
             peer,
         )
 
-    over_peers("cols", lambda offset, peer: piece_copy(offset, peer).start(), 2)
-    arrived_ref[chip] = piece_ref[chip]
-    over_peers("cols", lambda offset, peer: piece_copy(offset, peer).wait(), 2)
-    shared_ref[chip, 0] = jnp.sum(arrived_ref[...], axis=0)
-
-    def shared_copy(offset, peer):
-        return put_copy(
-            shared_ref.at[chip],
-            shared_ref.at[chip],
-            shared_sems.at[0, offset],
-            shared_sems.at[1, offset],
-            "cols",
-            peer,
-        )
-
-    over_peers("cols", lambda offset, peer: shared_copy(offset, peer).start(), 2)
-    over_peers("cols", lambda offset, peer: shared_copy(offset, peer).wait(), 2)
-    for at in range(chips):
-        own_ref[few * at : few * (at + 1), :] = shared_ref[at, 0, :few, :]
-    own_rows = rows_at((core * ndata + data_at) * share, share)
-
-    def gram_copy(offset, peer):
-        return put_copy(
-            own_ref,
-            gram_ref.at[own_rows, :],
-            gram_sems.at[0, offset],
-            gram_sems.at[1, offset],
-            "dp",
-            peer,
-        )
-
-    over_peers("dp", lambda offset, peer: gram_copy(offset, peer).start())
+    over_peers("cols", lambda offset, peer: plane_copy(offset, peer).start(), 4)
+    over_peers("cols", lambda offset, peer: plane_copy(offset, peer).wait(), 4)
+    own_ref[...] = jnp.sum(plane_ref[:, :share, :], axis=0)
+    own_rows = rows_at((core * spots + spot) * share, share)
+
+    def gram_copy(offset, to, device):
+        return copy_to(own_ref, gram_ref.at[own_rows, :], gram_sems, offset, device)
+
+    over_plane(lambda *at: gram_copy(*at).start())
     gram_ref[own_rows, :] = own_ref[...]
-    totals_ref[0] = jnp.sum(shared_ref[:, 1], axis=0)
-    totals_ref[1] = jnp.sum(shared_ref[:, 2], axis=0)
-    over_peers("dp", lambda offset, peer: gram_copy(offset, peer).wait())
+    totals_ref[...] = jnp.sum(plane_ref[:, share:, :], axis=0).reshape(totals_ref.shape)
+    over_plane(lambda *at: gram_copy(*at).wait())
     own_half = gram_ref.at[rows_at(core * half, half), :]
     last_copy = put_copy(
         own_half, own_half, pair_sems.at[0, 2], pair_sems.at[1, 2], "cols", pair
@@ -269,7 +262,7 @@
             for r in range(c + 1, pivots):
                 low[r][c] = left[r][c] * recip[c]
                 for e in range(c + 1, r + 1):
-                    left[r][e] = left[r][e] - low[r][c] * left[e][c]
+                    left[r][e] = left[r][e] - (left[r][c] * left[e][c]) * recip[c]
         for r in range(pivots):
             for c in range(r):
                 rows[r] = rows[r] - low[r][c] * rows[c]
@@ -482,7 +475,11 @@
     here_ref, total_ref, col_sems, here_sems, mine_sems, *scratch = scratch
     ring = Ring(2, *scratch[:5])
     data_at, col_at = lax.axis_index("dp"), lax.axis_index("cols")
-    greet(("cols", 1), ("dp", 1))()
+    ndata = lax.axis_size("dp")
+    across = [
+        {"dp": lax.rem(data_at + offset, ndata), "cols": ring.across} for offset in range(1, ndata)
+    ]
+    greet(("cols", 1), ("dp", 1), plane=across)()
 
     ncols = lax.axis_size("cols")
     near = 12
@@ -589,14 +586,13 @@
 def sketch_and_gram(own, part, block, width):
     ndata, ncols = lax.axis_size("dp"), lax.axis_size("cols")
     whole, size = part.shape
-    chips = ncols // 2
     lanes = own.shape[-1]
     f32 = jnp.float32
     packed = len(lower_blocks(whole, lanes)) * lanes
     half = packed // 2
-    share = half // ndata
+    share = half // (2 * ndata)
     tile = (8, lanes)
-    assert share % 8 == 0 and share % chips == 0 and share // chips <= 8
+    assert share % 8 == 0
     dma = pltpu.SemaphoreType.DMA
     return pl.pallas_call(
         functools.partial(sketch_kernel, block, width),
@@ -618,18 +614,15 @@
             pltpu.VMEM((packed, lanes), f32),
             pltpu.VMEM((half, lanes), f32),
             pltpu.VMEM((half, lanes), f32),
-            pltpu.VMEM((ndata, share, lanes), f32),
-            pltpu.VMEM((chips, *tile), f32),
-            pltpu.VMEM((chips, *tile), f32),
-            pltpu.VMEM((chips, 3, *tile), f32),
+            pltpu.VMEM((2 * ndata, share, lanes), f32),
+            pltpu.VMEM((ncols // 4, share + 2 * tile[0], lanes), f32),
             pltpu.VMEM((share, lanes), f32),
-            pltpu.VMEM((2, 2, *tile), f32),
+            pltpu.VMEM((3, 2, *tile), f32),
             dma((2, ndata)),
-            dma((2, 3)),
-            dma((2, ndata)),
-            dma((2, chips)),
-            dma((2, chips)),
-            dma((2, ndata)),
+            dma((2, 4)),
+            dma((2, 2 * ndata)),
+            dma((2, ncols // 4)),
+            dma((2, 2 * ndata)),
         ],
         compiler_params=pltpu.CompilerParams(
             collective_id=0, has_side_effects=True, vmem_limit_bytes=40 * 2**20

time: 169 us -> 164 us (0.970)
  Pallas kernels: 161 us -> 156 us
    pallas_call x1, Pallas kernels: 92.7 us -> 87.5 us  [sketch_and_gram(): pl.pallas_call(functools.partial(sketch_kernel, block, width), out_shape=...]
where the time goes in v9:
time: 164 us; the launch traced here: 163 us
  Pallas kernels  156 us (95%)
  other arithmetic  4.35 us (3%)
    pallas_call x1, Pallas kernels, sketch_and_gram(): pl.pallas_call(functools.partial(sketch_kernel, block, width), out_shape=...  87.5 us
    pallas_call x1, Pallas kernels, project(): pl.pallas_call(functools.partial(project_kernel, scale, block, width), ou...  68.9 us

profile of v9, /device:TPU:1, one launch (start us, length us, event | category | flops | bytes accessed | tf_op | source)
XLA Modules:
  0.0 162.6 jit_solution(11764586831226267527)
XLA Ops:
  0.6 0.0 copy-start
  0.7 0.9 add_convert_fusion
  1.5 0.8 compare_select_fusion
  2.4 0.0 copy-done
  2.4 0.2 constant_dynamic-slice_fusion
  2.6 0.2 copy.8
  2.8 87.5 %sketch.1 = (f32[8,32,2,128]{3,2,1,0:T(2,128)S(1)}, f32[8,64,256]{2,1,0:T(8,128)S(1)}, f32[1280,128]{1,0:T(8,128)S(1)}, f32[2,8,128]{2,1,0:T(8,128)S(1)}) custom-call(f32[32,2,128]{2,1,0:T(2,128)S(1)} %pad_maximum_fusion.own_ref, bf16[512,256]{1,0:T(8,128)(2,1)S(1)} %bitcast.9), custom_call_target="tpu_custom_call" | custom-call | tf_op jit(solution)/shard_map/sketch/pallas_call | solution.py:597
  90.3 68.9 %project.1 = (f32[64,2048]{1,0:T(8,128)S(1)}, bf16[2048,512]{1,0:T(8,128)(2,1)S(1)}) custom-call(f32[1280,128]{1,0:T(8,128)S(1)} %get-tuple-element.8.gram_ref, f32[512,256]{1,0:T(8,128)S(1)} %bitcast.10, f32[8,32,2,128]{3,2,1,0:T(2,128)S(1)} %get-tuple-element.10.mine_ref, f32[2,8,128]{2,1,0:T(8,128)S(1)} %get-tuple-element.11.totals_ref), custom_call_target="tpu_custom_call" | custom-call | tf_op jit(solution)/shard_map/project/pallas_call | solution.py:740
  159.2 2.6 %convert_multiply_fusion = f32[2048,512]{1,0:T(8,128)} fusion(bf16[2048,512]{1,0:T(8,128)(2,1)S(1)} %get-tuple-element.12), kind=kLoop, calls=%fused_computation | loop fusion | flops 2097152 | bytes 6291456 | tf_op jit(solution)/shard_map/mul | solution.py:787
  161.8 0.8 copy.12
  (1 shorter events, 0.0 us)
Async XLA Ops:
  0.6 1.8 %copy-start = (bf16[2048,512]{1,0:T(8,128)(2,1)S(1)}, bf16[2048,512]{1,0:T(8,128)(2,1)}, u32[]{:S(2)}) copy-start(bf16[2048,512]{1,0:T(8,128)(2,1)} %param.9) | copy-start | bytes 6291460

commit v10 on v9

--- a/solution.py
+++ b/solution.py
@@ -270,15 +270,31 @@
         for r in range(pivots):
             result = jnp.where(sub == r, rows[r] * lax.rsqrt(left[r][r]), result)
         done.append(jnp.where(lane <= sub + start, result, 0.0))
+        if at + 1 == blocks:
+            break
         back = [rows[r] * recip[r] for r in range(pivots)]
+
+        def columns(i):
+            return [full(work[i][:, start + c : start + c + 1]) for c in range(pivots)]
+
+        ahead = columns(at + 1)
+        for r in range(pivots):
+            for c in range(r):
+                ahead[r] = ahead[r] - low[r][c] * ahead[c]
+        terms = [ahead[c] * back[c] for c in range(pivots)]
+        while len(terms) > 1:
+            terms = [terms[c] + terms[c + 1] for c in range(0, len(terms), 2)]
+        following = jnp.where(group, 0.0, work[at + 1]) - terms[0]
         for r in range(pivots - 1, -1, -1):
             for c in range(r):
                 back[c] = back[c] - low[r][c] * back[r]
-        for i in range(at + 1, blocks):
+        for i in range(at + 2, blocks):
+            later = columns(i)
             rest = jnp.where(group, 0.0, work[i])
             for c in range(pivots):
-                rest = rest - full(work[i][:, start + c : start + c + 1]) * back[c]
+                rest = rest - later[c] * back[c]
             work[i] = rest
+        work[at + 1] = following
     return jnp.concatenate(done, axis=0)
 
 

time: 164 us -> 160 us (0.976)
  Pallas kernels: 156 us -> 152 us
    pallas_call x1, Pallas kernels: 68.9 us -> 64.7 us  [project(): pl.pallas_call(functools.partial(project_kernel, scale, block, width), ou...]
where the time goes in v10:
time: 160 us; the launch traced here: 158 us
  Pallas kernels  152 us (95%)
  other arithmetic  4.35 us (3%)
    pallas_call x1, Pallas kernels, sketch_and_gram(): pl.pallas_call(functools.partial(sketch_kernel, block, width), out_shape=...  87.5 us
    pallas_call x1, Pallas kernels, project(): pl.pallas_call(functools.partial(project_kernel, scale, block, width), ou...  64.7 us

profile of v10, /device:TPU:1, one launch (start us, length us, event | category | flops | bytes accessed | tf_op | source)
XLA Modules:
  0.0 158.4 jit_solution(11433796449118984132)
XLA Ops:
  0.6 0.0 copy-start
  0.7 0.9 add_convert_fusion
  1.5 0.8 compare_select_fusion
  2.4 0.0 copy-done
  2.4 0.2 constant_dynamic-slice_fusion
  2.6 0.2 copy.8
  2.8 87.5 %sketch.1 = (f32[8,32,2,128]{3,2,1,0:T(2,128)S(1)}, f32[8,64,256]{2,1,0:T(8,128)S(1)}, f32[1280,128]{1,0:T(8,128)S(1)}, f32[2,8,128]{2,1,0:T(8,128)S(1)}) custom-call(f32[32,2,128]{2,1,0:T(2,128)S(1)} %pad_maximum_fusion.own_ref, bf16[512,256]{1,0:T(8,128)(2,1)S(1)} %bitcast.9), custom_call_target="tpu_custom_call" | custom-call | tf_op jit(solution)/shard_map/sketch/pallas_call | solution.py:613
  90.3 64.7 %project.1 = (f32[64,2048]{1,0:T(8,128)S(1)}, bf16[2048,512]{1,0:T(8,128)(2,1)S(1)}) custom-call(f32[1280,128]{1,0:T(8,128)S(1)} %get-tuple-element.8.gram_ref, f32[512,256]{1,0:T(8,128)S(1)} %bitcast.10, f32[8,32,2,128]{3,2,1,0:T(2,128)S(1)} %get-tuple-element.10.mine_ref, f32[2,8,128]{2,1,0:T(8,128)S(1)} %get-tuple-element.11.totals_ref), custom_call_target="tpu_custom_call" | custom-call | tf_op jit(solution)/shard_map/project/pallas_call | solution.py:756
  155.0 2.6 %convert_multiply_fusion = f32[2048,512]{1,0:T(8,128)} fusion(bf16[2048,512]{1,0:T(8,128)(2,1)S(1)} %get-tuple-element.12), kind=kLoop, calls=%fused_computation | loop fusion | flops 2097152 | bytes 6291456 | tf_op jit(solution)/shard_map/mul | solution.py:803
  157.6 0.8 copy.12
  (1 shorter events, 0.0 us)
Async XLA Ops:
  0.6 1.8 %copy-start = (bf16[2048,512]{1,0:T(8,128)(2,1)S(1)}, bf16[2048,512]{1,0:T(8,128)(2,1)}, u32[]{:S(2)}) copy-start(bf16[2048,512]{1,0:T(8,128)(2,1)} %param.9) | copy-start | bytes 6291460

commit v11 on v10

--- a/solution.py
+++ b/solution.py
@@ -687,11 +687,11 @@
 
     def ready(start, end, q):
         half_ref[start:end, :] = q.astype(jnp.bfloat16)
-        basis_ref[:, start:end] = q.T.astype(jnp.bfloat16)
         if start == 0:
             greeted()
         for peer in range(start // width, end // width):
             pl.when(peer != data_at)(lambda peer=peer: half_copy(peer, data_at).start())
+        basis_ref[:, start:end] = q.T.astype(jnp.bfloat16)
 
     along = ndata // 2
     other = lax.rem(data_at + along, ndata)
@@ -732,9 +732,9 @@
     def work(slots):
         total_ref[...] += block_sums(all_ref, mine_ref, slots, slots, block, width, True)
 
+    total_ref[...] = jnp.zeros_like(total_ref)
     factor_steps(gram_ref, rows_ref, work_ref, inverse_ref, ready)
     all_ref[col_at, own_rows, :] = half_ref[own_rows, :]
-    total_ref[...] = jnp.zeros_like(total_ref)
     for peer in range(ndata):
         pl.when(peer != data_at)(lambda peer=peer: half_copy(peer, peer).wait())
     ring.begin()

time: 160 us -> 160 us (level)
  no operation moved by 1% of the time
where the time goes in v11:
time: 160 us; the launch traced here: 158 us
  Pallas kernels  152 us (95%)
  other arithmetic  4.35 us (3%)
    pallas_call x1, Pallas kernels, sketch_and_gram(): pl.pallas_call(functools.partial(sketch_kernel, block, width), out_shape=...  87.5 us
    pallas_call x1, Pallas kernels, project(): pl.pallas_call(functools.partial(project_kernel, scale, block, width), ou...  64.4 us

profile of v11, /device:TPU:1, one launch (start us, length us, event | category | flops | bytes accessed | tf_op | source)
XLA Modules:
  0.0 158.1 jit_solution(18068964848055384365)
XLA Ops:
  0.6 0.0 copy-start
  0.7 0.9 add_convert_fusion
  1.5 0.8 compare_select_fusion
  2.4 0.0 copy-done
  2.4 0.2 constant_dynamic-slice_fusion
  2.6 0.2 copy.8
  2.8 87.5 %sketch.1 = (f32[8,32,2,128]{3,2,1,0:T(2,128)S(1)}, f32[8,64,256]{2,1,0:T(8,128)S(1)}, f32[1280,128]{1,0:T(8,128)S(1)}, f32[2,8,128]{2,1,0:T(8,128)S(1)}) custom-call(f32[32,2,128]{2,1,0:T(2,128)S(1)} %pad_maximum_fusion.own_ref, bf16[512,256]{1,0:T(8,128)(2,1)S(1)} %bitcast.9), custom_call_target="tpu_custom_call" | custom-call | tf_op jit(solution)/shard_map/sketch/pallas_call | solution.py:613
  90.3 64.4 %project.1 = (f32[64,2048]{1,0:T(8,128)S(1)}, bf16[2048,512]{1,0:T(8,128)(2,1)S(1)}) custom-call(f32[1280,128]{1,0:T(8,128)S(1)} %get-tuple-element.8.gram_ref, f32[512,256]{1,0:T(8,128)S(1)} %bitcast.10, f32[8,32,2,128]{3,2,1,0:T(2,128)S(1)} %get-tuple-element.10.mine_ref, f32[2,8,128]{2,1,0:T(8,128)S(1)} %get-tuple-element.11.totals_ref), custom_call_target="tpu_custom_call" | custom-call | tf_op jit(solution)/shard_map/project/pallas_call | solution.py:756
  154.7 2.6 %convert_multiply_fusion = f32[2048,512]{1,0:T(8,128)} fusion(bf16[2048,512]{1,0:T(8,128)(2,1)S(1)} %get-tuple-element.12), kind=kLoop, calls=%fused_computation | loop fusion | flops 2097152 | bytes 6291456 | tf_op jit(solution)/shard_map/mul | solution.py:803
  157.3 0.8 copy.12
  (1 shorter events, 0.0 us)
Async XLA Ops:
  0.6 1.8 %copy-start = (bf16[2048,512]{1,0:T(8,128)(2,1)S(1)}, bf16[2048,512]{1,0:T(8,128)(2,1)}, u32[]{:S(2)}) copy-start(bf16[2048,512]{1,0:T(8,128)(2,1)} %param.9) | copy-start | bytes 6291460
